TPU v7x, 32 devices: a whole 2x2x4 slice. The times are simulated.
32 devices in a mesh: basin: 8 (over y, x, core), member: 4 (over z).
Axes of the slice: x: 2, y: 2, z: 4, core: 2. Of those that a mesh axis runs over, the one named last changes fastest.
Arguments:
- initial_reservoir_levels: float32 [64, 4, 8192], P('member', None, 'basin'), may hold values from 0 to 1
- normalized_catchment_settings: float32 [10, 8192], P(None, 'basin'), may hold values from 0 to 1
- rainfall_member_series: float32 [24, 64, 8192], P(None, 'member', 'basin'), may hold values from 0 to 0.03
- surface_heat_celsius: float32 [24, 8192], P(None, 'basin'), may hold values from -12 to 12
- potential_evapotranspiration: float32 [24, 8192], P(None, 'basin'), may hold values from 0 to 0.01
- gauge_measured_values: float32 [32, 32], P('basin'), may hold values from 0 to 1
- gauge_deviation_sigma: float32 [32, 32], P('basin'), may hold values from 0.05 to 0.5
- gauge_perturbation_draws: float32 [32, 32, 64], P('basin', None, 'member'), may hold values from -6 to 6
- gauge_catchment_position: int32 [32, 32], P('basin'), may hold values from 0 to 255
- gauge_present_flag: int32 [32, 32], P('basin'), may hold values 0 or 1
- adjacent_block_list: int32 [32, 3], replicated, may hold values from 0 to 31, as said below
Outputs:
- analysis: float32 [64, 4, 8192], P('member', None, 'basin')
- discharge_series: float32 [24, 64, 8192], P(None, 'member', 'basin')
Inputs may be any that keep to these rules, and one draw needn't show every extreme that they name: `adjacent_block_list`: no block lists itself. Of the 12 entries of any aligned range of 4 blocks, at most 3 point into any one aligned range of 4 blocks, and exactly 3 into some range.
All inputs are finite; a program needn't handle non-finite values. No bound on the sum of `gauge_present_flag` on one device may be relied on, other than what follows from the above.
Results may differ from a plain program's by a relative error of at most 0.0003.
Values sent between devices are 32-bit elements; how exact they have to be, the bound alone decides.
No kernel may reach another device: no remote copies, remote signals or barrier semaphores. Data moves between devices by JAX's collectives and lax.ppermute only.
A program may use at most 64 MiB of HBM per device.

v0:
```python
import jax
import jax.numpy as jnp
from jax import lax
from jax.sharding import PartitionSpec as P

NB = 256
OBS = 32
NBR = 3
LOCAL = 128


PARAM_LOW = (-1.5, 0.0002, 0.8, 1.0, 0.4, 0.01, 0.002, 0.0001, 0.1, 0.0001)
PARAM_HIGH = (1.5, 0.002, 4.0, 5.0, 1.0, 0.05, 0.02, 0.002, 0.5, 0.001)


def unpack_params(normalized_catchment_settings):
    return tuple(
        (
            PARAM_LOW[k] + (PARAM_HIGH[k] - PARAM_LOW[k]) * normalized_catchment_settings[k]
            for k in range(10)
        )
    )


def hbv_hour(reservoir_contents, forcing, hydrologic_settings):
    snowpack, moisture, upper_zone, lower_zone = reservoir_contents
    rain_in, air_temp, evap_pot = forcing
    (
        thresh,
        melt_rate,
        field_cap,
        shape_exp,
        evap_limit,
        quick_rate,
        upper_rate,
        lower_rate,
        upper_limit,
        percolation,
    ) = hydrologic_settings
    snow_share = jnp.clip((thresh + 1.0 - air_temp) * 0.5, 0.0, 1.0)
    snowpack = snowpack + snow_share * rain_in
    snowmelt = jnp.minimum(melt_rate * jnp.maximum(air_temp - thresh, 0.0), snowpack)
    snowpack = snowpack - snowmelt
    inflow = (1.0 - snow_share) * rain_in + snowmelt
    recharge = inflow * jnp.power(moisture / field_cap, shape_exp)
    moisture = moisture + inflow - recharge
    excess = jnp.maximum(moisture - field_cap, 0.0)
    moisture = moisture - excess
    actual = jnp.minimum(evap_pot * jnp.minimum(moisture / (evap_limit * field_cap), 1.0), moisture)
    moisture = moisture - actual
    upper_zone = upper_zone + recharge + excess
    perc_flow = jnp.minimum(percolation, upper_zone)
    upper_zone = upper_zone - perc_flow
    lower_zone = lower_zone + perc_flow
    quick_flow = quick_rate * jnp.maximum(upper_zone - upper_limit, 0.0)
    slow_flow = upper_rate * upper_zone
    base_flow = lower_rate * lower_zone
    upper_zone = upper_zone - quick_flow - slow_flow
    lower_zone = lower_zone - base_flow
    return ((snowpack, moisture, upper_zone, lower_zone), quick_flow + slow_flow + base_flow)


def predict_ensemble_discharge(
    initial_reservoir_levels,
    normalized_catchment_settings,
    rainfall_member_series,
    surface_heat_celsius,
    potential_evapotranspiration,
):
    hydrologic_settings = unpack_params(normalized_catchment_settings)
    reservoir_contents = (
        initial_reservoir_levels[:, 0],
        initial_reservoir_levels[:, 1],
        initial_reservoir_levels[:, 2],
        initial_reservoir_levels[:, 3],
    )

    def advance_single_interval(carry, forcing):
        new_state, runoff = hbv_hour(carry, forcing, hydrologic_settings)
        return (new_state, 100.0 * runoff)

    reservoir_contents, discharge_series = lax.scan(
        advance_single_interval,
        reservoir_contents,
        (rainfall_member_series, surface_heat_celsius, potential_evapotranspiration),
    )
    return (reservoir_contents, discharge_series, hydrologic_settings)


def solve_blocks(matrix, rhs):
    factor = jnp.linalg.cholesky(matrix)
    return jax.vmap(lambda lower_tri, right: jax.scipy.linalg.cho_solve((lower_tri, True), right))(
        factor, rhs
    )


def noise_term(scales):
    return scales[:, :, None] ** 2 * jnp.eye(LOCAL, dtype=jnp.float32)


def centred_terms(state_rows, local_pred, local_pert, local_avail, state_sum, pred_sum, members):
    state_anom = state_rows - state_sum / members
    anomaly = local_avail * (local_pred - pred_sum / members)
    innovation = jnp.transpose(local_avail * (local_pert - local_pred), (1, 2, 0))
    return (state_anom, anomaly, innovation)


def on_device(
    initial_reservoir_levels,
    normalized_catchment_settings,
    rainfall_member_series,
    surface_heat_celsius,
    potential_evapotranspiration,
    gauge_measured_values,
    gauge_deviation_sigma,
    gauge_perturbation_draws,
    gauge_catchment_position,
    gauge_present_flag,
    adjacent_block_list,
):
    highest = lax.Precision.HIGHEST
    reservoir_contents, discharge_series, hydrologic_settings = predict_ensemble_discharge(
        initial_reservoir_levels,
        normalized_catchment_settings,
        rainfall_member_series,
        surface_heat_celsius,
        potential_evapotranspiration,
    )
    snowpack, moisture, upper_zone, lower_zone = reservoir_contents
    local_members = moisture.shape[0]
    blk_count = gauge_measured_values.shape[0]
    members = local_members * lax.axis_size("member")
    wetness = 0.45 * moisture / hydrologic_settings[2]
    onehot = (gauge_catchment_position[..., None] == jnp.arange(NB, dtype=jnp.int32)).astype(
        jnp.float32
    )
    gauge_side = jnp.einsum(
        "bon,mbn->mbo",
        onehot,
        discharge_series[-1].reshape(local_members, blk_count, NB),
        precision=highest,
    )
    smap_side = jnp.einsum(
        "bon,mbn->mbo", onehot, wetness.reshape(local_members, blk_count, NB), precision=highest
    )
    slot_gauge = jnp.arange(OBS) < OBS // 2
    predicted = jnp.where(slot_gauge, gauge_side, smap_side)
    perturbed = gauge_measured_values[None] + gauge_deviation_sigma[None] * jnp.transpose(
        gauge_perturbation_draws, (2, 0, 1)
    )
    avail = gauge_present_flag.astype(jnp.float32)
    pred_pack = jnp.transpose(predicted, (1, 0, 2)).reshape(blk_count, local_members * OBS)
    pert_pack = jnp.transpose(perturbed, (1, 0, 2)).reshape(blk_count, local_members * OBS)
    entries = blk_count * NBR
    own_index = lax.axis_index("basin")
    own_list = lax.dynamic_slice_in_dim(
        adjacent_block_list, own_index * blk_count, blk_count, 0
    ).reshape(entries)
    gathered = (
        lax.all_gather(pred_pack, "basin", axis=0, tiled=True),
        lax.all_gather(pert_pack, "basin", axis=0, tiled=True),
        lax.all_gather(gauge_deviation_sigma, "basin", axis=0, tiled=True),
        lax.all_gather(avail, "basin", axis=0, tiled=True),
    )
    far_data = tuple((jnp.take(piece, own_list, axis=0) for piece in gathered))
    far_pred, far_pert, far_sd, far_avail = far_data

    def spread_members(piece):
        shaped = piece.reshape(blk_count, NBR, local_members, OBS)
        return jnp.transpose(shaped, (2, 0, 1, 3)).reshape(local_members, blk_count, NBR * OBS)

    local_pred = jnp.concatenate([predicted, spread_members(far_pred)], axis=2)
    local_pert = jnp.concatenate([perturbed, spread_members(far_pert)], axis=2)
    local_sd = jnp.concatenate(
        [gauge_deviation_sigma, far_sd.reshape(blk_count, NBR * OBS)], axis=1
    )
    local_avail = jnp.concatenate([avail, far_avail.reshape(blk_count, NBR * OBS)], axis=1)
    state_rows = jnp.concatenate(
        [
            moisture.reshape(local_members, blk_count, NB),
            upper_zone.reshape(local_members, blk_count, NB),
        ],
        axis=2,
    )
    scale = 1.0 / (members - 1)
    state_sum, pred_sum = lax.psum(
        (jnp.sum(state_rows, axis=0), jnp.sum(local_pred, axis=0)), "member"
    )
    state_anom, anomaly, innovation = centred_terms(
        state_rows, local_pred, local_pert, local_avail, state_sum, pred_sum, members
    )
    cov_part = jnp.einsum("mbl,mbk->blk", anomaly, anomaly, precision=highest)
    cross_part = jnp.einsum("mbr,mbl->brl", state_anom, anomaly, precision=highest)
    cov_sum, cross_sum = lax.psum((cov_part, cross_part), "member")
    weights = solve_blocks(cov_sum * scale + noise_term(local_sd), innovation)
    increment = jnp.einsum("brl,blm->mbr", cross_sum * scale, weights, precision=highest)
    updated = state_rows + increment
    moisture_new = updated[..., :NB].reshape(local_members, -1)
    upper_new = updated[..., NB:].reshape(local_members, -1)
    analysis = jnp.stack([snowpack, moisture_new, upper_new, lower_zone], axis=1)
    return (analysis, discharge_series)


def solution(mesh):
    placed = (
        P("member", None, "basin"),
        P(None, "basin"),
        P(None, "member", "basin"),
        P(None, "basin"),
        P(None, "basin"),
        P("basin", None),
        P("basin", None),
        P("basin", None, "member"),
        P("basin", None),
        P("basin", None),
        P(),
    )
    return jax.shard_map(
        on_device,
        mesh=mesh,
        in_specs=placed,
        out_specs=(P("member", None, "basin"), P(None, "member", "basin")),
        check_vma=False,
    )
```

profile of v0, /device:TPU:0, one launch (start us, length us, event | category | flops | bytes accessed | tf_op | source)
XLA Modules:
  0.0 332.6 jit_solution(14205390064601672607)
XLA Ops:
  8.1 1.1 multiply_add_fusion.3
  9.2 1.8 fusion.38
  11.2 100.5 %while.20 = (s32[]{:T(128)}, f32[16,1024]{1,0:T(8,128)S(1)}, f32[16,1024]{1,0:T(8,128)S(1)}, f32[16,1024]{1,0:T(8,128)S(1)}, f32[16,1024]{1,0:T(8,128)S(1)}, /*i...) while((s32[]{:T(128)}, f32[16,1024]{1,0:T(8,128)S(1)}, ...), condition=%wide.region_1.2_spmd, body=%wide.region_0.1_spmd.sunk | while | flops 876546 | bytes 1172161 | solution.py:82
  11.9 1.6 fusion.44
  14.3 1.0 minimum_subtract_fusion.4
  16.1 1.6 fusion.44
  18.5 1.0 minimum_subtract_fusion.4
  20.3 1.6 fusion.44
  22.7 1.0 minimum_subtract_fusion.4
  24.5 1.6 fusion.44
  26.9 1.0 minimum_subtract_fusion.4
  28.7 1.6 fusion.44
  31.1 1.0 minimum_subtract_fusion.4
  32.9 1.6 fusion.44
  35.3 1.0 minimum_subtract_fusion.4
  37.1 1.6 fusion.44
  39.5 1.0 minimum_subtract_fusion.4
  41.3 1.6 fusion.44
  43.6 1.0 minimum_subtract_fusion.4
  45.4 1.6 fusion.44
  47.8 1.0 minimum_subtract_fusion.4
  49.6 1.6 fusion.44
  52.0 1.0 minimum_subtract_fusion.4
  53.8 1.6 fusion.44
  56.2 1.0 minimum_subtract_fusion.4
  58.0 1.6 fusion.44
  60.4 1.0 minimum_subtract_fusion.4
  62.2 1.6 fusion.44
  64.6 1.0 minimum_subtract_fusion.4
  66.4 1.6 fusion.44
  68.8 1.0 minimum_subtract_fusion.4
  70.6 1.6 fusion.44
  73.0 1.0 minimum_subtract_fusion.4
  74.8 1.6 fusion.44
  77.1 1.0 minimum_subtract_fusion.4
  78.9 1.6 fusion.44
  81.3 1.0 minimum_subtract_fusion.4
  83.1 1.6 fusion.44
  85.5 1.0 minimum_subtract_fusion.4
  87.3 1.6 fusion.44
  89.7 1.0 minimum_subtract_fusion.4
  91.5 1.6 fusion.44
  93.9 1.0 minimum_subtract_fusion.4
  95.7 1.6 fusion.44
  98.1 1.0 minimum_subtract_fusion.4
  99.9 1.6 fusion.44
  102.3 1.0 minimum_subtract_fusion.4
  104.1 1.6 fusion.44
  106.5 1.0 minimum_subtract_fusion.4
  108.3 1.6 fusion.44
  110.6 1.0 minimum_subtract_fusion.4
  113.2 10.7 %all-gather.1 = f32[8,4,512]{2,1,0:T(4,128)S(1)} all-gather(f32[1,4,512]{2,1,0:T(4,128)S(1)} %reshape.213), channel_id=1, replica_groups=mesh['basin'=8,'member'=4] {'basin'}, dimensions={0}, use_global_device_ids=true | all-gather | bytes 73728 | tf_op jit(solution)/shard_map/all_gather | solution.py:160
  124.0 9.2 %all-gather.3 = f32[8,4,512]{2,1,0:T(4,128)S(1)} all-gather(f32[1,4,512]{2,1,0:T(4,128)S(1)} %reshape.217), channel_id=1, replica_groups=mesh['basin'=8,'member'=4] {'basin'}, dimensions={0}, use_global_device_ids=true | all-gather | bytes 73728 | tf_op jit(solution)/shard_map/all_gather | solution.py:161
  134.9 18.9 %all-reduce = (f32[4,128]{1,0:T(4,128)S(1)}, f32[4,512]{1,0:T(4,128)S(1)}) all-reduce(f32[4,128]{1,0:T(4,128)S(1)} %get-tuple-element.281, f32[4,512]{1,0:T(4,128)S(1)} %reduce_sum.19), channel_id=1, replica_groups=mesh['basin'=8,'member'=4] {'member'}, use_global_device_ids=true, to_apply=%region_3.6 | all-reduce | flops 2560 | bytes 20480 | tf_op jit(solution)/shard_map/psum | solution.py:186
  153.9 7.9 %all-gather = f32[8,4,32]{2,1,0:T(4,128)S(1)} all-gather(f32[1,4,32]{2,1,0:T(4,128)S(1)} %get-tuple-element.309), channel_id=1, replica_groups=mesh['basin'=8,'member'=4] {'basin'}, dimensions={0}, use_global_device_ids=true | all-gather | bytes 4608 | tf_op jit(solution)/shard_map/all_gather | solution.py:163
  162.3 9.1 %all-gather.2 = f32[8,4,32]{2,1,0:T(4,128)S(1)} all-gather(f32[1,4,32]{2,1,0:T(4,128)S(1)} %bitcast.143), channel_id=1, replica_groups=mesh['basin'=8,'member'=4] {'basin'}, dimensions={0}, use_global_device_ids=true | all-gather | bytes 4608 | tf_op jit(solution)/shard_map/all_gather | solution.py:162
  172.2 1.3 fusion.26
  173.5 2.8 fusion.12
  176.9 57.2 %all-reduce.4.cloned.1.call-done = (f32[4,128,128]{1,2,0:T(8,128)}, f32[4,512,128]{2,1,0:T(8,128)}) async-done(((f32[4,128,128]{1,2,0:T(8,128)}, f32[4,512,128]{2,1,0:T(8,128)}), (f32[4,128,128]{1,2,0:T(8,128)}, f32[4,512,128]{2,1,0:T(8,128)})) %all-reduce.4.cloned.1.call-update) | async-done | bytes 1310736 | tf_op jit(solution)/shard_map/psum | solution.py:194
  234.1 1.0 multiply_add_fusion.1
  235.2 1.1 fusion.11
  236.3 46.9 %custom-call.11 = f32[4,128,128]{2,1,0:T(8,128)S(1)} custom-call(f32[4,128,128]{2,1,0:T(8,128)S(1)} %fusion.11), custom_call_target="Cholesky" | custom-call | tf_op jit(solution)/shard_map/jit(cholesky)/cholesky | solution.py:91
  283.5 39.3 %custom-call.12 = f32[4,1,128,128]{2,3,1,0:T(8,128)S(1)} custom-call(f32[4,1,128,128]{3,2,1,0:T(8,128)S(1)} %select_bitcast_fusion), custom_call_target="InvertDiagBlocksLowerTriangular" | custom-call | tf_op jit(solution)/shard_map/vmap(jit(_cho_solve))/triangular_solve | solution.py:92
  323.7 0.9 fusion.4
  (124 shorter events, 45.5 us)
Async XLA Ops:
  7.2 0.7 copy-start
  7.2 226.9 %all-reduce.4.cloned.1.call-start = ((), (), s32[]{:S(2)}) async-start(), calls=%async_computation | async-start | bytes 2621440 | tf_op jit(solution)/shard_map/psum | solution.py:194
  11.1 101.5 %copy-start.4 = (s32[4,32]{1,0:T(4,128)S(1)}, s32[4,32]{1,0:T(4,128)}, u32[]{:S(2)}) copy-start(s32[4,32]{1,0:T(4,128)} %param.25) | copy-start | bytes 1540
  11.1 112.8 %copy-start.2 = (f32[4,32,16]{1,2,0:T(8,128)S(1)}, f32[4,32,16]{1,2,0:T(8,128)}, u32[]{:S(2)}) copy-start(f32[4,32,16]{1,2,0:T(8,128)} %param.24) | copy-start | bytes 24580
  11.1 112.8 %copy-start.3 = (f32[4,32]{1,0:T(4,128)S(1)}, f32[4,32]{1,0:T(4,128)}, u32[]{:S(2)}) copy-start(f32[4,32]{1,0:T(4,128)} %param.23) | copy-start | bytes 1540
  11.1 112.8 %copy-start.5 = (f32[4,32]{1,0:T(4,128)S(1)}, f32[4,32]{1,0:T(4,128)}, u32[]{:S(2)}) copy-start(f32[4,32]{1,0:T(4,128)} %param.22) | copy-start | bytes 1540
  111.7 42.2 %copy-start.6 = (s32[4,32]{1,0:T(4,128)S(1)}, s32[4,32]{1,0:T(4,128)}, u32[]{:S(2)}) copy-start(s32[4,32]{1,0:T(4,128)} %param.26) | copy-start | bytes 1540
  235.1 88.6 %copy-start.1 = (f32[4,512,128]{2,1,0:T(8,128)S(1)}, f32[4,512,128]{2,1,0:T(8,128)}, u32[]{:S(2)}) copy-start(f32[4,512,128]{2,1,0:T(8,128)} %get-tuple-element.276) | copy-start | bytes 3145732
Sparse Core Ops, SparseCore 0:
  176.5 57.5 all-reduce.3
where the time goes:
time: 339 us; the launch traced here: 333 us
  other arithmetic  172 us (51%)
  waiting for transfers between devices  57.2 us (17%)
  blocking collectives  55.8 us (16%)
  local copies, waits for them, and re-layouts  26.3 us (8%)
  between operations  14.4 us (4%)
  matrix products  6.47 us (2%)
    psum x1, waiting for transfers between devices, on_device(): cov_sum, cross_sum = lax.psum((cov_part, cross_part), 'member')  57.2 us
    another operation x4, other arithmetic, solve_blocks(): factor = jnp.linalg.cholesky(matrix)  47.1 us
    another operation x3, other arithmetic, solve_blocks(): jax.scipy.linalg.cho_solve((lower_tri, True), right)  39.4 us
    dynamic_update_slice x24, other arithmetic, predict_ensemble_discharge(): lax.scan(advance_single_interval, reservoir_contents, (rainfall_member_se...  39 us
    sub x24, other arithmetic, hbv_hour(): moisture = moisture - actual  24 us
    psum x1, blocking collectives, on_device(): lax.psum((jnp.sum(state_rows, axis=0), jnp.sum(local_pred, axis=0)), 'mem...  18.9 us
    sub x24, other arithmetic, hbv_hour(): inflow = (1.0 - snow_share) * rain_in + snowmelt  18.7 us
    dynamic_slice x24, local copies, waits for them, and re-layouts, predict_ensemble_discharge(): lax.scan(advance_single_interval, reservoir_contents, (rainfall_member_se...  18.3 us
  transfers between devices with their start and end apart: 1, of which 1 were waited for; matrix products, arithmetic and copies ran while one was open for 0% of the time, Pallas kernels for 0%

commit v1 on v0

v1 whole, which is shorter than its diff:
```python
import functools

import jax
import jax.numpy as jnp
from jax import lax
from jax.experimental import pallas as pl
from jax.experimental.pallas import tpu as pltpu
from jax.sharding import PartitionSpec as P

NB = 256
OBS = 32
NBR = 3
LOCAL = 128

PARAM_LOW = (-1.5, 0.0002, 0.8, 1.0, 0.4, 0.01, 0.002, 0.0001, 0.1, 0.0001)
PARAM_HIGH = (1.5, 0.002, 4.0, 5.0, 1.0, 0.05, 0.02, 0.002, 0.5, 0.001)

HIGHEST = lax.Precision.HIGHEST
STRIP = 512
CHUNK = 6
PACK = 40
VMEM_LIMIT = 48 * 1024 * 1024


def lanes_of(table):
    return jnp.concatenate([table[b : b + 1] for b in range(table.shape[0])], axis=1)


def three_parts(x):
    high = x.astype(jnp.bfloat16)
    rest = x - high.astype(jnp.float32)
    middle = rest.astype(jnp.bfloat16)
    low = (rest - middle.astype(jnp.float32)).astype(jnp.bfloat16)
    return [high, middle, low]


def forecast_kernel(
    levels,
    settings,
    rain_hbm,
    heat,
    evap,
    measured,
    sigma,
    draws,
    position,
    present,
    flow_hbm,
    wet_state,
    dry_state,
    pack,
    rain,
    flow,
    share,
    melt_cap,
    last_flow,
    in_sems,
    out_sems,
):
    hours, members, width = rain_hbm.shape
    strip = min(STRIP, width)
    pieces = [(s, c) for s in range(width // strip) for c in range(hours // CHUNK)]

    def part(s, c):
        return (pl.ds(c * CHUNK, CHUNK), slice(None), pl.ds(s * strip, strip))

    def rain_copy(n):
        where = part(*pieces[n])
        return pltpu.make_async_copy(rain_hbm.at[where], rain.at[where], in_sems.at[n])

    def flow_copy(n):
        where = part(*pieces[n])
        return pltpu.make_async_copy(flow.at[where], flow_hbm.at[where], out_sems.at[n])

    for n in range(len(pieces)):
        rain_copy(n).start()

    def parameter(k, where=slice(None)):
        return PARAM_LOW[k] + (PARAM_HIGH[k] - PARAM_LOW[k]) * settings[k : k + 1, where]

    share[...] = jnp.clip((parameter(0) + 1.0 - heat[...]) * 0.5, 0.0, 1.0)
    melt_cap[...] = parameter(1) * jnp.maximum(heat[...] - parameter(0), 0.0)

    for s in range(width // strip):
        where = pl.ds(s * strip, strip)
        field_cap = parameter(2, where)
        inv_cap = 1.0 / field_cap
        shape_exp = parameter(3, where)
        inv_limit = 1.0 / (parameter(4, where) * field_cap)
        quick_rate, upper_rate, lower_rate, upper_limit, percolation = (
            parameter(k, where) for k in range(5, 10)
        )
        state = tuple(levels[:, k, where] for k in range(4))

        def hour(h, state):
            snow, moist, upper, lower = state
            fall = rain[h, :, where]
            snow_fall = share[pl.ds(h, 1), where] * fall
            snow = snow + snow_fall
            melt = jnp.minimum(melt_cap[pl.ds(h, 1), where], snow)
            snow = snow - melt
            inflow = (fall - snow_fall) + melt
            recharge = inflow * jnp.exp2(shape_exp * jnp.log2(moist * inv_cap))
            moist = moist + inflow - recharge
            excess = jnp.maximum(moist - field_cap, 0.0)
            moist = moist - excess
            actual = jnp.minimum(
                evap[pl.ds(h, 1), where] * jnp.minimum(moist * inv_limit, 1.0), moist
            )
            moist = moist - actual
            upper = upper + recharge + excess
            perc_flow = jnp.minimum(percolation, upper)
            upper = upper - perc_flow
            lower = lower + perc_flow
            fast = quick_rate * jnp.maximum(upper - upper_limit, 0.0) + upper_rate * upper
            base = lower_rate * lower
            upper = upper - fast
            lower = lower - base
            flow[h, :, where] = 100.0 * (fast + base)
            return (snow, moist, upper, lower)

        for c in range(hours // CHUNK):
            n = s * (hours // CHUNK) + c
            rain_copy(n).wait()
            state = lax.fori_loop(c * CHUNK, (c + 1) * CHUNK, hour, state, unroll=2)
            flow_copy(n).start()
        snow, moist, upper, lower = state
        wet_state[0, :, where] = moist
        wet_state[1, :, where] = upper
        dry_state[0, :, where] = snow
        dry_state[1, :, where] = lower
        last_flow[:, where] = 0.45 * moist * inv_cap

    slots = lanes_of(position[...])
    pick = (lax.broadcasted_iota(jnp.int32, (NB, LOCAL), 0) == slots).astype(jnp.bfloat16)
    blocks = width // NB
    fields = []
    for b in range(blocks):
        where = pl.ds(b * NB, NB)
        fields += three_parts(flow[hours - 1, :, where]) + three_parts(last_flow[:, where])
    taken = jnp.dot(jnp.concatenate(fields, axis=0), pick, preferred_element_type=jnp.float32)
    lane = lax.broadcasted_iota(jnp.int32, (members, LOCAL), 1)
    predicted = jnp.zeros((members, LOCAL), jnp.float32)
    for b in range(blocks):
        part6 = [taken[(b * 6 + k) * members : (b * 6 + k + 1) * members] for k in range(6)]
        gauge = (part6[2] + part6[1]) + part6[0]
        smap = (part6[5] + part6[4]) + part6[3]
        chosen = jnp.where(lane % OBS < OBS // 2, gauge, smap)
        predicted = jnp.where(lane // OBS == b, chosen, predicted)
    sd = lanes_of(sigma[...])
    spread = jnp.transpose(draws[...].reshape(LOCAL, members))
    pack[0:members] = predicted
    pack[members : 2 * members] = lanes_of(measured[...]) + sd * spread
    tail = pack.shape[0] - 2 * members
    pack[2 * members :] = jnp.broadcast_to(
        lanes_of(present[...].astype(jnp.float32)) / sd, (tail, LOCAL)
    )
    for n in range(len(pieces)):
        flow_copy(n).wait()


def forecast(levels, settings, rain, heat, evap, measured, sigma, draws, position, present):
    hours, members, width = rain.shape
    copies = (width // min(STRIP, width)) * (hours // CHUNK)
    f32 = jnp.float32
    vmem = pl.BlockSpec(memory_space=pltpu.VMEM)
    hbm = pl.BlockSpec(memory_space=pl.ANY)
    return pl.pallas_call(
        forecast_kernel,
        out_shape=(
            jax.ShapeDtypeStruct((hours, members, width), f32),
            jax.ShapeDtypeStruct((2, members, width), f32),
            jax.ShapeDtypeStruct((2, members, width), f32),
            jax.ShapeDtypeStruct((2 * members + 8, LOCAL), f32),
        ),
        in_specs=[vmem, vmem, hbm] + [vmem] * 7,
        out_specs=(hbm, vmem, vmem, vmem),
        scratch_shapes=[
            pltpu.VMEM((hours, members, width), f32),
            pltpu.VMEM((hours, members, width), f32),
            pltpu.VMEM((hours, width), f32),
            pltpu.VMEM((hours, width), f32),
            pltpu.VMEM((members, width), f32),
            pltpu.SemaphoreType.DMA((copies,)),
            pltpu.SemaphoreType.DMA((copies,)),
        ],
        compiler_params=pltpu.CompilerParams(vmem_limit_bytes=VMEM_LIMIT),
        name="forecast",
    )(levels, settings, rain, heat, evap, measured, sigma, draws, position, present)


def localize_kernel(relative, count, index, adjacency, *refs):
    pieces, (pred_out, innov_out, weight_out, table) = refs[:count], refs[count:]
    at = 0
    for piece in pieces:
        n = piece.shape[0] if len(piece.shape) == 3 else 1
        table[at : at + n] = piece[...].reshape((n,) + table.shape[1:])
        at += n
    me = index[0]
    blocks, members, _ = pred_out.shape
    rows = table.shape[1]
    lane = lax.broadcasted_iota(jnp.int32, (rows, LOCAL), 1) // OBS
    for b in range(blocks):
        local = jnp.zeros((rows, LOCAL), jnp.float32)
        for i in range(NBR + 1):
            source = me * blocks + b if i == 0 else adjacency[me * blocks + b, i - 1]
            owner = source // blocks
            if relative:
                owner = owner ^ me
            shift = ((i + blocks - source % blocks) % blocks) * OBS
            local = jnp.where(lane == i, pltpu.roll(table[owner], shift, 1), local)
        weight = local[2 * members : 2 * members + 1]
        pred_out[b] = local[:members]
        innov_out[b] = weight * (local[members : 2 * members] - local[:members])
        weight_out[b] = weight


def localize(pieces, relative, index, adjacency, blocks, members):
    f32 = jnp.float32
    rows = 2 * members + 8
    total = sum(p.shape[0] if p.ndim == 3 else 1 for p in pieces)
    vmem = pl.BlockSpec(memory_space=pltpu.VMEM)
    smem = pl.BlockSpec(memory_space=pltpu.SMEM)
    return pl.pallas_call(
        functools.partial(localize_kernel, relative, len(pieces)),
        out_shape=(
            jax.ShapeDtypeStruct((blocks, members, LOCAL), f32),
            jax.ShapeDtypeStruct((blocks, members, LOCAL), f32),
            jax.ShapeDtypeStruct((blocks, 1, LOCAL), f32),
        ),
        in_specs=[smem, smem] + [vmem] * len(pieces),
        out_specs=(vmem, vmem, vmem),
        scratch_shapes=[pltpu.VMEM((total, rows, LOCAL), f32)],
        name="localize",
    )(index, adjacency, *pieces)


def eliminate(systems):
    size = systems[0][0].shape[0]
    groups = size // 8
    sub = lax.broadcasted_iota(jnp.int32, (8, LOCAL), 0)
    mats = [[m[g * 8 : g * 8 + 8] for g in range(groups)] for (m,) in systems]
    for k in range(size):
        home, at = divmod(k, 8)
        for mat in mats:
            columns = [jnp.broadcast_to(part[:, k : k + 1], (8, LOCAL)) for part in mat]
            pivot = jnp.broadcast_to(columns[home][at : at + 1], (8, LOCAL))
            row = jnp.broadcast_to(mat[home][at : at + 1], (8, LOCAL)) / pivot
            for g in range(groups):
                part = mat[g] - columns[g] * row
                mat[g] = jnp.where(sub == at, row, part) if g == home else part
    return [jnp.concatenate(mat, axis=0) for mat in mats]


def update_kernel(count, *refs):
    innov, weight, wet_own, dry = refs[:4]
    preds, wets = refs[4 : 4 + count], refs[4 + count : 4 + 2 * count]
    analysis = refs[-1]
    blocks, members, _ = innov.shape
    systems = []
    for b in range(blocks):
        pred = jnp.concatenate([p[b] if len(p.shape) == 3 else p[:, b].reshape(-1, LOCAL) for p in preds], axis=0)
        total = pred.shape[0]
        scaled = (pred - jnp.mean(pred, axis=0, keepdims=True)) * weight[b]
        both = jnp.concatenate(
            [scaled, innov[b], jnp.zeros((LOCAL - total - members, LOCAL), jnp.float32)], axis=0
        )
        matrix = lax.dot_general(
            scaled, both, (((1,), (1,)), ((), ())), precision=HIGHEST, preferred_element_type=jnp.float32
        )
        rows = lax.broadcasted_iota(jnp.int32, (total, LOCAL), 0)
        cols = lax.broadcasted_iota(jnp.int32, (total, LOCAL), 1)
        systems.append((matrix + jnp.where(rows == cols, float(total - 1), 0.0),))
    solved = eliminate(systems)
    for b in range(blocks):
        where = pl.ds(b * NB, NB)
        gain = solved[b]
        gain = gain - jnp.mean(gain, axis=0, keepdims=True)
        turned = jnp.transpose(gain)[total : total + members]
        for k, slot in ((0, 1), (1, 2)):
            states = jnp.concatenate(
                [w[k, :, where] if len(w.shape) == 3 else w[:, k, :, where].reshape(-1, NB) for w in wets], axis=0
            )
            analysis[:, slot, where] = wet_own[k, :, where] + jnp.dot(
                turned, states, precision=HIGHEST, preferred_element_type=jnp.float32
            )
    analysis[:, 0, :] = dry[0]
    analysis[:, 3, :] = dry[1]


def update(innov, weight, wet, dry, preds, wets):
    _, members, width = wet.shape
    vmem = pl.BlockSpec(memory_space=pltpu.VMEM)
    count = len(preds)
    return pl.pallas_call(
        functools.partial(update_kernel, count),
        out_shape=jax.ShapeDtypeStruct((members, 4, width), jnp.float32),
        in_specs=[vmem] * (4 + 2 * count),
        out_specs=vmem,
        compiler_params=pltpu.CompilerParams(vmem_limit_bytes=VMEM_LIMIT),
        name="update",
    )(innov, weight, wet, dry, *preds, *wets)


def exchange(x, axis, limit=8):
    size = lax.axis_size(axis)
    if size > limit:
        return [lax.all_gather(x, axis, axis=0, tiled=False)], False
    others = [
        lax.ppermute(x, axis, [(i, i ^ s) for i in range(size)]) for s in range(1, size)
    ]
    return [x] + others, True


def on_device(
    initial_reservoir_levels,
    normalized_catchment_settings,
    rainfall_member_series,
    surface_heat_celsius,
    potential_evapotranspiration,
    gauge_measured_values,
    gauge_deviation_sigma,
    gauge_perturbation_draws,
    gauge_catchment_position,
    gauge_present_flag,
    adjacent_block_list,
):
    members = rainfall_member_series.shape[1]
    blocks = gauge_measured_values.shape[0]
    discharge, wet, dry, pack = forecast(
        initial_reservoir_levels,
        normalized_catchment_settings,
        rainfall_member_series,
        surface_heat_celsius,
        potential_evapotranspiration,
        gauge_measured_values,
        gauge_deviation_sigma,
        gauge_perturbation_draws,
        gauge_catchment_position,
        gauge_present_flag,
    )
    index = jnp.full((1,), lax.axis_index("basin"), jnp.int32)
    packs, relative = exchange(pack, "basin")
    pred, innov, weight = localize(packs, relative, index, adjacent_block_list, blocks, members)
    preds, _ = exchange(pred, "member", 4)
    wets, _ = exchange(wet, "member", 4)
    analysis = update(innov, weight, wet, dry, preds, wets)
    return (analysis, discharge)


def solution(mesh):
    placed = (
        P("member", None, "basin"),
        P(None, "basin"),
        P(None, "member", "basin"),
        P(None, "basin"),
        P(None, "basin"),
        P("basin", None),
        P("basin", None),
        P("basin", None, "member"),
        P("basin", None),
        P("basin", None),
        P(),
    )
    return jax.shard_map(
        on_device,
        mesh=mesh,
        in_specs=placed,
        out_specs=(P("member", None, "basin"), P(None, "member", "basin")),
        check_vma=False,
    )
```

time: 339 us -> 58.5 us (0.17); the launches traced: 333 us -> 57.8 us
  other arithmetic: 172 us -> 0 us
  blocking collectives: 55.8 us -> 0 us
  waiting for transfers between devices: 57.2 us -> 15.5 us
  Pallas kernels: 0 us -> 15.7 us
  local copies, waits for them, and re-layouts: 26.3 us -> 12 us
  starting transfers between devices: 0.04 us -> 13.9 us
  between operations: 14.4 us -> 0.76 us
  matrix products: 6.47 us -> 0 us
    another operation x8 -> x0, other arithmetic: 86.5 us -> none  [the longest x4 47.1 us: solve_blocks(): factor = jnp.linalg.cholesky(matrix)]
    psum x1 -> x0, waiting for transfers between devices: 57.2 us -> none  [on_device(): cov_sum, cross_sum = lax.psum((cov_part, cross_part), 'member')]
    sub x48 -> x0, other arithmetic: 42.7 us -> none  [the longest x24 24 us: hbv_hour(): moisture = moisture - actual]
    dynamic_update_slice x24 -> x0, other arithmetic: 39 us -> none  [predict_ensemble_discharge(): lax.scan(advance_single_interval, reservoir_contents, (rainfall_member_se...]
    all_gather x4 -> x0, blocking collectives: 36.9 us -> none  [the longest x1 10.7 us: on_device(): lax.all_gather(pred_pack, 'basin', axis=0, tiled=True)]
    psum x1 -> x0, blocking collectives: 18.9 us -> none  [on_device(): lax.psum((jnp.sum(state_rows, axis=0), jnp.sum(local_pred, axis=0)), 'mem...]
    dynamic_slice x26 -> x0, local copies, waits for them, and re-layouts: 18.5 us -> none  [the longest x24 18.3 us: predict_ensemble_discharge(): lax.scan(advance_single_interval, reservoir_contents, (rainfall_member_se...]
    pallas_call x0 -> x3, Pallas kernels: none -> 15.7 us  [the longest x1 10.2 us: update(): pl.pallas_call(functools.partial(update_kernel, count), out_shape=jax.Sha...]
  transfers between devices with their start and end apart: 1 -> 13, of which waited for: 1 -> 6; matrix products, arithmetic and copies ran while one was open for 0% -> 1% of each run, Pallas kernels for 0% -> 3%
where the time goes in v1:
time: 58.5 us; the launch traced here: 57.8 us
  Pallas kernels  15.7 us (27%)
  waiting for transfers between devices  15.5 us (26%)
  starting transfers between devices  13.9 us (24%)
  local copies, waits for them, and re-layouts  12 us (21%)
  between operations  0.76 us (1%)
    ppermute x13, waiting for transfers between devices, exchange(): lax.ppermute(x, axis, [(i, i ^ s) for i in range(size)])  15.5 us
    ppermute x13, starting transfers between devices, exchange(): lax.ppermute(x, axis, [(i, i ^ s) for i in range(size)])  13.9 us
    unnamed x44, local copies, waits for them, and re-layouts  12 us
    pallas_call x1, Pallas kernels, update(): pl.pallas_call(functools.partial(update_kernel, count), out_shape=jax.Sha...  10.2 us
    pallas_call x1, Pallas kernels, forecast(): pl.pallas_call(forecast_kernel, out_shape=(jax.ShapeDtypeStruct((hours, m...  3.54 us
    pallas_call x1, Pallas kernels, localize(): pl.pallas_call(functools.partial(localize_kernel, relative, len(pieces)),...  1.9 us
  transfers between devices with their start and end apart: 13, of which 6 were waited for; matrix products, arithmetic and copies ran while one was open for 1% of the time, Pallas kernels for 3%

profile of v1, /device:TPU:0, one launch (start us, length us, event | category | flops | bytes accessed | tf_op | source)
XLA Modules:
  0.0 57.8 jit_solution(12041974394173039662)
XLA Ops:
  0.6 0.0 copy-start.20
  0.6 0.8 %copy.13.draws = f32[4,32,16]{2,1,0:T(8,128)S(1)} copy(f32[4,32,16]{1,2,0:T(8,128)} %param.18) | data formatting | bytes 16384 | tf_op args[7]
  1.5 0.0 copy-start
  1.5 1.4 %copy-done = f32[24,16,1024]{2,1,0:T(8,128)S(1)} copy-done((f32[24,16,1024]{2,1,0:T(8,128)S(1)}, f32[24,16,1024]{2,1,0:T(8,128)}, u32[]{:S(2)}) %copy-start) | copy-done | bytes 1572888
  2.9 0.0 copy-start.1
  2.9 0.9 %copy-done.1 = f32[16,4,1024]{2,1,0:T(4,128)S(1)} copy-done((f32[16,4,1024]{2,1,0:T(4,128)S(1)}, f32[16,4,1024]{2,1,0:T(4,128)}, u32[]{:S(2)}) %copy-start.1) | copy-done | bytes 262168
  3.8 0.0 copy-start.2
  3.8 0.9 %copy-done.2 = f32[24,1024]{1,0:T(8,128)S(1)} copy-done((f32[24,1024]{1,0:T(8,128)S(1)}, f32[24,1024]{1,0:T(8,128)}, u32[]{:S(2)}) %copy-start.2) | copy-done | bytes 98328
  4.7 0.0 copy-start.3
  4.7 0.9 %copy-done.3 = f32[24,1024]{1,0:T(8,128)S(1)} copy-done((f32[24,1024]{1,0:T(8,128)S(1)}, f32[24,1024]{1,0:T(8,128)}, u32[]{:S(2)}) %copy-start.3) | copy-done | bytes 98328
  5.6 0.0 copy-start.4
  5.6 0.8 %copy-done.4 = f32[10,1024]{1,0:T(8,128)S(1)} copy-done((f32[10,1024]{1,0:T(8,128)S(1)}, f32[10,1024]{1,0:T(8,128)}, u32[]{:S(2)}) %copy-start.4) | copy-done | bytes 40984
  6.5 0.0 copy-start.9
  6.5 0.7 %copy-done.9 = f32[4,32]{1,0:T(4,128)S(1)} copy-done((f32[4,32]{1,0:T(4,128)S(1)}, f32[4,32]{1,0:T(4,128)}, u32[]{:S(2)}) %copy-start.9) | copy-done | bytes 536
  7.2 0.0 copy-start.10
  7.2 0.7 %copy-done.10 = f32[4,32]{1,0:T(4,128)S(1)} copy-done((f32[4,32]{1,0:T(4,128)S(1)}, f32[4,32]{1,0:T(4,128)}, u32[]{:S(2)}) %copy-start.10) | copy-done | bytes 536
  7.8 0.0 copy-start.11
  7.8 0.7 %copy-done.11 = s32[4,32]{1,0:T(4,128)S(1)} copy-done((s32[4,32]{1,0:T(4,128)S(1)}, s32[4,32]{1,0:T(4,128)}, u32[]{:S(2)}) %copy-start.11) | copy-done | bytes 536
  8.5 0.0 copy-start.12
  8.5 0.7 %copy-done.12 = s32[4,32]{1,0:T(4,128)S(1)} copy-done((s32[4,32]{1,0:T(4,128)S(1)}, s32[4,32]{1,0:T(4,128)}, u32[]{:S(2)}) %copy-start.12) | copy-done | bytes 536
  9.2 3.5 %forecast.1 = (f32[24,16,1024]{2,1,0:T(8,128)}, f32[2,16,1024]{2,1,0:T(8,128)S(1)}, f32[2,16,1024]{2,1,0:T(8,128)S(1)}, f32[40,128]{1,0:T(8,128)S(1)}) custom-call(f32[16,4,1024]{2,1,0:T(4,128)S(1)} %copy-done.1, f32[10,1024]{1,0:T(8,128)S(1)} %copy-done.4, f32[24,16,1024]{2,1,0:T(8,128)S(1)} %copy-done, f32[24,1024]{1,0:T(8,128)S(1)} %copy-done.2, ...), custom_call_target="tpu_custom_call" | custom-call | tf_op jit(solution)/shard_map/forecast/pallas_call | solution.py:168
  12.7 0.0 copy-start.7
  12.8 3.4 %collective-permute-start.6 = (f32[40,128]{1,0:T(8,128)S(1)}, f32[40,128]{1,0:T(8,128)S(1)}, u32[]{:S(2)}, u32[]{:S(2)}) collective-permute-start(f32[40,128]{1,0:T(8,128)S(1)} %get-tuple-element.9.refs_0_), channel_id=1, source_target_pairs={{0,28},{4,24},{8,20},{12,16},{16,12},{20,8},{24,4},{28,0},{1,29},{... | collective-permute-start | bytes 61448 | tf_op jit(solution)/shard_map/ppermute | solution.py:310
  16.2 3.6 %collective-permute-start.12 = (f32[2,16,1024]{2,1,0:T(8,128)S(1)}, f32[2,16,1024]{2,1,0:T(8,128)S(1)}, u32[]{:S(2)}, u32[]{:S(2)}) collective-permute-start(f32[2,16,1024]{2,1,0:T(8,128)S(1)} %get-tuple-element.12.refs_2_.refs_8_), channel_id=1, source_target_pairs={{0,3},{1,2},{2,1},{3,0},{4,7},{5,6},{6,5},{7,4},{8,11},{9,10},{10,... | collective-permute-start | bytes 393224 | tf_op jit(solution)/shard_map/ppermute | solution.py:310
  19.8 0.0 collective-permute-start.11
  19.8 0.8 %collective-permute-start.10 = (f32[2,16,1024]{2,1,0:T(8,128)S(1)}, f32[2,16,1024]{2,1,0:T(8,128)S(1)}, u32[]{:S(2)}, u32[]{:S(2)}) collective-permute-start(f32[2,16,1024]{2,1,0:T(8,128)S(1)} %get-tuple-element.12.refs_2_.refs_8_), channel_id=1, source_target_pairs={{0,1},{1,0},{2,3},{3,2},{4,5},{5,4},{6,7},{7,6},{8,9},{9,8},{10,11... | collective-permute-start | bytes 393224 | tf_op jit(solution)/shard_map/ppermute | solution.py:310
  20.5 0.6 %collective-permute-start.5 = (f32[40,128]{1,0:T(8,128)S(1)}, f32[40,128]{1,0:T(8,128)S(1)}, u32[]{:S(2)}, u32[]{:S(2)}) collective-permute-start(f32[40,128]{1,0:T(8,128)S(1)} %get-tuple-element.9.refs_0_), channel_id=1, source_target_pairs={{0,24},{4,28},{8,16},{12,20},{16,8},{20,12},{24,0},{28,4},{1,25},{... | collective-permute-start | bytes 61448 | tf_op jit(solution)/shard_map/ppermute | solution.py:310
  21.2 0.0 collective-permute-done.6.refs_7_
  21.2 0.6 %collective-permute-start.4 = (f32[40,128]{1,0:T(8,128)S(1)}, f32[40,128]{1,0:T(8,128)S(1)}, u32[]{:S(2)}, u32[]{:S(2)}) collective-permute-start(f32[40,128]{1,0:T(8,128)S(1)} %get-tuple-element.9.refs_0_), channel_id=1, source_target_pairs={{0,20},{4,16},{8,28},{12,24},{16,4},{20,0},{24,12},{28,8},{1,21},{... | collective-permute-start | bytes 61448 | tf_op jit(solution)/shard_map/ppermute | solution.py:310
  21.8 3.5 %collective-permute-done.5.refs_6_ = f32[40,128]{1,0:T(8,128)S(1)} collective-permute-done((f32[40,128]{1,0:T(8,128)S(1)}, f32[40,128]{1,0:T(8,128)S(1)}, u32[]{:S(2)}, u32[]{:S(2)}) %collective-permute-start.5) | collective-permute-done | bytes 20512 | tf_op jit(solution)/shard_map/ppermute | solution.py:310
  25.2 0.6 %collective-permute-start.3 = (f32[40,128]{1,0:T(8,128)S(1)}, f32[40,128]{1,0:T(8,128)S(1)}, u32[]{:S(2)}, u32[]{:S(2)}) collective-permute-start(f32[40,128]{1,0:T(8,128)S(1)} %get-tuple-element.9.refs_0_), channel_id=1, source_target_pairs={{0,16},{4,20},{8,24},{12,28},{16,0},{20,4},{24,8},{28,12},{1,17},{... | collective-permute-start | bytes 61448 | tf_op jit(solution)/shard_map/ppermute | solution.py:310
  25.8 0.0 collective-permute-done.4.refs_5_
  25.8 0.0 collective-permute-start.2
  25.9 3.1 %collective-permute-done.3.refs_4_ = f32[40,128]{1,0:T(8,128)S(1)} collective-permute-done((f32[40,128]{1,0:T(8,128)S(1)}, f32[40,128]{1,0:T(8,128)S(1)}, u32[]{:S(2)}, u32[]{:S(2)}) %collective-permute-start.3) | collective-permute-done | bytes 20512 | tf_op jit(solution)/shard_map/ppermute | solution.py:310
  29.0 0.6 %collective-permute-start.1 = (f32[40,128]{1,0:T(8,128)S(1)}, f32[40,128]{1,0:T(8,128)S(1)}, u32[]{:S(2)}, u32[]{:S(2)}) collective-permute-start(f32[40,128]{1,0:T(8,128)S(1)} %get-tuple-element.9.refs_0_), channel_id=1, source_target_pairs={{0,8},{4,12},{8,0},{12,4},{16,24},{20,28},{24,16},{28,20},{1,9},{5... | collective-permute-start | bytes 61448 | tf_op jit(solution)/shard_map/ppermute | solution.py:310
  29.7 0.0 collective-permute-done.2.refs_3_
  29.7 0.0 collective-permute-start
  29.7 0.0 copy-done.20
  29.7 0.7 %copy.14.adjacency = s32[32,3]{1,0:T(8,128)} copy(s32[32,3]{0,1:T(4,128)S(1)} %copy-done.20) | data formatting | bytes 768 | tf_op args[10]
  30.4 2.4 %collective-permute-done.1.refs_2_ = f32[40,128]{1,0:T(8,128)S(1)} collective-permute-done((f32[40,128]{1,0:T(8,128)S(1)}, f32[40,128]{1,0:T(8,128)S(1)}, u32[]{:S(2)}, u32[]{:S(2)}) %collective-permute-start.1) | collective-permute-done | bytes 20512 | tf_op jit(solution)/shard_map/ppermute | solution.py:310
  32.8 0.0 collective-permute-done.refs_1_
  32.8 0.0 copy-done.7
  32.8 0.0 copy-done.13
  32.8 0.0 copy-done.14
  32.8 0.0 copy-done.15
  32.8 0.0 copy-done.16
  32.8 0.0 copy-done.17
  32.9 0.5 copy-done.18
  33.4 0.0 copy-done.19
  33.4 1.9 %localize.1 = (f32[4,16,128]{2,1,0:T(8,128)}, f32[4,16,128]{2,1,0:T(8,128)}, f32[4,1,128]{2,1,0:T(1,128)}) custom-call(s32[1]{0:T(128)} %bitcast.index, s32[32,3]{1,0:T(8,128)} %copy.14.adjacency, f32[40,128]{1,0:T(8,128)} %copy-done.7, f32[40,128]{1,0:T(8,128)} %copy-done.19, f32[40,128]{1,0:T(8,128)} %copy-done.18, f32[40,128]{1,0:T(8,128)} %copy-done.17, ...), custom_call_target="tpu_custom_call" | custom-call | tf_op jit(solution)/shard_map/localize/pallas_call | solution.py:224
  35.3 3.6 %collective-permute-start.9 = (f32[4,16,128]{2,1,0:T(8,128)}, f32[4,16,128]{2,1,0:T(8,128)S(1)}, u32[]{:S(2)}, u32[]{:S(2)}) collective-permute-start(f32[4,16,128]{2,1,0:T(8,128)} %get-tuple-element.14.refs_4_), channel_id=1, source_target_pairs={{0,3},{1,2},{2,1},{3,0},{4,7},{5,6},{6,5},{7,4},{8,11},{9,10},{10,... | collective-permute-start | bytes 98312 | tf_op jit(solution)/shard_map/ppermute | solution.py:310
  38.9 0.0 collective-permute-start.8
  38.9 2.3 %collective-permute-done.9.refs_7_ = f32[4,16,128]{2,1,0:T(8,128)S(1)} collective-permute-done((f32[4,16,128]{2,1,0:T(8,128)}, f32[4,16,128]{2,1,0:T(8,128)S(1)}, u32[]{:S(2)}, u32[]{:S(2)}) %collective-permute-start.9) | collective-permute-done | bytes 32800 | tf_op jit(solution)/shard_map/ppermute | solution.py:310
  41.3 0.0 collective-permute-start.7
  41.3 2.7 %collective-permute-done.8.refs_6_ = f32[4,16,128]{2,1,0:T(8,128)S(1)} collective-permute-done((f32[4,16,128]{2,1,0:T(8,128)}, f32[4,16,128]{2,1,0:T(8,128)S(1)}, u32[]{:S(2)}, u32[]{:S(2)}) %collective-permute-start.8) | collective-permute-done | bytes 32800 | tf_op jit(solution)/shard_map/ppermute | solution.py:310
  43.9 1.4 %collective-permute-done.7.refs_5_ = f32[4,16,128]{2,1,0:T(8,128)S(1)} collective-permute-done((f32[4,16,128]{2,1,0:T(8,128)}, f32[4,16,128]{2,1,0:T(8,128)S(1)}, u32[]{:S(2)}, u32[]{:S(2)}) %collective-permute-start.7) | collective-permute-done | bytes 32800 | tf_op jit(solution)/shard_map/ppermute | solution.py:310
  45.4 0.0 collective-permute-done.12.refs_11_
  45.4 0.0 collective-permute-done.11.refs_10_
  45.4 0.0 collective-permute-done.10.refs_9_
  45.4 0.0 copy-start.5
  45.4 0.7 %copy-done.5 = f32[4,16,128]{2,1,0:T(8,128)S(1)} copy-done((f32[4,16,128]{2,1,0:T(8,128)S(1)}, f32[4,16,128]{2,1,0:T(8,128)}, u32[]{:S(2)}) %copy-start.5) | copy-done | bytes 32792
  46.2 0.8 %copy-done.6 = f32[4,16,128]{2,1,0:T(8,128)S(1)} copy-done((f32[4,16,128]{2,1,0:T(8,128)S(1)}, f32[4,16,128]{2,1,0:T(8,128)}, u32[]{:S(2)}) %copy-start.6) | copy-done | bytes 32792
  46.9 0.7 %copy-done.8 = f32[4,1,128]{2,1,0:T(1,128)S(1)} copy-done((f32[4,1,128]{2,1,0:T(1,128)S(1)}, f32[4,1,128]{2,1,0:T(1,128)}, u32[]{:S(2)}) %copy-start.8) | copy-done | bytes 2072
  47.6 10.2 %update.1 = f32[16,4,1024]{2,1,0:T(4,128)} custom-call(f32[4,16,128]{2,1,0:T(8,128)S(1)} %copy-done.6, f32[4,1,128]{2,1,0:T(1,128)S(1)} %copy-done.8, f32[2,16,1024]{2,1,0:T(8,128)S(1)} %get-tuple-element.12.refs_2_.refs_8_, f32[2,16,1024]{2,1,0:T(8,128)S(1)} %get-tuple-element.13.refs_3_, f32[4,16,128]{2,1,0:T(8,128)S(1)} %copy-done.5, ...), custom_call_target="tpu_custom_call" | custom-call | tf_op jit(solution)/shard_map/update/pallas_call | solution.py:295
  (9 shorter events, 0.0 us)
Async XLA Ops:
  0.6 29.0 %copy-start.20 = (s32[32,3]{0,1:T(4,128)S(1)}, s32[32,3]{0,1:T(4,128)}, u32[]{:S(2)}) copy-start(s32[32,3]{0,1:T(4,128)} %param.21) | copy-start | bytes 1156
  1.5 1.4 %copy-start = (f32[24,16,1024]{2,1,0:T(8,128)S(1)}, f32[24,16,1024]{2,1,0:T(8,128)}, u32[]{:S(2)}) copy-start(f32[24,16,1024]{2,1,0:T(8,128)} %rain_hbm.1) | copy-start | bytes 4718596
  2.9 0.9 %copy-start.1 = (f32[16,4,1024]{2,1,0:T(4,128)S(1)}, f32[16,4,1024]{2,1,0:T(4,128)}, u32[]{:S(2)}) copy-start(f32[16,4,1024]{2,1,0:T(4,128)} %levels.1) | copy-start | bytes 786436
  3.8 0.9 %copy-start.2 = (f32[24,1024]{1,0:T(8,128)S(1)}, f32[24,1024]{1,0:T(8,128)}, u32[]{:S(2)}) copy-start(f32[24,1024]{1,0:T(8,128)} %heat.1) | copy-start | bytes 294916
  4.7 0.9 %copy-start.3 = (f32[24,1024]{1,0:T(8,128)S(1)}, f32[24,1024]{1,0:T(8,128)}, u32[]{:S(2)}) copy-start(f32[24,1024]{1,0:T(8,128)} %evap.1) | copy-start | bytes 294916
  5.6 0.8 %copy-start.4 = (f32[10,1024]{1,0:T(8,128)S(1)}, f32[10,1024]{1,0:T(8,128)}, u32[]{:S(2)}) copy-start(f32[10,1024]{1,0:T(8,128)} %settings.1) | copy-start | bytes 122884
  6.5 0.7 %copy-start.9 = (f32[4,32]{1,0:T(4,128)S(1)}, f32[4,32]{1,0:T(4,128)}, u32[]{:S(2)}) copy-start(f32[4,32]{1,0:T(4,128)} %measured.1) | copy-start | bytes 1540
  7.2 0.7 %copy-start.10 = (f32[4,32]{1,0:T(4,128)S(1)}, f32[4,32]{1,0:T(4,128)}, u32[]{:S(2)}) copy-start(f32[4,32]{1,0:T(4,128)} %sigma.1) | copy-start | bytes 1540
  7.8 0.7 %copy-start.11 = (s32[4,32]{1,0:T(4,128)S(1)}, s32[4,32]{1,0:T(4,128)}, u32[]{:S(2)}) copy-start(s32[4,32]{1,0:T(4,128)} %position.1) | copy-start | bytes 1540
  8.5 0.7 %copy-start.12 = (s32[4,32]{1,0:T(4,128)S(1)}, s32[4,32]{1,0:T(4,128)}, u32[]{:S(2)}) copy-start(s32[4,32]{1,0:T(4,128)} %present.1) | copy-start | bytes 1540
  12.7 20.1 %copy-start.7 = (f32[40,128]{1,0:T(8,128)}, f32[40,128]{1,0:T(8,128)S(1)}, u32[]{:S(2)}) copy-start(f32[40,128]{1,0:T(8,128)S(1)} %get-tuple-element.9.refs_0_) | copy-start | bytes 61444
  12.8 8.4 %collective-permute-start.6 = (f32[40,128]{1,0:T(8,128)S(1)}, f32[40,128]{1,0:T(8,128)S(1)}, u32[]{:S(2)}, u32[]{:S(2)}) collective-permute-start(f32[40,128]{1,0:T(8,128)S(1)} %get-tuple-element.9.refs_0_), channel_id=1, source_target_pairs={{0,28},{4,24},{8,20},{12,16},{16,12},{20,8},{24,4},{28,0},{1,29},{... | collective-permute-start | bytes 61448 | tf_op jit(solution)/shard_map/ppermute | solution.py:310
  16.2 29.2 %collective-permute-start.12 = (f32[2,16,1024]{2,1,0:T(8,128)S(1)}, f32[2,16,1024]{2,1,0:T(8,128)S(1)}, u32[]{:S(2)}, u32[]{:S(2)}) collective-permute-start(f32[2,16,1024]{2,1,0:T(8,128)S(1)} %get-tuple-element.12.refs_2_.refs_8_), channel_id=1, source_target_pairs={{0,3},{1,2},{2,1},{3,0},{4,7},{5,6},{6,5},{7,4},{8,11},{9,10},{10,... | collective-permute-start | bytes 393224 | tf_op jit(solution)/shard_map/ppermute | solution.py:310
  19.8 25.6 %collective-permute-start.11 = (f32[2,16,1024]{2,1,0:T(8,128)S(1)}, f32[2,16,1024]{2,1,0:T(8,128)S(1)}, u32[]{:S(2)}, u32[]{:S(2)}) collective-permute-start(f32[2,16,1024]{2,1,0:T(8,128)S(1)} %get-tuple-element.12.refs_2_.refs_8_), channel_id=1, source_target_pairs={{0,2},{1,3},{2,0},{3,1},{4,6},{5,7},{6,4},{7,5},{8,10},{9,11},{10,... | collective-permute-start | bytes 393224 | tf_op jit(solution)/shard_map/ppermute | solution.py:310
  19.8 25.6 %collective-permute-start.10 = (f32[2,16,1024]{2,1,0:T(8,128)S(1)}, f32[2,16,1024]{2,1,0:T(8,128)S(1)}, u32[]{:S(2)}, u32[]{:S(2)}) collective-permute-start(f32[2,16,1024]{2,1,0:T(8,128)S(1)} %get-tuple-element.12.refs_2_.refs_8_), channel_id=1, source_target_pairs={{0,1},{1,0},{2,3},{3,2},{4,5},{5,4},{6,7},{7,6},{8,9},{9,8},{10,11... | collective-permute-start | bytes 393224 | tf_op jit(solution)/shard_map/ppermute | solution.py:310
  20.5 4.7 %collective-permute-start.5 = (f32[40,128]{1,0:T(8,128)S(1)}, f32[40,128]{1,0:T(8,128)S(1)}, u32[]{:S(2)}, u32[]{:S(2)}) collective-permute-start(f32[40,128]{1,0:T(8,128)S(1)} %get-tuple-element.9.refs_0_), channel_id=1, source_target_pairs={{0,24},{4,28},{8,16},{12,20},{16,8},{20,12},{24,0},{28,4},{1,25},{... | collective-permute-start | bytes 61448 | tf_op jit(solution)/shard_map/ppermute | solution.py:310
  21.2 11.6 %copy-start.13 = (f32[40,128]{1,0:T(8,128)}, f32[40,128]{1,0:T(8,128)S(1)}, u32[]{:S(2)}) copy-start(f32[40,128]{1,0:T(8,128)S(1)} %collective-permute-done.6.refs_7_) | copy-start | bytes 61444
  21.2 4.7 %collective-permute-start.4 = (f32[40,128]{1,0:T(8,128)S(1)}, f32[40,128]{1,0:T(8,128)S(1)}, u32[]{:S(2)}, u32[]{:S(2)}) collective-permute-start(f32[40,128]{1,0:T(8,128)S(1)} %get-tuple-element.9.refs_0_), channel_id=1, source_target_pairs={{0,20},{4,16},{8,28},{12,24},{16,4},{20,0},{24,12},{28,8},{1,21},{... | collective-permute-start | bytes 61448 | tf_op jit(solution)/shard_map/ppermute | solution.py:310
  25.2 7.6 %copy-start.14 = (f32[40,128]{1,0:T(8,128)}, f32[40,128]{1,0:T(8,128)S(1)}, u32[]{:S(2)}) copy-start(f32[40,128]{1,0:T(8,128)S(1)} %collective-permute-done.5.refs_6_) | copy-start | bytes 61444
  25.2 3.8 %collective-permute-start.3 = (f32[40,128]{1,0:T(8,128)S(1)}, f32[40,128]{1,0:T(8,128)S(1)}, u32[]{:S(2)}, u32[]{:S(2)}) collective-permute-start(f32[40,128]{1,0:T(8,128)S(1)} %get-tuple-element.9.refs_0_), channel_id=1, source_target_pairs={{0,16},{4,20},{8,24},{12,28},{16,0},{20,4},{24,8},{28,12},{1,17},{... | collective-permute-start | bytes 61448 | tf_op jit(solution)/shard_map/ppermute | solution.py:310
  25.8 7.0 %copy-start.15 = (f32[40,128]{1,0:T(8,128)}, f32[40,128]{1,0:T(8,128)S(1)}, u32[]{:S(2)}) copy-start(f32[40,128]{1,0:T(8,128)S(1)} %collective-permute-done.4.refs_5_) | copy-start | bytes 61444
  25.8 3.8 %collective-permute-start.2 = (f32[40,128]{1,0:T(8,128)S(1)}, f32[40,128]{1,0:T(8,128)S(1)}, u32[]{:S(2)}, u32[]{:S(2)}) collective-permute-start(f32[40,128]{1,0:T(8,128)S(1)} %get-tuple-element.9.refs_0_), channel_id=1, source_target_pairs={{0,12},{4,8},{8,4},{12,0},{16,28},{20,24},{24,20},{28,16},{1,13},{... | collective-permute-start | bytes 61448 | tf_op jit(solution)/shard_map/ppermute | solution.py:310
  29.0 3.8 %copy-start.16 = (f32[40,128]{1,0:T(8,128)}, f32[40,128]{1,0:T(8,128)S(1)}, u32[]{:S(2)}) copy-start(f32[40,128]{1,0:T(8,128)S(1)} %collective-permute-done.3.refs_4_) | copy-start | bytes 61444
  29.0 3.8 %collective-permute-start.1 = (f32[40,128]{1,0:T(8,128)S(1)}, f32[40,128]{1,0:T(8,128)S(1)}, u32[]{:S(2)}, u32[]{:S(2)}) collective-permute-start(f32[40,128]{1,0:T(8,128)S(1)} %get-tuple-element.9.refs_0_), channel_id=1, source_target_pairs={{0,8},{4,12},{8,0},{12,4},{16,24},{20,28},{24,16},{28,20},{1,9},{5... | collective-permute-start | bytes 61448 | tf_op jit(solution)/shard_map/ppermute | solution.py:310
  29.7 3.2 %copy-start.17 = (f32[40,128]{1,0:T(8,128)}, f32[40,128]{1,0:T(8,128)S(1)}, u32[]{:S(2)}) copy-start(f32[40,128]{1,0:T(8,128)S(1)} %collective-permute-done.2.refs_3_) | copy-start | bytes 61444
  29.7 3.1 %collective-permute-start = (f32[40,128]{1,0:T(8,128)S(1)}, f32[40,128]{1,0:T(8,128)S(1)}, u32[]{:S(2)}, u32[]{:S(2)}) collective-permute-start(f32[40,128]{1,0:T(8,128)S(1)} %get-tuple-element.9.refs_0_), channel_id=1, source_target_pairs={{0,4},{4,0},{8,12},{12,8},{16,20},{20,16},{24,28},{28,24},{1,5},{5... | collective-permute-start | bytes 61448 | tf_op jit(solution)/shard_map/ppermute | solution.py:310
  32.8 0.6 %copy-start.18 = (f32[40,128]{1,0:T(8,128)}, f32[40,128]{1,0:T(8,128)S(1)}, u32[]{:S(2)}) copy-start(f32[40,128]{1,0:T(8,128)S(1)} %collective-permute-done.1.refs_2_) | copy-start | bytes 61444
  32.8 0.6 %copy-start.19 = (f32[40,128]{1,0:T(8,128)}, f32[40,128]{1,0:T(8,128)S(1)}, u32[]{:S(2)}) copy-start(f32[40,128]{1,0:T(8,128)S(1)} %collective-permute-done.refs_1_) | copy-start | bytes 61444
  35.3 5.9 %collective-permute-start.9 = (f32[4,16,128]{2,1,0:T(8,128)}, f32[4,16,128]{2,1,0:T(8,128)S(1)}, u32[]{:S(2)}, u32[]{:S(2)}) collective-permute-start(f32[4,16,128]{2,1,0:T(8,128)} %get-tuple-element.14.refs_4_), channel_id=1, source_target_pairs={{0,3},{1,2},{2,1},{3,0},{4,7},{5,6},{6,5},{7,4},{8,11},{9,10},{10,... | collective-permute-start | bytes 98312 | tf_op jit(solution)/shard_map/ppermute | solution.py:310
  38.9 5.0 %collective-permute-start.8 = (f32[4,16,128]{2,1,0:T(8,128)}, f32[4,16,128]{2,1,0:T(8,128)S(1)}, u32[]{:S(2)}, u32[]{:S(2)}) collective-permute-start(f32[4,16,128]{2,1,0:T(8,128)} %get-tuple-element.14.refs_4_), channel_id=1, source_target_pairs={{0,2},{1,3},{2,0},{3,1},{4,6},{5,7},{6,4},{7,5},{8,10},{9,11},{10,... | collective-permute-start | bytes 98312 | tf_op jit(solution)/shard_map/ppermute | solution.py:310
  41.3 4.1 %collective-permute-start.7 = (f32[4,16,128]{2,1,0:T(8,128)}, f32[4,16,128]{2,1,0:T(8,128)S(1)}, u32[]{:S(2)}, u32[]{:S(2)}) collective-permute-start(f32[4,16,128]{2,1,0:T(8,128)} %get-tuple-element.14.refs_4_), channel_id=1, source_target_pairs={{0,1},{1,0},{2,3},{3,2},{4,5},{5,4},{6,7},{7,6},{8,9},{9,8},{10,11... | collective-permute-start | bytes 98312 | tf_op jit(solution)/shard_map/ppermute | solution.py:310
  45.4 0.8 %copy-start.5 = (f32[4,16,128]{2,1,0:T(8,128)S(1)}, f32[4,16,128]{2,1,0:T(8,128)}, u32[]{:S(2)}) copy-start(f32[4,16,128]{2,1,0:T(8,128)} %get-tuple-element.14.refs_4_) | copy-start | bytes 98308
  46.2 0.8 %copy-start.6 = (f32[4,16,128]{2,1,0:T(8,128)S(1)}, f32[4,16,128]{2,1,0:T(8,128)}, u32[]{:S(2)}) copy-start(f32[4,16,128]{2,1,0:T(8,128)} %get-tuple-element.10.refs_0_) | copy-start | bytes 98308
  46.9 0.7 %copy-start.8 = (f32[4,1,128]{2,1,0:T(1,128)S(1)}, f32[4,1,128]{2,1,0:T(1,128)}, u32[]{:S(2)}) copy-start(f32[4,1,128]{2,1,0:T(1,128)} %get-tuple-element.11.refs_1_) | copy-start | bytes 6148

commit v2 on v1

--- a/solution.py
+++ b/solution.py
@@ -19,7 +19,7 @@
 STRIP = 512
 CHUNK = 6
 PACK = 40
-VMEM_LIMIT = 48 * 1024 * 1024
+VMEM_LIMIT = 16 * 1024 * 1024
 
 
 def lanes_of(table):
@@ -34,35 +34,20 @@
     return [high, middle, low]
 
 
-def forecast_kernel(
-    levels,
-    settings,
-    rain_hbm,
-    heat,
-    evap,
-    measured,
-    sigma,
-    draws,
-    position,
-    present,
-    flow_hbm,
-    wet_state,
-    dry_state,
-    pack,
-    rain,
-    flow,
-    share,
-    melt_cap,
-    last_flow,
-    in_sems,
-    out_sems,
-):
-    hours, members, width = rain_hbm.shape
+def forecast_kernel(*refs):
+    inputs, (flow_hbm, wet_state, dry_state, pack) = refs[:10], refs[10:14]
+    held, (flow, share, melt_cap, last_flow, held_sems, in_sems, out_sems) = refs[14:24], refs[24:]
+    levels, settings, rain, heat, evap, measured, sigma, draws, position, present = held
+    rain_hbm = inputs[2]
+    hours, members, width = rain.shape
     strip = min(STRIP, width)
     pieces = [(s, c) for s in range(width // strip) for c in range(hours // CHUNK)]
 
     def part(s, c):
         return (pl.ds(c * CHUNK, CHUNK), slice(None), pl.ds(s * strip, strip))
+
+    def whole_copy(k):
+        return pltpu.make_async_copy(inputs[k], held[k], held_sems.at[k])
 
     def rain_copy(n):
         where = part(*pieces[n])
@@ -72,14 +57,22 @@
         where = part(*pieces[n])
         return pltpu.make_async_copy(flow.at[where], flow_hbm.at[where], out_sems.at[n])
 
+    for k in (1, 3, 4, 0):
+        whole_copy(k).start()
     for n in range(len(pieces)):
         rain_copy(n).start()
+    for k in range(5, 10):
+        whole_copy(k).start()
 
     def parameter(k, where=slice(None)):
         return PARAM_LOW[k] + (PARAM_HIGH[k] - PARAM_LOW[k]) * settings[k : k + 1, where]
 
+    whole_copy(1).wait()
+    whole_copy(3).wait()
     share[...] = jnp.clip((parameter(0) + 1.0 - heat[...]) * 0.5, 0.0, 1.0)
     melt_cap[...] = parameter(1) * jnp.maximum(heat[...] - parameter(0), 0.0)
+    whole_copy(4).wait()
+    whole_copy(0).wait()
 
     for s in range(width // strip):
         where = pl.ds(s * strip, strip)
@@ -131,6 +124,8 @@
         dry_state[1, :, where] = lower
         last_flow[:, where] = 0.45 * moist * inv_cap
 
+    for k in range(5, 10):
+        whole_copy(k).wait()
     slots = lanes_of(position[...])
     pick = (lax.broadcasted_iota(jnp.int32, (NB, LOCAL), 0) == slots).astype(jnp.bfloat16)
     blocks = width // NB
@@ -148,7 +143,7 @@
         chosen = jnp.where(lane % OBS < OBS // 2, gauge, smap)
         predicted = jnp.where(lane // OBS == b, chosen, predicted)
     sd = lanes_of(sigma[...])
-    spread = jnp.transpose(draws[...].reshape(LOCAL, members))
+    spread = jnp.concatenate([draws[b] for b in range(blocks)], axis=1)
     pack[0:members] = predicted
     pack[members : 2 * members] = lanes_of(measured[...]) + sd * spread
     tail = pack.shape[0] - 2 * members
@@ -159,12 +154,12 @@
         flow_copy(n).wait()
 
 
-def forecast(levels, settings, rain, heat, evap, measured, sigma, draws, position, present):
-    hours, members, width = rain.shape
+def forecast(*arrays):
+    hours, members, width = arrays[2].shape
     copies = (width // min(STRIP, width)) * (hours // CHUNK)
     f32 = jnp.float32
     vmem = pl.BlockSpec(memory_space=pltpu.VMEM)
-    hbm = pl.BlockSpec(memory_space=pl.ANY)
+    hbm = pl.BlockSpec(memory_space=pltpu.HBM)
     return pl.pallas_call(
         forecast_kernel,
         out_shape=(
@@ -173,28 +168,29 @@
             jax.ShapeDtypeStruct((2, members, width), f32),
             jax.ShapeDtypeStruct((2 * members + 8, LOCAL), f32),
         ),
-        in_specs=[vmem, vmem, hbm] + [vmem] * 7,
+        in_specs=[hbm] * len(arrays),
         out_specs=(hbm, vmem, vmem, vmem),
-        scratch_shapes=[
-            pltpu.VMEM((hours, members, width), f32),
+        scratch_shapes=[pltpu.VMEM(x.shape, x.dtype) for x in arrays]
+        + [
             pltpu.VMEM((hours, members, width), f32),
             pltpu.VMEM((hours, width), f32),
             pltpu.VMEM((hours, width), f32),
             pltpu.VMEM((members, width), f32),
+            pltpu.SemaphoreType.DMA((len(arrays),)),
             pltpu.SemaphoreType.DMA((copies,)),
             pltpu.SemaphoreType.DMA((copies,)),
         ],
         compiler_params=pltpu.CompilerParams(vmem_limit_bytes=VMEM_LIMIT),
         name="forecast",
-    )(levels, settings, rain, heat, evap, measured, sigma, draws, position, present)
+    )(*(pltpu.with_memory_space_constraint(x, pltpu.HBM) for x in arrays))
 
 
 def localize_kernel(relative, count, index, adjacency, *refs):
     pieces, (pred_out, innov_out, weight_out, table) = refs[:count], refs[count:]
     at = 0
     for piece in pieces:
-        n = piece.shape[0] if len(piece.shape) == 3 else 1
-        table[at : at + n] = piece[...].reshape((n,) + table.shape[1:])
+        n = piece.shape[0]
+        table[at : at + n] = piece[...]
         at += n
     me = index[0]
     blocks, members, _ = pred_out.shape
@@ -203,7 +199,7 @@
     for b in range(blocks):
         local = jnp.zeros((rows, LOCAL), jnp.float32)
         for i in range(NBR + 1):
-            source = me * blocks + b if i == 0 else adjacency[me * blocks + b, i - 1]
+            source = me * blocks + b if i == 0 else adjacency[i - 1, me * blocks + b]
             owner = source // blocks
             if relative:
                 owner = owner ^ me
@@ -218,7 +214,7 @@
 def localize(pieces, relative, index, adjacency, blocks, members):
     f32 = jnp.float32
     rows = 2 * members + 8
-    total = sum(p.shape[0] if p.ndim == 3 else 1 for p in pieces)
+    total = sum(p.shape[0] for p in pieces)
     vmem = pl.BlockSpec(memory_space=pltpu.VMEM)
     smem = pl.BlockSpec(memory_space=pltpu.SMEM)
     return pl.pallas_call(
@@ -231,85 +227,151 @@
         in_specs=[smem, smem] + [vmem] * len(pieces),
         out_specs=(vmem, vmem, vmem),
         scratch_shapes=[pltpu.VMEM((total, rows, LOCAL), f32)],
+        compiler_params=pltpu.CompilerParams(vmem_limit_bytes=VMEM_LIMIT),
         name="localize",
     )(index, adjacency, *pieces)
 
 
-def eliminate(systems):
-    size = systems[0][0].shape[0]
-    groups = size // 8
+def spread_lane(x, k):
+    return jnp.broadcast_to(x[:, k : k + 1], (8, LOCAL))
+
+
+def spread_row(x, k):
+    return jnp.broadcast_to(x[k : k + 1], (8, LOCAL))
+
+
+def reduce_rows(rows, first):
     sub = lax.broadcasted_iota(jnp.int32, (8, LOCAL), 0)
-    mats = [[m[g * 8 : g * 8 + 8] for g in range(groups)] for (m,) in systems]
-    for k in range(size):
-        home, at = divmod(k, 8)
-        for mat in mats:
-            columns = [jnp.broadcast_to(part[:, k : k + 1], (8, LOCAL)) for part in mat]
-            pivot = jnp.broadcast_to(columns[home][at : at + 1], (8, LOCAL))
-            row = jnp.broadcast_to(mat[home][at : at + 1], (8, LOCAL)) / pivot
-            for g in range(groups):
-                part = mat[g] - columns[g] * row
-                mat[g] = jnp.where(sub == at, row, part) if g == home else part
-    return [jnp.concatenate(mat, axis=0) for mat in mats]
-
-
-def update_kernel(count, *refs):
+    columns = [spread_lane(rows, first + j) for j in range(8)]
+    for j in range(8):
+        inverse = 1.0 / spread_row(columns[j], j)
+        for i in range(j + 1, 8):
+            scaled = spread_row(columns[i], j) * inverse
+            columns[i] = jnp.where(sub == j, scaled, columns[i] - columns[j] * scaled)
+        scaled = spread_row(rows, j) * inverse
+        rows = jnp.where(sub == j, scaled, rows - columns[j] * scaled)
+    return rows
+
+
+def solve(systems):
+    size = systems[0].shape[0]
+    half = size // 2
+    groups = half // 8
+
+    def reduce_half(mats, first):
+        mats = [[m[g * 8 : g * 8 + 8] for g in range(groups)] for m in mats]
+        for p in range(groups):
+            for mat in mats:
+                at = first + p * 8
+                mat[p] = reduce_rows(mat[p], at)
+                rows = [spread_row(mat[p], j) for j in range(8)]
+                for g in range(groups):
+                    if g != p:
+                        terms = [spread_lane(mat[g], at + j) * rows[j] for j in range(8)]
+                        while len(terms) > 1:
+                            terms = [terms[i] + terms[i + 1] for i in range(0, len(terms), 2)]
+                        mat[g] = mat[g] - terms[0]
+        return [jnp.concatenate(mat, axis=0) for mat in mats]
+
+    def minus(x, left, right):
+        return x - jnp.dot(left, right, precision=HIGHEST, preferred_element_type=jnp.float32)
+
+    tops = reduce_half([m[:half] for m in systems], 0)
+    lows = [minus(m[half:], m[half:, :half], top) for m, top in zip(systems, tops)]
+    lows = reduce_half(lows, half)
+    tops = [minus(top, top[:, half:size], low) for top, low in zip(tops, lows)]
+    return [jnp.concatenate([top, low], axis=0) for top, low in zip(tops, lows)]
+
+
+def update_kernel(count, others, *refs):
     innov, weight, wet_own, dry = refs[:4]
-    preds, wets = refs[4 : 4 + count], refs[4 + count : 4 + 2 * count]
-    analysis = refs[-1]
+    preds, wets = refs[4 : 4 + count], refs[4 + count : 4 + count + others]
+    analysis_hbm, analysis, out_sems = refs[4 + count + others :]
     blocks, members, _ = innov.shape
+
+    def out_copy(b):
+        where = (slice(None), slice(None), pl.ds(b * NB, NB))
+        return pltpu.make_async_copy(analysis.at[where], analysis_hbm.at[where], out_sems.at[b])
+
     systems = []
     for b in range(blocks):
-        pred = jnp.concatenate([p[b] if len(p.shape) == 3 else p[:, b].reshape(-1, LOCAL) for p in preds], axis=0)
+        pred = jnp.concatenate(
+            [p[b] if len(p.shape) == 3 else p[:, b].reshape(-1, LOCAL) for p in preds], axis=0
+        )
         total = pred.shape[0]
         scaled = (pred - jnp.mean(pred, axis=0, keepdims=True)) * weight[b]
         both = jnp.concatenate(
             [scaled, innov[b], jnp.zeros((LOCAL - total - members, LOCAL), jnp.float32)], axis=0
         )
         matrix = lax.dot_general(
-            scaled, both, (((1,), (1,)), ((), ())), precision=HIGHEST, preferred_element_type=jnp.float32
+            scaled,
+            both,
+            (((1,), (1,)), ((), ())),
+            precision=HIGHEST,
+            preferred_element_type=jnp.float32,
         )
         rows = lax.broadcasted_iota(jnp.int32, (total, LOCAL), 0)
         cols = lax.broadcasted_iota(jnp.int32, (total, LOCAL), 1)
-        systems.append((matrix + jnp.where(rows == cols, float(total - 1), 0.0),))
-    solved = eliminate(systems)
+        systems.append(matrix + jnp.where(rows == cols, float(total - 1), 0.0))
+    solved = solve(systems)
+    analysis[:, 0, :] = dry[0]
+    analysis[:, 3, :] = dry[1]
     for b in range(blocks):
         where = pl.ds(b * NB, NB)
         gain = solved[b]
         gain = gain - jnp.mean(gain, axis=0, keepdims=True)
         turned = jnp.transpose(gain)[total : total + members]
         for k, slot in ((0, 1), (1, 2)):
-            states = jnp.concatenate(
-                [w[k, :, where] if len(w.shape) == 3 else w[:, k, :, where].reshape(-1, NB) for w in wets], axis=0
+            if len(wets[0].shape) == 3:
+                states = [wet_own[k, :, where]] + [w[k, :, where] for w in wets]
+            else:
+                states = [w[:, k, :, where].reshape(-1, NB) for w in wets]
+            analysis[:, slot, where] = wet_own[k, :, where] + jnp.dot(
+                turned,
+                jnp.concatenate(states, axis=0),
+                precision=HIGHEST,
+                preferred_element_type=jnp.float32,
             )
-            analysis[:, slot, where] = wet_own[k, :, where] + jnp.dot(
-                turned, states, precision=HIGHEST, preferred_element_type=jnp.float32
-            )
-    analysis[:, 0, :] = dry[0]
-    analysis[:, 3, :] = dry[1]
+        out_copy(b).start()
+    for b in range(blocks):
+        out_copy(b).wait()
 
 
 def update(innov, weight, wet, dry, preds, wets):
     _, members, width = wet.shape
     vmem = pl.BlockSpec(memory_space=pltpu.VMEM)
-    count = len(preds)
+    hbm = pl.BlockSpec(memory_space=pltpu.HBM)
     return pl.pallas_call(
-        functools.partial(update_kernel, count),
+        functools.partial(update_kernel, len(preds), len(wets)),
         out_shape=jax.ShapeDtypeStruct((members, 4, width), jnp.float32),
-        in_specs=[vmem] * (4 + 2 * count),
-        out_specs=vmem,
+        in_specs=[vmem] * (4 + len(preds) + len(wets)),
+        out_specs=hbm,
+        scratch_shapes=[
+            pltpu.VMEM((members, 4, width), jnp.float32),
+            pltpu.SemaphoreType.DMA((width // NB,)),
+        ],
         compiler_params=pltpu.CompilerParams(vmem_limit_bytes=VMEM_LIMIT),
         name="update",
     )(innov, weight, wet, dry, *preds, *wets)
 
 
-def exchange(x, axis, limit=8):
-    size = lax.axis_size(axis)
-    if size > limit:
-        return [lax.all_gather(x, axis, axis=0, tiled=False)], False
-    others = [
-        lax.ppermute(x, axis, [(i, i ^ s) for i in range(size)]) for s in range(1, size)
-    ]
-    return [x] + others, True
+def permute(x, axis, mask):
+    return lax.ppermute(x, axis, [(i, i ^ mask) for i in range(lax.axis_size(axis))])
+
+
+def over_members(x):
+    size = lax.axis_size("member")
+    if size > 4:
+        return [lax.all_gather(x, "member", axis=0)]
+    return [permute(x, "member", mask) for mask in range(1, size)]
+
+
+def over_basins(pack):
+    size = lax.axis_size("basin")
+    if size > 8:
+        return [lax.all_gather(pack, "basin", axis=0)], False
+    pair = jnp.stack([pack, permute(pack, "basin", 1)])
+    return [pair] + [permute(pair, "basin", mask) for mask in range(2, size, 2)], True
 
 
 def on_device(
@@ -335,15 +397,19 @@
         potential_evapotranspiration,
         gauge_measured_values,
         gauge_deviation_sigma,
-        gauge_perturbation_draws,
+        jnp.transpose(gauge_perturbation_draws, (0, 2, 1)),
         gauge_catchment_position,
         gauge_present_flag,
     )
     index = jnp.full((1,), lax.axis_index("basin"), jnp.int32)
-    packs, relative = exchange(pack, "basin")
-    pred, innov, weight = localize(packs, relative, index, adjacent_block_list, blocks, members)
-    preds, _ = exchange(pred, "member", 4)
-    wets, _ = exchange(wet, "member", 4)
+    packs, relative = over_basins(pack)
+    pred, innov, weight = localize(
+        packs, relative, index, jnp.transpose(adjacent_block_list), blocks, members
+    )
+    preds = over_members(pred)
+    wets = over_members(wet)
+    if len(preds) > 1:
+        preds = [pred] + preds
     analysis = update(innov, weight, wet, dry, preds, wets)
     return (analysis, discharge)
 

time: 58.5 us -> 34.5 us (0.59)
  local copies, waits for them, and re-layouts: 12 us -> 0.01 us
  waiting for transfers between devices: 15.5 us -> 8.64 us
  Pallas kernels: 15.7 us -> 9.66 us
  starting transfers between devices: 13.9 us -> 15.4 us
    unnamed x44 -> x2, local copies, waits for them, and re-layouts: 12 us -> 0.01 us
    ppermute x13 -> x10, waiting for transfers between devices: 15.5 us -> 8.64 us  [permute(): lax.ppermute(x, axis, [(i, i ^ mask) for i in range(lax.axis_size(axis))])]
    pallas_call x1, Pallas kernels: 10.2 us -> 4.14 us  [update(): pl.pallas_call(functools.partial(update_kernel, len(preds), len(wets)), o...]
    ppermute x13 -> x10, starting transfers between devices: 13.9 us -> 15.4 us  [permute(): lax.ppermute(x, axis, [(i, i ^ mask) for i in range(lax.axis_size(axis))])]
    pallas_call x1, Pallas kernels: 3.54 us -> 4.73 us  [forecast(): pl.pallas_call(forecast_kernel, out_shape=(jax.ShapeDtypeStruct((hours, m...]
    pallas_call x1, Pallas kernels: 1.9 us -> 0.79 us  [localize(): pl.pallas_call(functools.partial(localize_kernel, relative, len(pieces)),...]
  transfers between devices with their start and end apart: 13 -> 10, of which waited for: 6 -> 6; matrix products, arithmetic and copies ran while one was open for 1% -> 0% of each run, Pallas kernels for 3% -> 2%
where the time goes in v2:
time: 34.5 us; the launch traced here: 34.3 us
  starting transfers between devices  15.4 us (45%)
  Pallas kernels  9.66 us (28%)
  waiting for transfers between devices  8.64 us (25%)
  between operations  0.67 us (2%)
    ppermute x10, starting transfers between devices, permute(): lax.ppermute(x, axis, [(i, i ^ mask) for i in range(lax.axis_size(axis))])  15.4 us
    ppermute x10, waiting for transfers between devices, permute(): lax.ppermute(x, axis, [(i, i ^ mask) for i in range(lax.axis_size(axis))])  8.64 us
    pallas_call x1, Pallas kernels, forecast(): pl.pallas_call(forecast_kernel, out_shape=(jax.ShapeDtypeStruct((hours, m...  4.73 us
    pallas_call x1, Pallas kernels, update(): pl.pallas_call(functools.partial(update_kernel, len(preds), len(wets)), o...  4.14 us
    pallas_call x1, Pallas kernels, localize(): pl.pallas_call(functools.partial(localize_kernel, relative, len(pieces)),...  0.79 us
  transfers between devices with their start and end apart: 10, of which 6 were waited for; matrix products, arithmetic and copies ran while one was open for 0% of the time, Pallas kernels for 2%

profile of v2, /device:TPU:0, one launch (start us, length us, event | category | flops | bytes accessed | tf_op | source)
XLA Modules:
  0.0 34.3 jit_solution(14361469522813556869)
XLA Ops:
  0.6 0.0 copy-start
  0.6 4.7 %forecast.1 = (f32[24,16,1024]{2,1,0:T(8,128)}, f32[2,16,1024]{2,1,0:T(8,128)S(1)}, f32[2,16,1024]{2,1,0:T(8,128)S(1)}, f32[40,128]{1,0:T(8,128)S(1)}) custom-call(f32[16,4,1024]{2,1,0:T(4,128)} %refs_0_.1, f32[10,1024]{1,0:T(8,128)} %refs_1_.1, f32[24,16,1024]{2,1,0:T(8,128)} %refs_2_.1, f32[24,1024]{1,0:T(8,128)} %refs_3_.1, f32[24,1024]{1,0:T(8,128)} %refs_4_.1, ...), custom_call_target="tpu_custom_call" | custom-call | tf_op jit(solution)/shard_map/forecast/pallas_call | solution.py:163
  5.4 0.5 %collective-permute-start = (f32[40,128]{1,0:T(8,128)S(1)}, f32[40,128]{1,0:T(8,128)S(1)}, u32[]{:S(2)}, u32[]{:S(2)}) collective-permute-start(f32[40,128]{1,0:T(8,128)S(1)} %get-tuple-element.9), channel_id=1, source_target_pairs={{0,4},{4,0},{8,12},{12,8},{16,20},{20,16},{24,28},{28,24},{1,5},{5... | collective-permute-start | bytes 61448 | tf_op jit(solution)/shard_map/ppermute | solution.py:359
  5.9 0.8 %collective-permute-done = f32[40,128]{1,0:T(8,128)S(1)} collective-permute-done((f32[40,128]{1,0:T(8,128)S(1)}, f32[40,128]{1,0:T(8,128)S(1)}, u32[]{:S(2)}, u32[]{:S(2)}) %collective-permute-start) | collective-permute-done | bytes 20512 | tf_op jit(solution)/shard_map/ppermute | solution.py:359
  6.7 3.8 %collective-permute-start.3 = (f32[2,40,128]{2,1,0:T(8,128)S(1)}, f32[2,40,128]{2,1,0:T(8,128)S(1)}, u32[]{:S(2)}, u32[]{:S(2)}) collective-permute-start(f32[2,40,128]{2,1,0:T(8,128)S(1)} %pad_maximum_fusion.refs_0_), channel_id=1, source_target_pairs={{0,24},{4,28},{8,16},{12,20},{16,8},{20,12},{24,0},{28,4},{1,25},{... | collective-permute-start | bytes 122888 | tf_op jit(solution)/shard_map/ppermute | solution.py:359
  10.5 3.6 %collective-permute-start.9 = (f32[2,16,1024]{2,1,0:T(8,128)S(1)}, f32[2,16,1024]{2,1,0:T(8,128)S(1)}, u32[]{:S(2)}, u32[]{:S(2)}) collective-permute-start(f32[2,16,1024]{2,1,0:T(8,128)S(1)} %get-tuple-element.12.refs_2_), channel_id=1, source_target_pairs={{0,3},{1,2},{2,1},{3,0},{4,7},{5,6},{6,5},{7,4},{8,11},{9,10},{10,... | collective-permute-start | bytes 393224 | tf_op jit(solution)/shard_map/ppermute | solution.py:359
  14.1 0.0 collective-permute-start.8
  14.1 0.8 %collective-permute-start.7 = (f32[2,16,1024]{2,1,0:T(8,128)S(1)}, f32[2,16,1024]{2,1,0:T(8,128)S(1)}, u32[]{:S(2)}, u32[]{:S(2)}) collective-permute-start(f32[2,16,1024]{2,1,0:T(8,128)S(1)} %get-tuple-element.12.refs_2_), channel_id=1, source_target_pairs={{0,1},{1,0},{2,3},{3,2},{4,5},{5,4},{6,7},{7,6},{8,9},{9,8},{10,11... | collective-permute-start | bytes 393224 | tf_op jit(solution)/shard_map/ppermute | solution.py:359
  14.9 0.5 %collective-permute-start.2 = (f32[2,40,128]{2,1,0:T(8,128)S(1)}, f32[2,40,128]{2,1,0:T(8,128)S(1)}, u32[]{:S(2)}, u32[]{:S(2)}) collective-permute-start(f32[2,40,128]{2,1,0:T(8,128)S(1)} %pad_maximum_fusion.refs_0_), channel_id=1, source_target_pairs={{0,16},{4,20},{8,24},{12,28},{16,0},{20,4},{24,8},{28,12},{1,17},{... | collective-permute-start | bytes 122888 | tf_op jit(solution)/shard_map/ppermute | solution.py:359
  15.4 0.0 collective-permute-done.3.refs_3_
  15.4 0.3 collective-permute-start.1
  15.8 3.2 %collective-permute-done.2.refs_2_ = f32[2,40,128]{2,1,0:T(8,128)S(1)} collective-permute-done((f32[2,40,128]{2,1,0:T(8,128)S(1)}, f32[2,40,128]{2,1,0:T(8,128)S(1)}, u32[]{:S(2)}, u32[]{:S(2)}) %collective-permute-start.2) | collective-permute-done | bytes 40992 | tf_op jit(solution)/shard_map/ppermute | solution.py:359
  18.9 0.5 %collective-permute-done.1.refs_1_ = f32[2,40,128]{2,1,0:T(8,128)S(1)} collective-permute-done((f32[2,40,128]{2,1,0:T(8,128)S(1)}, f32[2,40,128]{2,1,0:T(8,128)S(1)}, u32[]{:S(2)}, u32[]{:S(2)}) %collective-permute-start.1) | collective-permute-done | bytes 40992 | tf_op jit(solution)/shard_map/ppermute | solution.py:359
  19.4 0.0 copy-done
  19.4 0.8 %localize.1 = (f32[4,16,128]{2,1,0:T(8,128)S(1)}, f32[4,16,128]{2,1,0:T(8,128)S(1)}, f32[4,1,128]{2,1,0:T(1,128)S(1)}) custom-call(s32[1]{0:T(128)} %bitcast.index, s32[3,32]{1,0:T(4,128)S(1)} %bitcast.6, f32[2,40,128]{2,1,0:T(8,128)S(1)} %pad_maximum_fusion.refs_0_, f32[2,40,128]{2,1,0:T(8,128)S(1)} %collective-permute-done.1.refs_1_, ...), custom_call_target="tpu_custom_call" | custom-call | tf_op jit(solution)/shard_map/localize/pallas_call | solution.py:220
  20.2 3.7 %collective-permute-start.6 = (f32[4,16,128]{2,1,0:T(8,128)S(1)}, f32[4,16,128]{2,1,0:T(8,128)S(1)}, u32[]{:S(2)}, u32[]{:S(2)}) collective-permute-start(f32[4,16,128]{2,1,0:T(8,128)S(1)} %get-tuple-element.14.refs_4_), channel_id=1, source_target_pairs={{0,3},{1,2},{2,1},{3,0},{4,7},{5,6},{6,5},{7,4},{8,11},{9,10},{10,... | collective-permute-start | bytes 98312 | tf_op jit(solution)/shard_map/ppermute | solution.py:359
  23.9 0.0 collective-permute-start.5
  23.9 2.2 %collective-permute-done.6.refs_7_ = f32[4,16,128]{2,1,0:T(8,128)S(1)} collective-permute-done((f32[4,16,128]{2,1,0:T(8,128)S(1)}, f32[4,16,128]{2,1,0:T(8,128)S(1)}, u32[]{:S(2)}, u32[]{:S(2)}) %collective-permute-start.6) | collective-permute-done | bytes 32800 | tf_op jit(solution)/shard_map/ppermute | solution.py:359
  26.1 2.2 %collective-permute-start.4 = (f32[4,16,128]{2,1,0:T(8,128)S(1)}, f32[4,16,128]{2,1,0:T(8,128)S(1)}, u32[]{:S(2)}, u32[]{:S(2)}) collective-permute-start(f32[4,16,128]{2,1,0:T(8,128)S(1)} %get-tuple-element.14.refs_4_), channel_id=1, source_target_pairs={{0,1},{1,0},{2,3},{3,2},{4,5},{5,4},{6,7},{7,6},{8,9},{9,8},{10,11... | collective-permute-start | bytes 98312 | tf_op jit(solution)/shard_map/ppermute | solution.py:359
  28.3 0.4 %collective-permute-done.5.refs_6_ = f32[4,16,128]{2,1,0:T(8,128)S(1)} collective-permute-done((f32[4,16,128]{2,1,0:T(8,128)S(1)}, f32[4,16,128]{2,1,0:T(8,128)S(1)}, u32[]{:S(2)}, u32[]{:S(2)}) %collective-permute-start.5) | collective-permute-done | bytes 32800 | tf_op jit(solution)/shard_map/ppermute | solution.py:359
  28.7 1.5 %collective-permute-done.4.refs_5_ = f32[4,16,128]{2,1,0:T(8,128)S(1)} collective-permute-done((f32[4,16,128]{2,1,0:T(8,128)S(1)}, f32[4,16,128]{2,1,0:T(8,128)S(1)}, u32[]{:S(2)}, u32[]{:S(2)}) %collective-permute-start.4) | collective-permute-done | bytes 32800 | tf_op jit(solution)/shard_map/ppermute | solution.py:359
  30.2 0.0 collective-permute-done.9.refs_10_
  30.2 0.0 collective-permute-done.8.refs_9_
  30.2 0.0 collective-permute-done.7.refs_8_
  30.2 4.1 %update.1 = f32[16,4,1024]{2,1,0:T(4,128)} custom-call(f32[4,16,128]{2,1,0:T(8,128)S(1)} %get-tuple-element.10.refs_0_, f32[4,1,128]{2,1,0:T(1,128)S(1)} %get-tuple-element.11.refs_1_, f32[2,16,1024]{2,1,0:T(8,128)S(1)} %get-tuple-element.12.refs_2_, f32[2,16,1024]{2,1,0:T(8,128)S(1)} %get-tuple-element.13.refs_3_, ...), custom_call_target="tpu_custom_call" | custom-call | tf_op jit(solution)/shard_map/update/pallas_call | solution.py:344
  (1 shorter events, 0.0 us)
Async XLA Ops:
  0.6 18.8 %copy-start = (s32[32,3]{0,1:T(4,128)S(1)}, s32[32,3]{0,1:T(4,128)}, u32[]{:S(2)}) copy-start(s32[32,3]{0,1:T(4,128)} %param.21) | copy-start | bytes 1156
  5.4 1.4 %collective-permute-start = (f32[40,128]{1,0:T(8,128)S(1)}, f32[40,128]{1,0:T(8,128)S(1)}, u32[]{:S(2)}, u32[]{:S(2)}) collective-permute-start(f32[40,128]{1,0:T(8,128)S(1)} %get-tuple-element.9), channel_id=1, source_target_pairs={{0,4},{4,0},{8,12},{12,8},{16,20},{20,16},{24,28},{28,24},{1,5},{5... | collective-permute-start | bytes 61448 | tf_op jit(solution)/shard_map/ppermute | solution.py:359
  6.7 8.7 %collective-permute-start.3 = (f32[2,40,128]{2,1,0:T(8,128)S(1)}, f32[2,40,128]{2,1,0:T(8,128)S(1)}, u32[]{:S(2)}, u32[]{:S(2)}) collective-permute-start(f32[2,40,128]{2,1,0:T(8,128)S(1)} %pad_maximum_fusion.refs_0_), channel_id=1, source_target_pairs={{0,24},{4,28},{8,16},{12,20},{16,8},{20,12},{24,0},{28,4},{1,25},{... | collective-permute-start | bytes 122888 | tf_op jit(solution)/shard_map/ppermute | solution.py:359
  10.5 19.6 %collective-permute-start.9 = (f32[2,16,1024]{2,1,0:T(8,128)S(1)}, f32[2,16,1024]{2,1,0:T(8,128)S(1)}, u32[]{:S(2)}, u32[]{:S(2)}) collective-permute-start(f32[2,16,1024]{2,1,0:T(8,128)S(1)} %get-tuple-element.12.refs_2_), channel_id=1, source_target_pairs={{0,3},{1,2},{2,1},{3,0},{4,7},{5,6},{6,5},{7,4},{8,11},{9,10},{10,... | collective-permute-start | bytes 393224 | tf_op jit(solution)/shard_map/ppermute | solution.py:359
  14.1 16.0 %collective-permute-start.8 = (f32[2,16,1024]{2,1,0:T(8,128)S(1)}, f32[2,16,1024]{2,1,0:T(8,128)S(1)}, u32[]{:S(2)}, u32[]{:S(2)}) collective-permute-start(f32[2,16,1024]{2,1,0:T(8,128)S(1)} %get-tuple-element.12.refs_2_), channel_id=1, source_target_pairs={{0,2},{1,3},{2,0},{3,1},{4,6},{5,7},{6,4},{7,5},{8,10},{9,11},{10,... | collective-permute-start | bytes 393224 | tf_op jit(solution)/shard_map/ppermute | solution.py:359
  14.1 16.0 %collective-permute-start.7 = (f32[2,16,1024]{2,1,0:T(8,128)S(1)}, f32[2,16,1024]{2,1,0:T(8,128)S(1)}, u32[]{:S(2)}, u32[]{:S(2)}) collective-permute-start(f32[2,16,1024]{2,1,0:T(8,128)S(1)} %get-tuple-element.12.refs_2_), channel_id=1, source_target_pairs={{0,1},{1,0},{2,3},{3,2},{4,5},{5,4},{6,7},{7,6},{8,9},{9,8},{10,11... | collective-permute-start | bytes 393224 | tf_op jit(solution)/shard_map/ppermute | solution.py:359
  14.9 4.0 %collective-permute-start.2 = (f32[2,40,128]{2,1,0:T(8,128)S(1)}, f32[2,40,128]{2,1,0:T(8,128)S(1)}, u32[]{:S(2)}, u32[]{:S(2)}) collective-permute-start(f32[2,40,128]{2,1,0:T(8,128)S(1)} %pad_maximum_fusion.refs_0_), channel_id=1, source_target_pairs={{0,16},{4,20},{8,24},{12,28},{16,0},{20,4},{24,8},{28,12},{1,17},{... | collective-permute-start | bytes 122888 | tf_op jit(solution)/shard_map/ppermute | solution.py:359
  15.4 4.0 %collective-permute-start.1 = (f32[2,40,128]{2,1,0:T(8,128)S(1)}, f32[2,40,128]{2,1,0:T(8,128)S(1)}, u32[]{:S(2)}, u32[]{:S(2)}) collective-permute-start(f32[2,40,128]{2,1,0:T(8,128)S(1)} %pad_maximum_fusion.refs_0_), channel_id=1, source_target_pairs={{0,8},{4,12},{8,0},{12,4},{16,24},{20,28},{24,16},{28,20},{1,9},{5... | collective-permute-start | bytes 122888 | tf_op jit(solution)/shard_map/ppermute | solution.py:359
  20.2 5.9 %collective-permute-start.6 = (f32[4,16,128]{2,1,0:T(8,128)S(1)}, f32[4,16,128]{2,1,0:T(8,128)S(1)}, u32[]{:S(2)}, u32[]{:S(2)}) collective-permute-start(f32[4,16,128]{2,1,0:T(8,128)S(1)} %get-tuple-element.14.refs_4_), channel_id=1, source_target_pairs={{0,3},{1,2},{2,1},{3,0},{4,7},{5,6},{6,5},{7,4},{8,11},{9,10},{10,... | collective-permute-start | bytes 98312 | tf_op jit(solution)/shard_map/ppermute | solution.py:359
  23.9 4.8 %collective-permute-start.5 = (f32[4,16,128]{2,1,0:T(8,128)S(1)}, f32[4,16,128]{2,1,0:T(8,128)S(1)}, u32[]{:S(2)}, u32[]{:S(2)}) collective-permute-start(f32[4,16,128]{2,1,0:T(8,128)S(1)} %get-tuple-element.14.refs_4_), channel_id=1, source_target_pairs={{0,2},{1,3},{2,0},{3,1},{4,6},{5,7},{6,4},{7,5},{8,10},{9,11},{10,... | collective-permute-start | bytes 98312 | tf_op jit(solution)/shard_map/ppermute | solution.py:359
  26.1 4.1 %collective-permute-start.4 = (f32[4,16,128]{2,1,0:T(8,128)S(1)}, f32[4,16,128]{2,1,0:T(8,128)S(1)}, u32[]{:S(2)}, u32[]{:S(2)}) collective-permute-start(f32[4,16,128]{2,1,0:T(8,128)S(1)} %get-tuple-element.14.refs_4_), channel_id=1, source_target_pairs={{0,1},{1,0},{2,3},{3,2},{4,5},{5,4},{6,7},{7,6},{8,9},{9,8},{10,11... | collective-permute-start | bytes 98312 | tf_op jit(solution)/shard_map/ppermute | solution.py:359

commit v3 on v2

--- a/solution.py
+++ b/solution.py
@@ -17,6 +17,8 @@
 
 HIGHEST = lax.Precision.HIGHEST
 STRIP = 512
+COSTS = (10**10, 10**10)
+MERGE = (1,)
 CHUNK = 6
 PACK = 40
 VMEM_LIMIT = 16 * 1024 * 1024
@@ -35,8 +37,8 @@
 
 
 def forecast_kernel(*refs):
-    inputs, (flow_hbm, wet_state, dry_state, pack) = refs[:10], refs[10:14]
-    held, (flow, share, melt_cap, last_flow, held_sems, in_sems, out_sems) = refs[14:24], refs[24:]
+    inputs, (flow_hbm, wet, dry_state, pred, fixed) = refs[:10], refs[10:15]
+    held, (flow, share, melt_cap, last_flow, held_sems, in_sems, out_sems) = refs[15:25], refs[25:]
     levels, settings, rain, heat, evap, measured, sigma, draws, position, present = held
     rain_hbm = inputs[2]
     hours, members, width = rain.shape
@@ -118,8 +120,10 @@
             state = lax.fori_loop(c * CHUNK, (c + 1) * CHUNK, hour, state, unroll=2)
             flow_copy(n).start()
         snow, moist, upper, lower = state
-        wet_state[0, :, where] = moist
-        wet_state[1, :, where] = upper
+        for t in range(strip // LOCAL):
+            tile = s * (strip // LOCAL) + t
+            wet[tile] = moist[:, t * LOCAL : (t + 1) * LOCAL]
+            wet[width // LOCAL + tile] = upper[:, t * LOCAL : (t + 1) * LOCAL]
         dry_state[0, :, where] = snow
         dry_state[1, :, where] = lower
         last_flow[:, where] = 0.45 * moist * inv_cap
@@ -144,11 +148,11 @@
         predicted = jnp.where(lane // OBS == b, chosen, predicted)
     sd = lanes_of(sigma[...])
     spread = jnp.concatenate([draws[b] for b in range(blocks)], axis=1)
-    pack[0:members] = predicted
-    pack[members : 2 * members] = lanes_of(measured[...]) + sd * spread
-    tail = pack.shape[0] - 2 * members
-    pack[2 * members :] = jnp.broadcast_to(
-        lanes_of(present[...].astype(jnp.float32)) / sd, (tail, LOCAL)
+    pred[...] = predicted
+    wet[wet.shape[0] - 1] = predicted
+    fixed[0:members] = lanes_of(measured[...]) + sd * spread
+    fixed[members:] = jnp.broadcast_to(
+        lanes_of(present[...].astype(jnp.float32)) / sd, (fixed.shape[0] - members, LOCAL)
     )
     for n in range(len(pieces)):
         flow_copy(n).wait()
@@ -164,12 +168,13 @@
         forecast_kernel,
         out_shape=(
             jax.ShapeDtypeStruct((hours, members, width), f32),
+            jax.ShapeDtypeStruct((2 * width // LOCAL + 1, members, LOCAL), f32),
             jax.ShapeDtypeStruct((2, members, width), f32),
-            jax.ShapeDtypeStruct((2, members, width), f32),
-            jax.ShapeDtypeStruct((2 * members + 8, LOCAL), f32),
+            jax.ShapeDtypeStruct((members, LOCAL), f32),
+            jax.ShapeDtypeStruct((members + 8, LOCAL), f32),
         ),
         in_specs=[hbm] * len(arrays),
-        out_specs=(hbm, vmem, vmem, vmem),
+        out_specs=(hbm, vmem, vmem, vmem, vmem),
         scratch_shapes=[pltpu.VMEM(x.shape, x.dtype) for x in arrays]
         + [
             pltpu.VMEM((hours, members, width), f32),
@@ -183,53 +188,6 @@
         compiler_params=pltpu.CompilerParams(vmem_limit_bytes=VMEM_LIMIT),
         name="forecast",
     )(*(pltpu.with_memory_space_constraint(x, pltpu.HBM) for x in arrays))
-
-
-def localize_kernel(relative, count, index, adjacency, *refs):
-    pieces, (pred_out, innov_out, weight_out, table) = refs[:count], refs[count:]
-    at = 0
-    for piece in pieces:
-        n = piece.shape[0]
-        table[at : at + n] = piece[...]
-        at += n
-    me = index[0]
-    blocks, members, _ = pred_out.shape
-    rows = table.shape[1]
-    lane = lax.broadcasted_iota(jnp.int32, (rows, LOCAL), 1) // OBS
-    for b in range(blocks):
-        local = jnp.zeros((rows, LOCAL), jnp.float32)
-        for i in range(NBR + 1):
-            source = me * blocks + b if i == 0 else adjacency[i - 1, me * blocks + b]
-            owner = source // blocks
-            if relative:
-                owner = owner ^ me
-            shift = ((i + blocks - source % blocks) % blocks) * OBS
-            local = jnp.where(lane == i, pltpu.roll(table[owner], shift, 1), local)
-        weight = local[2 * members : 2 * members + 1]
-        pred_out[b] = local[:members]
-        innov_out[b] = weight * (local[members : 2 * members] - local[:members])
-        weight_out[b] = weight
-
-
-def localize(pieces, relative, index, adjacency, blocks, members):
-    f32 = jnp.float32
-    rows = 2 * members + 8
-    total = sum(p.shape[0] for p in pieces)
-    vmem = pl.BlockSpec(memory_space=pltpu.VMEM)
-    smem = pl.BlockSpec(memory_space=pltpu.SMEM)
-    return pl.pallas_call(
-        functools.partial(localize_kernel, relative, len(pieces)),
-        out_shape=(
-            jax.ShapeDtypeStruct((blocks, members, LOCAL), f32),
-            jax.ShapeDtypeStruct((blocks, members, LOCAL), f32),
-            jax.ShapeDtypeStruct((blocks, 1, LOCAL), f32),
-        ),
-        in_specs=[smem, smem] + [vmem] * len(pieces),
-        out_specs=(vmem, vmem, vmem),
-        scratch_shapes=[pltpu.VMEM((total, rows, LOCAL), f32)],
-        compiler_params=pltpu.CompilerParams(vmem_limit_bytes=VMEM_LIMIT),
-        name="localize",
-    )(index, adjacency, *pieces)
 
 
 def spread_lane(x, k):
@@ -283,25 +241,43 @@
     return [jnp.concatenate([top, low], axis=0) for top, low in zip(tops, lows)]
 
 
-def update_kernel(count, others, *refs):
-    innov, weight, wet_own, dry = refs[:4]
-    preds, wets = refs[4 : 4 + count], refs[4 + count : 4 + count + others]
-    analysis_hbm, analysis, out_sems = refs[4 + count + others :]
-    blocks, members, _ = innov.shape
-
-    def out_copy(b):
-        where = (slice(None), slice(None), pl.ds(b * NB, NB))
-        return pltpu.make_async_copy(analysis.at[where], analysis_hbm.at[where], out_sems.at[b])
-
+def gain_kernel(total, count, relative, index, adjacency, *refs):
+    pieces, (gain_out, table) = refs[:count], refs[count:]
+    at = 0
+    for piece in pieces:
+        table[at : at + piece.shape[0]] = piece[...]
+        at += piece.shape[0]
+    me = index[0]
+    blocks, members, _ = gain_out.shape
+    rows = table.shape[1]
+    lane = lax.broadcasted_iota(jnp.int32, (rows, LOCAL), 1) // OBS
     systems = []
     for b in range(blocks):
-        pred = jnp.concatenate(
-            [p[b] if len(p.shape) == 3 else p[:, b].reshape(-1, LOCAL) for p in preds], axis=0
-        )
-        total = pred.shape[0]
-        scaled = (pred - jnp.mean(pred, axis=0, keepdims=True)) * weight[b]
+        local = jnp.zeros((rows, LOCAL), jnp.float32)
+        for i in range(NBR + 1):
+            source = me * blocks + b if i == 0 else adjacency[i - 1, me * blocks + b]
+            owner = source // blocks
+            if relative:
+                owner = owner ^ me
+                far = (owner // 4 + owner // 2 + owner) % 2
+                near = table[far * (at // 2) + owner // 2]
+                far = table[(1 - far) * (at // 2) + owner // 2]
+                parts = [
+                    (near if k in (0,) + MERGE else far)[k * members : (k + 1) * members]
+                    for k in range(total // members)
+                ]
+                found = jnp.concatenate(parts + [near[total:]], axis=0)
+            else:
+                found = table[owner]
+            shift = ((i + blocks - source % blocks) % blocks) * OBS
+            local = jnp.where(lane == i, pltpu.roll(found, shift, 1), local)
+        pred, drawn = local[:total], local[total : total + members]
+        own = local[:members] if relative else local[total + members : total + 2 * members]
+        weight = local[rows - 8 : rows - 7]
+        scaled = (pred - jnp.mean(pred, axis=0, keepdims=True)) * weight
+        innov = (drawn - own) * weight
         both = jnp.concatenate(
-            [scaled, innov[b], jnp.zeros((LOCAL - total - members, LOCAL), jnp.float32)], axis=0
+            [scaled, innov, jnp.zeros((LOCAL - total - members, LOCAL), jnp.float32)], axis=0
         )
         matrix = lax.dot_general(
             scaled,
@@ -310,68 +286,108 @@
             precision=HIGHEST,
             preferred_element_type=jnp.float32,
         )
-        rows = lax.broadcasted_iota(jnp.int32, (total, LOCAL), 0)
-        cols = lax.broadcasted_iota(jnp.int32, (total, LOCAL), 1)
-        systems.append(matrix + jnp.where(rows == cols, float(total - 1), 0.0))
+        row = lax.broadcasted_iota(jnp.int32, (total, LOCAL), 0)
+        col = lax.broadcasted_iota(jnp.int32, (total, LOCAL), 1)
+        systems.append(matrix + jnp.where(row == col, float(total - 1), 0.0))
     solved = solve(systems)
-    analysis[:, 0, :] = dry[0]
-    analysis[:, 3, :] = dry[1]
+    for b in range(blocks):
+        gain = solved[b] - jnp.mean(solved[b], axis=0, keepdims=True)
+        gain_out[b] = jnp.transpose(gain)[total : total + members]
+
+
+def find_gain(pieces, relative, index, adjacency, blocks, members, total):
+    vmem = pl.BlockSpec(memory_space=pltpu.VMEM)
+    smem = pl.BlockSpec(memory_space=pltpu.SMEM)
+    owners = sum(p.shape[0] for p in pieces)
+    return pl.pallas_call(
+        functools.partial(gain_kernel, total, len(pieces), relative),
+        out_shape=jax.ShapeDtypeStruct((blocks, members, total), jnp.float32),
+        in_specs=[smem, smem] + [vmem] * len(pieces),
+        out_specs=vmem,
+        scratch_shapes=[pltpu.VMEM((owners,) + pieces[0].shape[1:], jnp.float32)],
+        compiler_params=pltpu.CompilerParams(vmem_limit_bytes=VMEM_LIMIT),
+        cost_estimate=pl.CostEstimate(flops=1, bytes_accessed=1, transcendentals=0),
+        name="gain",
+    )(index, adjacency, *pieces)
+
+
+def carry_kernel(x, y):
+    y[...] = x[...]
+
+
+def carry(x, cost):
+    vmem = pl.BlockSpec(memory_space=pltpu.VMEM)
+    return pl.pallas_call(
+        carry_kernel,
+        out_shape=jax.ShapeDtypeStruct(x.shape, x.dtype),
+        in_specs=[vmem],
+        out_specs=vmem,
+        compiler_params=pltpu.CompilerParams(vmem_limit_bytes=VMEM_LIMIT),
+        cost_estimate=pl.CostEstimate(flops=cost, bytes_accessed=0, transcendentals=0),
+        name="carry",
+    )(x)
+
+
+def update_kernel(gain, wet_own, dry, *refs):
+    wets, (analysis_hbm, analysis, out_sems) = refs[:-3], refs[-3:]
+    blocks = gain.shape[0]
+
+    def out_copy(b):
+        where = (slice(None), slice(None), pl.ds(b * NB, NB))
+        return pltpu.make_async_copy(analysis.at[where], analysis_hbm.at[where], out_sems.at[b])
+
+    tiles = dry.shape[2] // LOCAL
     for b in range(blocks):
         where = pl.ds(b * NB, NB)
-        gain = solved[b]
-        gain = gain - jnp.mean(gain, axis=0, keepdims=True)
-        turned = jnp.transpose(gain)[total : total + members]
-        for k, slot in ((0, 1), (1, 2)):
-            if len(wets[0].shape) == 3:
-                states = [wet_own[k, :, where]] + [w[k, :, where] for w in wets]
-            else:
-                states = [w[:, k, :, where].reshape(-1, NB) for w in wets]
-            analysis[:, slot, where] = wet_own[k, :, where] + jnp.dot(
-                turned,
-                jnp.concatenate(states, axis=0),
-                precision=HIGHEST,
-                preferred_element_type=jnp.float32,
-            )
+        analysis[:, 0, where] = dry[0, :, where]
+        analysis[:, 3, where] = dry[1, :, where]
+        for k in range(2):
+            for t in range(b * NB // LOCAL, (b + 1) * NB // LOCAL):
+                at = k * tiles + t
+                if len(wets[0].shape) == 3:
+                    states = [wet_own[at]] + [w[at] for w in wets]
+                else:
+                    states = [w[:, at].reshape(-1, LOCAL) for w in wets]
+                analysis[:, 1 + k, pl.ds(t * LOCAL, LOCAL)] = wet_own[at] + jnp.dot(
+                    gain[b],
+                    jnp.concatenate(states, axis=0),
+                    precision=HIGHEST,
+                    preferred_element_type=jnp.float32,
+                )
         out_copy(b).start()
     for b in range(blocks):
         out_copy(b).wait()
 
 
-def update(innov, weight, wet, dry, preds, wets):
-    _, members, width = wet.shape
+def update(gain, wet, dry, wets):
+    _, members, width = dry.shape
     vmem = pl.BlockSpec(memory_space=pltpu.VMEM)
-    hbm = pl.BlockSpec(memory_space=pltpu.HBM)
     return pl.pallas_call(
-        functools.partial(update_kernel, len(preds), len(wets)),
+        update_kernel,
         out_shape=jax.ShapeDtypeStruct((members, 4, width), jnp.float32),
-        in_specs=[vmem] * (4 + len(preds) + len(wets)),
-        out_specs=hbm,
+        in_specs=[vmem] * (3 + len(wets)),
+        out_specs=pl.BlockSpec(memory_space=pltpu.HBM),
         scratch_shapes=[
             pltpu.VMEM((members, 4, width), jnp.float32),
             pltpu.SemaphoreType.DMA((width // NB,)),
         ],
         compiler_params=pltpu.CompilerParams(vmem_limit_bytes=VMEM_LIMIT),
         name="update",
-    )(innov, weight, wet, dry, *preds, *wets)
+    )(gain, wet, dry, *wets)
 
 
 def permute(x, axis, mask):
     return lax.ppermute(x, axis, [(i, i ^ mask) for i in range(lax.axis_size(axis))])
 
 
-def over_members(x):
-    size = lax.axis_size("member")
-    if size > 4:
-        return [lax.all_gather(x, "member", axis=0)]
-    return [permute(x, "member", mask) for mask in range(1, size)]
-
-
-def over_basins(pack):
-    size = lax.axis_size("basin")
-    if size > 8:
-        return [lax.all_gather(pack, "basin", axis=0)], False
-    pair = jnp.stack([pack, permute(pack, "basin", 1)])
-    return [pair] + [permute(pair, "basin", mask) for mask in range(2, size, 2)], True
+def across(x, flip_member):
+    basins, members = lax.axis_size("basin"), lax.axis_size("member")
+    pairs = [
+        (b * members + m, (b ^ 1) * members + (m ^ flip_member))
+        for b in range(basins)
+        for m in range(members)
+    ]
+    return lax.ppermute(x, ("basin", "member"), pairs)
 
 
 def on_device(
@@ -389,7 +405,8 @@
 ):
     members = rainfall_member_series.shape[1]
     blocks = gauge_measured_values.shape[0]
-    discharge, wet, dry, pack = forecast(
+    basin_size, member_size = lax.axis_size("basin"), lax.axis_size("member")
+    discharge, wet, dry, pred, fixed = forecast(
         initial_reservoir_levels,
         normalized_catchment_settings,
         rainfall_member_series,
@@ -402,15 +419,30 @@
         gauge_present_flag,
     )
     index = jnp.full((1,), lax.axis_index("basin"), jnp.int32)
-    packs, relative = over_basins(pack)
-    pred, innov, weight = localize(
-        packs, relative, index, jnp.transpose(adjacent_block_list), blocks, members
+    adjacency = jnp.transpose(adjacent_block_list)
+    relative = basin_size <= 8 and member_size <= 4
+    if relative:
+        others = list(range(1, member_size))
+        first = {k: permute(wet, "member", k) if k in MERGE else across(pred, k) for k in others}
+        wets = [first[k] if k in MERGE else permute(wet, "member", k) for k in others]
+        preds = [pred] + [first[k][-1] if k in MERGE else first[k] for k in others]
+        near = jnp.concatenate(preds + [fixed], axis=0)[None]
+        flip = 2
+        while flip < basin_size:
+            near = jnp.concatenate([near, permute(near, "basin", flip + 1)], axis=0)
+            flip *= 2
+        packs = [near, permute(near, "basin", 1)]
+        for cost in COSTS:
+            dry = carry(dry, cost)
+    else:
+        preds = lax.all_gather(pred, "member", axis=0).reshape(-1, LOCAL)
+        wets = [lax.all_gather(wet, "member", axis=0)]
+        mine = jnp.concatenate([preds, fixed[:members], pred, fixed[members:]], axis=0)
+        packs = [lax.all_gather(mine, "basin", axis=0)]
+    gain = find_gain(
+        packs, relative, index, adjacency, blocks, members, members * member_size
     )
-    preds = over_members(pred)
-    wets = over_members(wet)
-    if len(preds) > 1:
-        preds = [pred] + preds
-    analysis = update(innov, weight, wet, dry, preds, wets)
+    analysis = update(gain, wet, dry, wets)
     return (analysis, discharge)
 
 

time: 34.5 us -> 30.5 us (0.88)
  starting transfers between devices: 15.4 us -> 11.4 us
    ppermute x10 -> x6, starting transfers between devices: 15.4 us -> 9.19 us  [permute(): lax.ppermute(x, axis, [(i, i ^ mask) for i in range(lax.axis_size(axis))])]
    ppermute x10 -> x6, waiting for transfers between devices: 8.64 us -> 5.4 us  [permute(): lax.ppermute(x, axis, [(i, i ^ mask) for i in range(lax.axis_size(axis))])]
    ppermute x0 -> x2, waiting for transfers between devices: none -> 2.95 us  [across(): return lax.ppermute(x, ('basin', 'member'), pairs)]
    ppermute x0 -> x2, starting transfers between devices: none -> 2.16 us  [across(): return lax.ppermute(x, ('basin', 'member'), pairs)]
    pallas_call x2 -> x4, Pallas kernels: 4.93 us -> 5.23 us  [the longest x1 3.98 us: find_gain(): pl.pallas_call(functools.partial(gain_kernel, total, len(pieces), relativ...]
  transfers between devices with their start and end apart: 10 -> 8, of which waited for: 6 -> 6; matrix products, arithmetic and copies ran while one was open for 0% -> 0% of each run, Pallas kernels for 2% -> 13%
where the time goes in v3:
time: 30.5 us; the launch traced here: 30.4 us
  starting transfers between devices  11.4 us (37%)
  Pallas kernels  9.95 us (33%)
  waiting for transfers between devices  8.35 us (27%)
  between operations  0.69 us (2%)
    ppermute x6, starting transfers between devices, permute(): lax.ppermute(x, axis, [(i, i ^ mask) for i in range(lax.axis_size(axis))])  9.19 us
    ppermute x6, waiting for transfers between devices, permute(): lax.ppermute(x, axis, [(i, i ^ mask) for i in range(lax.axis_size(axis))])  5.4 us
    pallas_call x1, Pallas kernels, forecast(): pl.pallas_call(forecast_kernel, out_shape=(jax.ShapeDtypeStruct((hours, m...  4.72 us
    pallas_call x1, Pallas kernels, find_gain(): pl.pallas_call(functools.partial(gain_kernel, total, len(pieces), relativ...  3.98 us
    ppermute x2, waiting for transfers between devices, across(): return lax.ppermute(x, ('basin', 'member'), pairs)  2.95 us
    ppermute x2, starting transfers between devices, across(): return lax.ppermute(x, ('basin', 'member'), pairs)  2.16 us
    pallas_call x1, Pallas kernels, update(): pl.pallas_call(update_kernel, out_shape=jax.ShapeDtypeStruct((members, 4,...  1.24 us
  transfers between devices with their start and end apart: 8, of which 6 were waited for; matrix products, arithmetic and copies ran while one was open for 0% of the time, Pallas kernels for 13%

profile of v3, /device:TPU:0, one launch (start us, length us, event | category | flops | bytes accessed | tf_op | source)
XLA Modules:
  0.0 30.4 jit_solution(11679827738628132638)
XLA Ops:
  0.6 4.7 %forecast.1 = (f32[24,16,1024]{2,1,0:T(8,128)}, f32[17,16,128]{2,1,0:T(8,128)S(1)}, f32[2,16,1024]{2,1,0:T(8,128)S(1)}, f32[16,128]{1,0:T(8,128)S(1)}, f32[24,128]{1,0:T(8,128)S(1)}) custom-call(f32[16,4,1024]{2,1,0:T(4,128)} %refs_0_.1, f32[10,1024]{1,0:T(8,128)} %refs_1_.1, f32[24,16,1024]{2,1,0:T(8,128)} %refs_2_.1, f32[24,1024]{1,0:T(8,128)} %refs_3_.1, ...), custom_call_target="tpu_custom_call" | custom-call | tf_op jit(solution)/shard_map/forecast/pallas_call | solution.py:167
  5.4 3.1 %collective-permute-start = (f32[17,16,128]{2,1,0:T(8,128)S(1)}, f32[17,16,128]{2,1,0:T(8,128)S(1)}, u32[]{:S(2)}, u32[]{:S(2)}) collective-permute-start(f32[17,16,128]{2,1,0:T(8,128)S(1)} %get-tuple-element.8.wet_own), channel_id=1, source_target_pairs={{0,1},{1,0},{2,3},{3,2},{4,5},{5,4},{6,7},{7,6},{8,9},{9,8},{10,11... | collective-permute-start | bytes 417800 | tf_op jit(solution)/shard_map/ppermute | solution.py:380
  8.4 1.7 %collective-permute-start.1 = (f32[16,128]{1,0:T(8,128)S(1)}, f32[16,128]{1,0:T(8,128)S(1)}, u32[]{:S(2)}, u32[]{:S(2)}) collective-permute-start(f32[16,128]{1,0:T(8,128)S(1)} %get-tuple-element.7), channel_id=1, source_target_pairs={{0,6},{1,7},{2,4},{3,5},{4,2},{5,3},{6,0},{7,1},{8,14},{9,15},{10,... | collective-permute-start | bytes 24584 | tf_op jit(solution)/shard_map/ppermute | solution.py:390
  10.2 0.4 %collective-permute-start.2 = (f32[16,128]{1,0:T(8,128)S(1)}, f32[16,128]{1,0:T(8,128)S(1)}, u32[]{:S(2)}, u32[]{:S(2)}) collective-permute-start(f32[16,128]{1,0:T(8,128)S(1)} %get-tuple-element.7), channel_id=1, source_target_pairs={{0,7},{1,6},{2,5},{3,4},{4,3},{5,2},{6,1},{7,0},{8,15},{9,14},{10,... | collective-permute-start | bytes 24584 | tf_op jit(solution)/shard_map/ppermute | solution.py:390
  10.6 1.5 %collective-permute-done.refs_0_ = f32[17,16,128]{2,1,0:T(8,128)S(1)} collective-permute-done((f32[17,16,128]{2,1,0:T(8,128)S(1)}, f32[17,16,128]{2,1,0:T(8,128)S(1)}, u32[]{:S(2)}, u32[]{:S(2)}) %collective-permute-start) | collective-permute-done | bytes 139296 | tf_op jit(solution)/shard_map/ppermute | solution.py:380
  12.1 0.3 collective-permute-done.1
  12.4 2.6 %collective-permute-done.2 = f32[16,128]{1,0:T(8,128)S(1)} collective-permute-done((f32[16,128]{1,0:T(8,128)S(1)}, f32[16,128]{1,0:T(8,128)S(1)}, u32[]{:S(2)}, u32[]{:S(2)}) %collective-permute-start.2) | collective-permute-done | bytes 8224 | tf_op jit(solution)/shard_map/ppermute | solution.py:390
  15.1 2.1 %collective-permute-start.3 = (f32[1,88,128]{2,1,0:T(8,128)S(1)}, f32[1,88,128]{2,1,0:T(8,128)S(1)}, u32[]{:S(2)}, u32[]{:S(2)}) collective-permute-start(f32[1,88,128]{2,1,0:T(8,128)S(1)} %bitcast.9), channel_id=1, source_target_pairs={{0,12},{4,8},{8,4},{12,0},{16,28},{20,24},{24,20},{28,16},{1,13},{... | collective-permute-start | bytes 135176 | tf_op jit(solution)/shard_map/ppermute | solution.py:380
  17.1 0.0 collective-permute-start.6
  17.1 1.3 %collective-permute-start.7 = (f32[17,16,128]{2,1,0:T(8,128)S(1)}, f32[17,16,128]{2,1,0:T(8,128)S(1)}, u32[]{:S(2)}, u32[]{:S(2)}) collective-permute-start(f32[17,16,128]{2,1,0:T(8,128)S(1)} %get-tuple-element.8.wet_own), channel_id=1, source_target_pairs={{0,3},{1,2},{2,1},{3,0},{4,7},{5,6},{6,5},{7,4},{8,11},{9,10},{10,... | collective-permute-start | bytes 417800 | tf_op jit(solution)/shard_map/ppermute | solution.py:380
  18.4 0.4 %collective-permute-done.3 = f32[1,88,128]{2,1,0:T(8,128)S(1)} collective-permute-done((f32[1,88,128]{2,1,0:T(8,128)S(1)}, f32[1,88,128]{2,1,0:T(8,128)S(1)}, u32[]{:S(2)}, u32[]{:S(2)}) %collective-permute-start.3) | collective-permute-done | bytes 45088 | tf_op jit(solution)/shard_map/ppermute | solution.py:380
  18.9 1.8 %collective-permute-start.4 = (f32[2,88,128]{2,1,0:T(8,128)S(1)}, f32[2,88,128]{2,1,0:T(8,128)S(1)}, u32[]{:S(2)}, u32[]{:S(2)}) collective-permute-start(f32[2,88,128]{2,1,0:T(8,128)S(1)} %pad_maximum_fusion.1), channel_id=1, source_target_pairs={{0,20},{4,16},{8,28},{12,24},{16,4},{20,0},{24,12},{28,8},{1,21},{... | collective-permute-start | bytes 270344 | tf_op jit(solution)/shard_map/ppermute | solution.py:380
  20.7 2.4 %collective-permute-done.4 = f32[2,88,128]{2,1,0:T(8,128)S(1)} collective-permute-done((f32[2,88,128]{2,1,0:T(8,128)S(1)}, f32[2,88,128]{2,1,0:T(8,128)S(1)}, u32[]{:S(2)}, u32[]{:S(2)}) %collective-permute-start.4) | collective-permute-done | bytes 90144 | tf_op jit(solution)/shard_map/ppermute | solution.py:380
  23.1 0.0 copy-start
  23.1 0.9 %collective-permute-start.5 = (f32[4,88,128]{2,1,0:T(8,128)S(1)}, f32[4,88,128]{2,1,0:T(8,128)S(1)}, u32[]{:S(2)}, u32[]{:S(2)}) collective-permute-start(f32[4,88,128]{2,1,0:T(8,128)S(1)} %pad_maximum_fusion.refs_0_), channel_id=1, source_target_pairs={{0,4},{4,0},{8,12},{12,8},{16,20},{20,16},{24,28},{28,24},{1,5},{5... | collective-permute-start | bytes 540680 | tf_op jit(solution)/shard_map/ppermute | solution.py:380
  24.1 1.0 %collective-permute-done.5.refs_1_ = f32[4,88,128]{2,1,0:T(8,128)S(1)} collective-permute-done((f32[4,88,128]{2,1,0:T(8,128)S(1)}, f32[4,88,128]{2,1,0:T(8,128)S(1)}, u32[]{:S(2)}, u32[]{:S(2)}) %collective-permute-start.5) | collective-permute-done | bytes 180256 | tf_op jit(solution)/shard_map/ppermute | solution.py:380
  25.1 0.0 copy-done
  25.1 4.0 %gain.1 = f32[4,16,64]{2,1,0:T(8,128)S(1)} custom-call(s32[1]{0:T(128)} %bitcast.index, s32[3,32]{1,0:T(4,128)S(1)} %bitcast.8, f32[4,88,128]{2,1,0:T(8,128)S(1)} %pad_maximum_fusion.refs_0_, f32[4,88,128]{2,1,0:T(8,128)S(1)} %collective-permute-done.5.refs_1_), custom_call_target="tpu_custom_call" | custom-call | flops 1 | bytes 1 | tf_op jit(solution)/shard_map/gain/pallas_call | solution.py:302
  29.1 0.0 collective-permute-done.6.refs_1_
  29.1 0.0 collective-permute-done.7.refs_2_
  29.1 1.2 %update.1 = f32[16,4,1024]{2,1,0:T(4,128)} custom-call(f32[4,16,64]{2,1,0:T(8,128)S(1)} %gain.1, f32[17,16,128]{2,1,0:T(8,128)S(1)} %get-tuple-element.8.wet_own, f32[2,16,1024]{2,1,0:T(8,128)S(1)} %carry.3.dry, f32[17,16,128]{2,1,0:T(8,128)S(1)} %collective-permute-done.refs_0_, f32[17,16,128]{2,1,0:T(8,128)S(1)} %collective-permute-done.6.refs_1_, ...), custom_call_target="tpu_custom_call" | custom-call | tf_op jit(solution)/shard_map/update/pallas_call | solution.py:365
  (9 shorter events, 0.1 us)
Async XLA Ops:
  5.4 6.8 %collective-permute-start = (f32[17,16,128]{2,1,0:T(8,128)S(1)}, f32[17,16,128]{2,1,0:T(8,128)S(1)}, u32[]{:S(2)}, u32[]{:S(2)}) collective-permute-start(f32[17,16,128]{2,1,0:T(8,128)S(1)} %get-tuple-element.8.wet_own), channel_id=1, source_target_pairs={{0,1},{1,0},{2,3},{3,2},{4,5},{5,4},{6,7},{7,6},{8,9},{9,8},{10,11... | collective-permute-start | bytes 417800 | tf_op jit(solution)/shard_map/ppermute | solution.py:380
  8.4 4.0 %collective-permute-start.1 = (f32[16,128]{1,0:T(8,128)S(1)}, f32[16,128]{1,0:T(8,128)S(1)}, u32[]{:S(2)}, u32[]{:S(2)}) collective-permute-start(f32[16,128]{1,0:T(8,128)S(1)} %get-tuple-element.7), channel_id=1, source_target_pairs={{0,6},{1,7},{2,4},{3,5},{4,2},{5,3},{6,0},{7,1},{8,14},{9,15},{10,... | collective-permute-start | bytes 24584 | tf_op jit(solution)/shard_map/ppermute | solution.py:390
  10.2 4.9 %collective-permute-start.2 = (f32[16,128]{1,0:T(8,128)S(1)}, f32[16,128]{1,0:T(8,128)S(1)}, u32[]{:S(2)}, u32[]{:S(2)}) collective-permute-start(f32[16,128]{1,0:T(8,128)S(1)} %get-tuple-element.7), channel_id=1, source_target_pairs={{0,7},{1,6},{2,5},{3,4},{4,3},{5,2},{6,1},{7,0},{8,15},{9,14},{10,... | collective-permute-start | bytes 24584 | tf_op jit(solution)/shard_map/ppermute | solution.py:390
  15.1 3.8 %collective-permute-start.3 = (f32[1,88,128]{2,1,0:T(8,128)S(1)}, f32[1,88,128]{2,1,0:T(8,128)S(1)}, u32[]{:S(2)}, u32[]{:S(2)}) collective-permute-start(f32[1,88,128]{2,1,0:T(8,128)S(1)} %bitcast.9), channel_id=1, source_target_pairs={{0,12},{4,8},{8,4},{12,0},{16,28},{20,24},{24,20},{28,16},{1,13},{... | collective-permute-start | bytes 135176 | tf_op jit(solution)/shard_map/ppermute | solution.py:380
  17.1 12.0 %collective-permute-start.6 = (f32[17,16,128]{2,1,0:T(8,128)S(1)}, f32[17,16,128]{2,1,0:T(8,128)S(1)}, u32[]{:S(2)}, u32[]{:S(2)}) collective-permute-start(f32[17,16,128]{2,1,0:T(8,128)S(1)} %get-tuple-element.8.wet_own), channel_id=1, source_target_pairs={{0,2},{1,3},{2,0},{3,1},{4,6},{5,7},{6,4},{7,5},{8,10},{9,11},{10,... | collective-permute-start | bytes 417800 | tf_op jit(solution)/shard_map/ppermute | solution.py:380
  17.1 12.0 %collective-permute-start.7 = (f32[17,16,128]{2,1,0:T(8,128)S(1)}, f32[17,16,128]{2,1,0:T(8,128)S(1)}, u32[]{:S(2)}, u32[]{:S(2)}) collective-permute-start(f32[17,16,128]{2,1,0:T(8,128)S(1)} %get-tuple-element.8.wet_own), channel_id=1, source_target_pairs={{0,3},{1,2},{2,1},{3,0},{4,7},{5,6},{6,5},{7,4},{8,11},{9,10},{10,... | collective-permute-start | bytes 417800 | tf_op jit(solution)/shard_map/ppermute | solution.py:380
  18.9 4.2 %collective-permute-start.4 = (f32[2,88,128]{2,1,0:T(8,128)S(1)}, f32[2,88,128]{2,1,0:T(8,128)S(1)}, u32[]{:S(2)}, u32[]{:S(2)}) collective-permute-start(f32[2,88,128]{2,1,0:T(8,128)S(1)} %pad_maximum_fusion.1), channel_id=1, source_target_pairs={{0,20},{4,16},{8,28},{12,24},{16,4},{20,0},{24,12},{28,8},{1,21},{... | collective-permute-start | bytes 270344 | tf_op jit(solution)/shard_map/ppermute | solution.py:380
  23.1 2.0 %copy-start = (s32[32,3]{0,1:T(4,128)S(1)}, s32[32,3]{0,1:T(4,128)}, u32[]{:S(2)}) copy-start(s32[32,3]{0,1:T(4,128)} %param.21) | copy-start | bytes 1156
  23.1 2.0 %collective-permute-start.5 = (f32[4,88,128]{2,1,0:T(8,128)S(1)}, f32[4,88,128]{2,1,0:T(8,128)S(1)}, u32[]{:S(2)}, u32[]{:S(2)}) collective-permute-start(f32[4,88,128]{2,1,0:T(8,128)S(1)} %pad_maximum_fusion.refs_0_), channel_id=1, source_target_pairs={{0,4},{4,0},{8,12},{12,8},{16,20},{20,16},{24,28},{28,24},{1,5},{5... | collective-permute-start | bytes 540680 | tf_op jit(solution)/shard_map/ppermute | solution.py:380

commit v4 on v3

--- a/solution.py
+++ b/solution.py
@@ -37,8 +37,8 @@
 
 
 def forecast_kernel(*refs):
-    inputs, (flow_hbm, wet, dry_state, pred, fixed) = refs[:10], refs[10:15]
-    held, (flow, share, melt_cap, last_flow, held_sems, in_sems, out_sems) = refs[15:25], refs[25:]
+    inputs, (flow, wet, dry_state, pred, fixed) = refs[:10], refs[10:15]
+    held, (share, melt_cap, last_flow, held_sems, in_sems) = refs[15:25], refs[25:]
     levels, settings, rain, heat, evap, measured, sigma, draws, position, present = held
     rain_hbm = inputs[2]
     hours, members, width = rain.shape
@@ -54,10 +54,6 @@
     def rain_copy(n):
         where = part(*pieces[n])
         return pltpu.make_async_copy(rain_hbm.at[where], rain.at[where], in_sems.at[n])
-
-    def flow_copy(n):
-        where = part(*pieces[n])
-        return pltpu.make_async_copy(flow.at[where], flow_hbm.at[where], out_sems.at[n])
 
     for k in (1, 3, 4, 0):
         whole_copy(k).start()
@@ -117,8 +113,7 @@
         for c in range(hours // CHUNK):
             n = s * (hours // CHUNK) + c
             rain_copy(n).wait()
-            state = lax.fori_loop(c * CHUNK, (c + 1) * CHUNK, hour, state, unroll=2)
-            flow_copy(n).start()
+            state = lax.fori_loop(c * CHUNK, (c + 1) * CHUNK, hour, state, unroll=CHUNK)
         snow, moist, upper, lower = state
         for t in range(strip // LOCAL):
             tile = s * (strip // LOCAL) + t
@@ -154,8 +149,6 @@
     fixed[members:] = jnp.broadcast_to(
         lanes_of(present[...].astype(jnp.float32)) / sd, (fixed.shape[0] - members, LOCAL)
     )
-    for n in range(len(pieces)):
-        flow_copy(n).wait()
 
 
 def forecast(*arrays):
@@ -167,22 +160,20 @@
     return pl.pallas_call(
         forecast_kernel,
         out_shape=(
-            jax.ShapeDtypeStruct((hours, members, width), f32),
+            pltpu.VMEM((hours, members, width), f32),
             jax.ShapeDtypeStruct((2 * width // LOCAL + 1, members, LOCAL), f32),
             jax.ShapeDtypeStruct((2, members, width), f32),
             jax.ShapeDtypeStruct((members, LOCAL), f32),
             jax.ShapeDtypeStruct((members + 8, LOCAL), f32),
         ),
         in_specs=[hbm] * len(arrays),
-        out_specs=(hbm, vmem, vmem, vmem, vmem),
+        out_specs=(vmem, vmem, vmem, vmem, vmem),
         scratch_shapes=[pltpu.VMEM(x.shape, x.dtype) for x in arrays]
         + [
-            pltpu.VMEM((hours, members, width), f32),
             pltpu.VMEM((hours, width), f32),
             pltpu.VMEM((hours, width), f32),
             pltpu.VMEM((members, width), f32),
             pltpu.SemaphoreType.DMA((len(arrays),)),
-            pltpu.SemaphoreType.DMA((copies,)),
             pltpu.SemaphoreType.DMA((copies,)),
         ],
         compiler_params=pltpu.CompilerParams(vmem_limit_bytes=VMEM_LIMIT),
@@ -427,10 +418,8 @@
         wets = [first[k] if k in MERGE else permute(wet, "member", k) for k in others]
         preds = [pred] + [first[k][-1] if k in MERGE else first[k] for k in others]
         near = jnp.concatenate(preds + [fixed], axis=0)[None]
-        flip = 2
-        while flip < basin_size:
-            near = jnp.concatenate([near, permute(near, "basin", flip + 1)], axis=0)
-            flip *= 2
+        flips = [k for k in range(2, basin_size) if k % 8 in (3, 5, 6)]
+        near = jnp.concatenate([near] + [permute(near, "basin", k) for k in flips], axis=0)
         packs = [near, permute(near, "basin", 1)]
         for cost in COSTS:
             dry = carry(dry, cost)

time: 30.5 us -> 27.4 us (0.90)
  waiting for transfers between devices: 8.35 us -> 4 us
  local copies, waits for them, and re-layouts: 0.01 us -> 1.16 us
  starting transfers between devices: 11.4 us -> 12.3 us
  Pallas kernels: 9.95 us -> 9.07 us
    ppermute x2, waiting for transfers between devices: 2.95 us -> 0.03 us  [across(): return lax.ppermute(x, ('basin', 'member'), pairs)]
    ppermute x6 -> x7, waiting for transfers between devices: 5.4 us -> 3.97 us  [permute(): lax.ppermute(x, axis, [(i, i ^ mask) for i in range(lax.axis_size(axis))])]
    ppermute x6 -> x7, starting transfers between devices: 9.19 us -> 10.5 us  [permute(): lax.ppermute(x, axis, [(i, i ^ mask) for i in range(lax.axis_size(axis))])]
    unnamed x6 -> x7, local copies, waits for them, and re-layouts: 0.01 us -> 1.16 us
    pallas_call x1, Pallas kernels: 4.72 us -> 3.83 us  [forecast(): pl.pallas_call(forecast_kernel, out_shape=(pltpu.VMEM((hours, members, wi...]
    ppermute x2, starting transfers between devices: 2.16 us -> 1.75 us  [across(): return lax.ppermute(x, ('basin', 'member'), pairs)]
  transfers between devices with their start and end apart: 8 -> 9, of which waited for: 6 -> 4; matrix products, arithmetic and copies ran while one was open for 0% -> 4% of each run, Pallas kernels for 13% -> 15%
where the time goes in v4:
time: 27.4 us; the launch traced here: 27.2 us
  starting transfers between devices  12.3 us (45%)
  Pallas kernels  9.07 us (33%)
  waiting for transfers between devices  4 us (15%)
  local copies, waits for them, and re-layouts  1.16 us (4%)
  between operations  0.7 us (3%)
    ppermute x7, starting transfers between devices, permute(): lax.ppermute(x, axis, [(i, i ^ mask) for i in range(lax.axis_size(axis))])  10.5 us
    pallas_call x1, Pallas kernels, find_gain(): pl.pallas_call(functools.partial(gain_kernel, total, len(pieces), relativ...  3.98 us
    ppermute x7, waiting for transfers between devices, permute(): lax.ppermute(x, axis, [(i, i ^ mask) for i in range(lax.axis_size(axis))])  3.97 us
    pallas_call x1, Pallas kernels, forecast(): pl.pallas_call(forecast_kernel, out_shape=(pltpu.VMEM((hours, members, wi...  3.83 us
    ppermute x2, starting transfers between devices, across(): return lax.ppermute(x, ('basin', 'member'), pairs)  1.75 us
    pallas_call x1, Pallas kernels, update(): pl.pallas_call(update_kernel, out_shape=jax.ShapeDtypeStruct((members, 4,...  1.24 us
    unnamed x7, local copies, waits for them, and re-layouts  1.16 us
  transfers between devices with their start and end apart: 9, of which 4 were waited for; matrix products, arithmetic and copies ran while one was open for 4% of the time, Pallas kernels for 15%

profile of v4, /device:TPU:0, one launch (start us, length us, event | category | flops | bytes accessed | tf_op | source)
XLA Modules:
  0.0 27.2 jit_solution(11620436052834258387)
XLA Ops:
  0.6 3.8 %forecast.1 = (f32[24,16,1024]{2,1,0:T(8,128)S(1)}, f32[17,16,128]{2,1,0:T(8,128)S(1)}, f32[2,16,1024]{2,1,0:T(8,128)S(1)}, f32[16,128]{1,0:T(8,128)S(1)}, f32[24,128]{1,0:T(8,128)S(1)}) custom-call(f32[16,4,1024]{2,1,0:T(4,128)} %refs_0_.1, f32[10,1024]{1,0:T(8,128)} %refs_1_.1, f32[24,16,1024]{2,1,0:T(8,128)} %refs_2_.1, f32[24,1024]{1,0:T(8,128)} %refs_3_.1, ...), custom_call_target="tpu_custom_call" | custom-call | tf_op jit(solution)/shard_map/forecast/pallas_call | solution.py:160
  4.5 3.1 %collective-permute-start = (f32[17,16,128]{2,1,0:T(8,128)S(1)}, f32[17,16,128]{2,1,0:T(8,128)S(1)}, u32[]{:S(2)}, u32[]{:S(2)}) collective-permute-start(f32[17,16,128]{2,1,0:T(8,128)S(1)} %get-tuple-element.8.wet_own), channel_id=1, source_target_pairs={{0,1},{1,0},{2,3},{3,2},{4,5},{5,4},{6,7},{7,6},{8,9},{9,8},{10,11... | collective-permute-start | bytes 417800 | tf_op jit(solution)/shard_map/ppermute | solution.py:371
  7.6 1.6 %collective-permute-start.2 = (f32[16,128]{1,0:T(8,128)S(1)}, f32[16,128]{1,0:T(8,128)S(1)}, u32[]{:S(2)}, u32[]{:S(2)}) collective-permute-start(f32[16,128]{1,0:T(8,128)S(1)} %get-tuple-element.7), channel_id=1, source_target_pairs={{0,7},{1,6},{2,5},{3,4},{4,3},{5,2},{6,1},{7,0},{8,15},{9,14},{10,... | collective-permute-start | bytes 24584 | tf_op jit(solution)/shard_map/ppermute | solution.py:381
  9.2 0.1 collective-permute-start.1
  9.3 3.5 %collective-permute-start.8 = (f32[17,16,128]{2,1,0:T(8,128)S(1)}, f32[17,16,128]{2,1,0:T(8,128)S(1)}, u32[]{:S(2)}, u32[]{:S(2)}) collective-permute-start(f32[17,16,128]{2,1,0:T(8,128)S(1)} %get-tuple-element.8.wet_own), channel_id=1, source_target_pairs={{0,3},{1,2},{2,1},{3,0},{4,7},{5,6},{6,5},{7,4},{8,11},{9,10},{10,... | collective-permute-start | bytes 417800 | tf_op jit(solution)/shard_map/ppermute | solution.py:371
  12.8 0.3 %collective-permute-start.7 = (f32[17,16,128]{2,1,0:T(8,128)S(1)}, f32[17,16,128]{2,1,0:T(8,128)S(1)}, u32[]{:S(2)}, u32[]{:S(2)}) collective-permute-start(f32[17,16,128]{2,1,0:T(8,128)S(1)} %get-tuple-element.8.wet_own), channel_id=1, source_target_pairs={{0,2},{1,3},{2,0},{3,1},{4,6},{5,7},{6,4},{7,5},{8,10},{9,11},{10,... | collective-permute-start | bytes 417800 | tf_op jit(solution)/shard_map/ppermute | solution.py:371
  13.1 0.0 collective-permute-done.refs_0_
  13.1 0.0 collective-permute-done.1
  13.2 0.0 collective-permute-done.2
  13.2 2.5 %collective-permute-start.5 = (f32[1,88,128]{2,1,0:T(8,128)S(1)}, f32[1,88,128]{2,1,0:T(8,128)S(1)}, u32[]{:S(2)}, u32[]{:S(2)}) collective-permute-start(f32[1,88,128]{2,1,0:T(8,128)S(1)} %bitcast.9), channel_id=1, source_target_pairs={{0,24},{4,28},{8,16},{12,20},{16,8},{20,12},{24,0},{28,4},{1,25},{... | collective-permute-start | bytes 135176 | tf_op jit(solution)/shard_map/ppermute | solution.py:371
  15.7 0.9 %collective-permute-start.4 = (f32[1,88,128]{2,1,0:T(8,128)S(1)}, f32[1,88,128]{2,1,0:T(8,128)S(1)}, u32[]{:S(2)}, u32[]{:S(2)}) collective-permute-start(f32[1,88,128]{2,1,0:T(8,128)S(1)} %bitcast.10), channel_id=1, source_target_pairs={{0,20},{4,16},{8,28},{12,24},{16,4},{20,0},{24,12},{28,8},{1,21},{... | collective-permute-start | bytes 135176 | tf_op jit(solution)/shard_map/ppermute | solution.py:371
  16.6 0.0 collective-permute-start.3
  16.6 2.0 %collective-permute-done.5 = f32[1,88,128]{2,1,0:T(8,128)S(1)} collective-permute-done((f32[1,88,128]{2,1,0:T(8,128)S(1)}, f32[1,88,128]{2,1,0:T(8,128)S(1)}, u32[]{:S(2)}, u32[]{:S(2)}) %collective-permute-start.5) | collective-permute-done | bytes 45088 | tf_op jit(solution)/shard_map/ppermute | solution.py:371
  18.6 0.6 %collective-permute-done.4 = f32[1,88,128]{2,1,0:T(8,128)S(1)} collective-permute-done((f32[1,88,128]{2,1,0:T(8,128)S(1)}, f32[1,88,128]{2,1,0:T(8,128)S(1)}, u32[]{:S(2)}, u32[]{:S(2)}) %collective-permute-start.4) | collective-permute-done | bytes 45088 | tf_op jit(solution)/shard_map/ppermute | solution.py:371
  19.2 1.3 %collective-permute-done.3 = f32[1,88,128]{2,1,0:T(8,128)S(1)} collective-permute-done((f32[1,88,128]{2,1,0:T(8,128)S(1)}, f32[1,88,128]{2,1,0:T(8,128)S(1)}, u32[]{:S(2)}, u32[]{:S(2)}) %collective-permute-start.3) | collective-permute-done | bytes 45088 | tf_op jit(solution)/shard_map/ppermute | solution.py:371
  20.5 0.2 collective-permute-start.6
  20.7 0.0 copy-start
  20.7 1.1 %copy.17 = f32[24,16,1024]{2,1,0:T(8,128)} copy(f32[24,16,1024]{2,1,0:T(8,128)S(1)} %get-tuple-element.13) | data formatting | bytes 3145728
  21.8 0.1 collective-permute-done.6.refs_1_
  22.0 0.0 copy-done
  22.0 4.0 %gain.1 = f32[4,16,64]{2,1,0:T(8,128)S(1)} custom-call(s32[1]{0:T(128)} %bitcast.index, s32[3,32]{1,0:T(4,128)S(1)} %bitcast.8, f32[4,88,128]{2,1,0:T(8,128)S(1)} %pad_maximum_fusion.refs_0_, f32[4,88,128]{2,1,0:T(8,128)S(1)} %collective-permute-done.6.refs_1_), custom_call_target="tpu_custom_call" | custom-call | flops 1 | bytes 1 | tf_op jit(solution)/shard_map/gain/pallas_call | solution.py:293
  25.9 0.0 collective-permute-done.8.refs_2_
  26.0 0.0 collective-permute-done.7.refs_1_
  26.0 1.2 %update.1 = f32[16,4,1024]{2,1,0:T(4,128)} custom-call(f32[4,16,64]{2,1,0:T(8,128)S(1)} %gain.1, f32[17,16,128]{2,1,0:T(8,128)S(1)} %get-tuple-element.8.wet_own, f32[2,16,1024]{2,1,0:T(8,128)S(1)} %carry.3.dry, f32[17,16,128]{2,1,0:T(8,128)S(1)} %collective-permute-done.refs_0_, f32[17,16,128]{2,1,0:T(8,128)S(1)} %collective-permute-done.7.refs_1_, ...), custom_call_target="tpu_custom_call" | custom-call | tf_op jit(solution)/shard_map/update/pallas_call | solution.py:356
  (8 shorter events, 0.0 us)
Async XLA Ops:
  4.5 8.7 %collective-permute-start = (f32[17,16,128]{2,1,0:T(8,128)S(1)}, f32[17,16,128]{2,1,0:T(8,128)S(1)}, u32[]{:S(2)}, u32[]{:S(2)}) collective-permute-start(f32[17,16,128]{2,1,0:T(8,128)S(1)} %get-tuple-element.8.wet_own), channel_id=1, source_target_pairs={{0,1},{1,0},{2,3},{3,2},{4,5},{5,4},{6,7},{7,6},{8,9},{9,8},{10,11... | collective-permute-start | bytes 417800 | tf_op jit(solution)/shard_map/ppermute | solution.py:371
  7.6 5.6 %collective-permute-start.2 = (f32[16,128]{1,0:T(8,128)S(1)}, f32[16,128]{1,0:T(8,128)S(1)}, u32[]{:S(2)}, u32[]{:S(2)}) collective-permute-start(f32[16,128]{1,0:T(8,128)S(1)} %get-tuple-element.7), channel_id=1, source_target_pairs={{0,7},{1,6},{2,5},{3,4},{4,3},{5,2},{6,1},{7,0},{8,15},{9,14},{10,... | collective-permute-start | bytes 24584 | tf_op jit(solution)/shard_map/ppermute | solution.py:381
  9.2 4.0 %collective-permute-start.1 = (f32[16,128]{1,0:T(8,128)S(1)}, f32[16,128]{1,0:T(8,128)S(1)}, u32[]{:S(2)}, u32[]{:S(2)}) collective-permute-start(f32[16,128]{1,0:T(8,128)S(1)} %get-tuple-element.7), channel_id=1, source_target_pairs={{0,6},{1,7},{2,4},{3,5},{4,2},{5,3},{6,0},{7,1},{8,14},{9,15},{10,... | collective-permute-start | bytes 24584 | tf_op jit(solution)/shard_map/ppermute | solution.py:381
  9.3 16.6 %collective-permute-start.8 = (f32[17,16,128]{2,1,0:T(8,128)S(1)}, f32[17,16,128]{2,1,0:T(8,128)S(1)}, u32[]{:S(2)}, u32[]{:S(2)}) collective-permute-start(f32[17,16,128]{2,1,0:T(8,128)S(1)} %get-tuple-element.8.wet_own), channel_id=1, source_target_pairs={{0,3},{1,2},{2,1},{3,0},{4,7},{5,6},{6,5},{7,4},{8,11},{9,10},{10,... | collective-permute-start | bytes 417800 | tf_op jit(solution)/shard_map/ppermute | solution.py:371
  12.8 13.2 %collective-permute-start.7 = (f32[17,16,128]{2,1,0:T(8,128)S(1)}, f32[17,16,128]{2,1,0:T(8,128)S(1)}, u32[]{:S(2)}, u32[]{:S(2)}) collective-permute-start(f32[17,16,128]{2,1,0:T(8,128)S(1)} %get-tuple-element.8.wet_own), channel_id=1, source_target_pairs={{0,2},{1,3},{2,0},{3,1},{4,6},{5,7},{6,4},{7,5},{8,10},{9,11},{10,... | collective-permute-start | bytes 417800 | tf_op jit(solution)/shard_map/ppermute | solution.py:371
  13.2 5.4 %collective-permute-start.5 = (f32[1,88,128]{2,1,0:T(8,128)S(1)}, f32[1,88,128]{2,1,0:T(8,128)S(1)}, u32[]{:S(2)}, u32[]{:S(2)}) collective-permute-start(f32[1,88,128]{2,1,0:T(8,128)S(1)} %bitcast.9), channel_id=1, source_target_pairs={{0,24},{4,28},{8,16},{12,20},{16,8},{20,12},{24,0},{28,4},{1,25},{... | collective-permute-start | bytes 135176 | tf_op jit(solution)/shard_map/ppermute | solution.py:371
  15.7 3.5 %collective-permute-start.4 = (f32[1,88,128]{2,1,0:T(8,128)S(1)}, f32[1,88,128]{2,1,0:T(8,128)S(1)}, u32[]{:S(2)}, u32[]{:S(2)}) collective-permute-start(f32[1,88,128]{2,1,0:T(8,128)S(1)} %bitcast.10), channel_id=1, source_target_pairs={{0,20},{4,16},{8,28},{12,24},{16,4},{20,0},{24,12},{28,8},{1,21},{... | collective-permute-start | bytes 135176 | tf_op jit(solution)/shard_map/ppermute | solution.py:371
  16.6 3.9 %collective-permute-start.3 = (f32[1,88,128]{2,1,0:T(8,128)S(1)}, f32[1,88,128]{2,1,0:T(8,128)S(1)}, u32[]{:S(2)}, u32[]{:S(2)}) collective-permute-start(f32[1,88,128]{2,1,0:T(8,128)S(1)} %bitcast.11), channel_id=1, source_target_pairs={{0,12},{4,8},{8,4},{12,0},{16,28},{20,24},{24,20},{28,16},{1,13},{... | collective-permute-start | bytes 135176 | tf_op jit(solution)/shard_map/ppermute | solution.py:371
  20.5 1.5 %collective-permute-start.6 = (f32[4,88,128]{2,1,0:T(8,128)S(1)}, f32[4,88,128]{2,1,0:T(8,128)S(1)}, u32[]{:S(2)}, u32[]{:S(2)}) collective-permute-start(f32[4,88,128]{2,1,0:T(8,128)S(1)} %pad_maximum_fusion.refs_0_), channel_id=1, source_target_pairs={{0,4},{4,0},{8,12},{12,8},{16,20},{20,16},{24,28},{28,24},{1,5},{5... | collective-permute-start | bytes 540680 | tf_op jit(solution)/shard_map/ppermute | solution.py:371
  20.7 1.3 %copy-start = (s32[32,3]{0,1:T(4,128)S(1)}, s32[32,3]{0,1:T(4,128)}, u32[]{:S(2)}) copy-start(s32[32,3]{0,1:T(4,128)} %param.21) | copy-start | bytes 1156

commit v5 on v4

--- a/solution.py
+++ b/solution.py
@@ -19,6 +19,7 @@
 STRIP = 512
 COSTS = (10**10, 10**10)
 MERGE = (1,)
+MEMBERS = (1, 3, 2)
 CHUNK = 6
 PACK = 40
 VMEM_LIMIT = 16 * 1024 * 1024
@@ -182,7 +183,8 @@
 
 
 def spread_lane(x, k):
-    return jnp.broadcast_to(x[:, k : k + 1], (8, LOCAL))
+    where = jnp.full((8, LOCAL), k, jnp.int32)
+    return jnp.take_along_axis(x, where, axis=1, mode="promise_in_bounds")
 
 
 def spread_row(x, k):
@@ -251,11 +253,13 @@
             if relative:
                 owner = owner ^ me
                 far = (owner // 4 + owner // 2 + owner) % 2
-                near = table[far * (at // 2) + owner // 2]
-                far = table[(1 - far) * (at // 2) + owner // 2]
+                place = (at // 2 - owner // 2) % (at // 2)
+                near = table[far * (at // 2) + place]
+                far = table[(1 - far) * (at // 2) + place]
+                flips = [0] + [k for k in MEMBERS if k < total // members]
                 parts = [
-                    (near if k in (0,) + MERGE else far)[k * members : (k + 1) * members]
-                    for k in range(total // members)
+                    (near if k in (0,) + MERGE else far)[p * members : (p + 1) * members]
+                    for p, k in enumerate(flips)
                 ]
                 found = jnp.concatenate(parts + [near[total:]], axis=0)
             else:
@@ -319,6 +323,30 @@
     )(x)
 
 
+def store_kernel(flow, x, flow_hbm, y, sem):
+    copy = pltpu.make_async_copy(flow, flow_hbm, sem)
+    copy.start()
+    y[...] = x[...]
+    copy.wait()
+
+
+def store(flow, x, cost):
+    vmem = pl.BlockSpec(memory_space=pltpu.VMEM)
+    return pl.pallas_call(
+        store_kernel,
+        out_shape=(
+            jax.ShapeDtypeStruct(flow.shape, flow.dtype),
+            jax.ShapeDtypeStruct(x.shape, x.dtype),
+        ),
+        in_specs=[vmem, vmem],
+        out_specs=(pl.BlockSpec(memory_space=pltpu.HBM), vmem),
+        scratch_shapes=[pltpu.SemaphoreType.DMA],
+        compiler_params=pltpu.CompilerParams(vmem_limit_bytes=VMEM_LIMIT),
+        cost_estimate=pl.CostEstimate(flops=cost, bytes_accessed=0, transcendentals=0),
+        name="store",
+    )(flow, x)
+
+
 def update_kernel(gain, wet_own, dry, *refs):
     wets, (analysis_hbm, analysis, out_sems) = refs[:-3], refs[-3:]
     blocks = gain.shape[0]
@@ -333,18 +361,22 @@
         analysis[:, 0, where] = dry[0, :, where]
         analysis[:, 3, where] = dry[1, :, where]
         for k in range(2):
-            for t in range(b * NB // LOCAL, (b + 1) * NB // LOCAL):
-                at = k * tiles + t
-                if len(wets[0].shape) == 3:
-                    states = [wet_own[at]] + [w[at] for w in wets]
-                else:
-                    states = [w[:, at].reshape(-1, LOCAL) for w in wets]
-                analysis[:, 1 + k, pl.ds(t * LOCAL, LOCAL)] = wet_own[at] + jnp.dot(
-                    gain[b],
-                    jnp.concatenate(states, axis=0),
-                    precision=HIGHEST,
-                    preferred_element_type=jnp.float32,
-                )
+            at = k * tiles + b * NB // LOCAL
+            spots = range(at, at + NB // LOCAL)
+
+            def side(x):
+                return jnp.concatenate([x[t] for t in spots], axis=1)
+
+            if len(wets[0].shape) == 3:
+                states = [side(wet_own)] + [side(w) for w in wets]
+            else:
+                states = [jnp.concatenate([w[:, t] for t in spots], axis=2).reshape(-1, NB) for w in wets]
+            analysis[:, 1 + k, where] = side(wet_own) + jnp.dot(
+                gain[b],
+                jnp.concatenate(states, axis=0),
+                precision=HIGHEST,
+                preferred_element_type=jnp.float32,
+            )
         out_copy(b).start()
     for b in range(blocks):
         out_copy(b).wait()
@@ -413,16 +445,16 @@
     adjacency = jnp.transpose(adjacent_block_list)
     relative = basin_size <= 8 and member_size <= 4
     if relative:
-        others = list(range(1, member_size))
+        others = [k for k in MEMBERS if k < member_size]
         first = {k: permute(wet, "member", k) if k in MERGE else across(pred, k) for k in others}
         wets = [first[k] if k in MERGE else permute(wet, "member", k) for k in others]
         preds = [pred] + [first[k][-1] if k in MERGE else first[k] for k in others]
         near = jnp.concatenate(preds + [fixed], axis=0)[None]
-        flips = [k for k in range(2, basin_size) if k % 8 in (3, 5, 6)]
+        flips = [k for k in range(basin_size - 1, 1, -1) if k in (3, 5, 6)]
         near = jnp.concatenate([near] + [permute(near, "basin", k) for k in flips], axis=0)
         packs = [near, permute(near, "basin", 1)]
-        for cost in COSTS:
-            dry = carry(dry, cost)
+        discharge, dry = store(discharge, dry, COSTS[0])
+        dry = carry(dry, COSTS[1])
     else:
         preds = lax.all_gather(pred, "member", axis=0).reshape(-1, LOCAL)
         wets = [lax.all_gather(wet, "member", axis=0)]

time: 27.4 us -> 26.7 us (0.974)
  local copies, waits for them, and re-layouts: 1.16 us -> 0.02 us
  Pallas kernels: 9.07 us -> 9.51 us
    pallas_call x0 -> x1, Pallas kernels: none -> 1.15 us  [store(): pl.pallas_call(store_kernel, out_shape=(jax.ShapeDtypeStruct(flow.shape,...]
    unnamed x7 -> x6, local copies, waits for them, and re-layouts: 1.16 us -> 0.01 us
    pallas_call x1, Pallas kernels: 3.98 us -> 3.49 us  [find_gain(): pl.pallas_call(functools.partial(gain_kernel, total, len(pieces), relativ...]
  transfers between devices with their start and end apart: 9 -> 9, of which waited for: 4 -> 5; matrix products, arithmetic and copies ran while one was open for 4% -> 0% of each run, Pallas kernels for 15% -> 17%
where the time goes in v5:
time: 26.7 us; the launch traced here: 26.6 us
  starting transfers between devices  12.2 us (46%)
  Pallas kernels  9.51 us (36%)
  waiting for transfers between devices  4.15 us (16%)
  between operations  0.71 us (3%)
    ppermute x7, starting transfers between devices, permute(): lax.ppermute(x, axis, [(i, i ^ mask) for i in range(lax.axis_size(axis))])  10.4 us
    ppermute x7, waiting for transfers between devices, permute(): lax.ppermute(x, axis, [(i, i ^ mask) for i in range(lax.axis_size(axis))])  4.13 us
    pallas_call x1, Pallas kernels, forecast(): pl.pallas_call(forecast_kernel, out_shape=(pltpu.VMEM((hours, members, wi...  3.83 us
    pallas_call x1, Pallas kernels, find_gain(): pl.pallas_call(functools.partial(gain_kernel, total, len(pieces), relativ...  3.49 us
    ppermute x2, starting transfers between devices, across(): return lax.ppermute(x, ('basin', 'member'), pairs)  1.75 us
    pallas_call x1, Pallas kernels, store(): pl.pallas_call(store_kernel, out_shape=(jax.ShapeDtypeStruct(flow.shape,...  1.15 us
    pallas_call x1, Pallas kernels, update(): pl.pallas_call(update_kernel, out_shape=jax.ShapeDtypeStruct((members, 4,...  1.03 us
  transfers between devices with their start and end apart: 9, of which 5 were waited for; matrix products, arithmetic and copies ran while one was open for 0% of the time, Pallas kernels for 17%

profile of v5, /device:TPU:0, one launch (start us, length us, event | category | flops | bytes accessed | tf_op | source)
XLA Modules:
  0.0 26.6 jit_solution(7369583789396597622)
XLA Ops:
  0.6 3.8 %forecast.1 = (f32[24,16,1024]{2,1,0:T(8,128)S(1)}, f32[17,16,128]{2,1,0:T(8,128)S(1)}, f32[2,16,1024]{2,1,0:T(8,128)S(1)}, f32[16,128]{1,0:T(8,128)S(1)}, f32[24,128]{1,0:T(8,128)S(1)}) custom-call(f32[16,4,1024]{2,1,0:T(4,128)} %refs_0_.1, f32[10,1024]{1,0:T(8,128)} %refs_1_.1, f32[24,16,1024]{2,1,0:T(8,128)} %refs_2_.1, f32[24,1024]{1,0:T(8,128)} %refs_3_.1, ...), custom_call_target="tpu_custom_call" | custom-call | tf_op jit(solution)/shard_map/forecast/pallas_call | solution.py:161
  4.5 3.1 %collective-permute-start = (f32[17,16,128]{2,1,0:T(8,128)S(1)}, f32[17,16,128]{2,1,0:T(8,128)S(1)}, u32[]{:S(2)}, u32[]{:S(2)}) collective-permute-start(f32[17,16,128]{2,1,0:T(8,128)S(1)} %get-tuple-element.10.wet_own), channel_id=1, source_target_pairs={{0,1},{1,0},{2,3},{3,2},{4,5},{5,4},{6,7},{7,6},{8,9},{9,8},{10,11... | collective-permute-start | bytes 417800 | tf_op jit(solution)/shard_map/ppermute | solution.py:403
  7.6 1.6 %collective-permute-start.1 = (f32[16,128]{1,0:T(8,128)S(1)}, f32[16,128]{1,0:T(8,128)S(1)}, u32[]{:S(2)}, u32[]{:S(2)}) collective-permute-start(f32[16,128]{1,0:T(8,128)S(1)} %get-tuple-element.9), channel_id=1, source_target_pairs={{0,7},{1,6},{2,5},{3,4},{4,3},{5,2},{6,1},{7,0},{8,15},{9,14},{10,... | collective-permute-start | bytes 24584 | tf_op jit(solution)/shard_map/ppermute | solution.py:413
  9.2 0.1 collective-permute-start.2
  9.3 3.5 %collective-permute-start.7 = (f32[17,16,128]{2,1,0:T(8,128)S(1)}, f32[17,16,128]{2,1,0:T(8,128)S(1)}, u32[]{:S(2)}, u32[]{:S(2)}) collective-permute-start(f32[17,16,128]{2,1,0:T(8,128)S(1)} %get-tuple-element.10.wet_own), channel_id=1, source_target_pairs={{0,3},{1,2},{2,1},{3,0},{4,7},{5,6},{6,5},{7,4},{8,11},{9,10},{10,... | collective-permute-start | bytes 417800 | tf_op jit(solution)/shard_map/ppermute | solution.py:403
  12.8 0.3 %collective-permute-start.8 = (f32[17,16,128]{2,1,0:T(8,128)S(1)}, f32[17,16,128]{2,1,0:T(8,128)S(1)}, u32[]{:S(2)}, u32[]{:S(2)}) collective-permute-start(f32[17,16,128]{2,1,0:T(8,128)S(1)} %get-tuple-element.10.wet_own), channel_id=1, source_target_pairs={{0,2},{1,3},{2,0},{3,1},{4,6},{5,7},{6,4},{7,5},{8,10},{9,11},{10,... | collective-permute-start | bytes 417800 | tf_op jit(solution)/shard_map/ppermute | solution.py:403
  13.1 0.0 collective-permute-done.refs_0_
  13.1 0.0 collective-permute-done.1
  13.2 0.0 collective-permute-done.2
  13.2 2.5 %collective-permute-start.3 = (f32[1,88,128]{2,1,0:T(8,128)S(1)}, f32[1,88,128]{2,1,0:T(8,128)S(1)}, u32[]{:S(2)}, u32[]{:S(2)}) collective-permute-start(f32[1,88,128]{2,1,0:T(8,128)S(1)} %bitcast.9), channel_id=1, source_target_pairs={{0,24},{4,28},{8,16},{12,20},{16,8},{20,12},{24,0},{28,4},{1,25},{... | collective-permute-start | bytes 135176 | tf_op jit(solution)/shard_map/ppermute | solution.py:403
  15.7 0.8 %collective-permute-start.4 = (f32[1,88,128]{2,1,0:T(8,128)S(1)}, f32[1,88,128]{2,1,0:T(8,128)S(1)}, u32[]{:S(2)}, u32[]{:S(2)}) collective-permute-start(f32[1,88,128]{2,1,0:T(8,128)S(1)} %bitcast.10), channel_id=1, source_target_pairs={{0,20},{4,16},{8,28},{12,24},{16,4},{20,0},{24,12},{28,8},{1,21},{... | collective-permute-start | bytes 135176 | tf_op jit(solution)/shard_map/ppermute | solution.py:403
  16.5 0.0 collective-permute-start.5
  16.5 1.1 %store.1 = (f32[24,16,1024]{2,1,0:T(8,128)}, f32[2,16,1024]{2,1,0:T(8,128)S(1)}) custom-call(f32[24,16,1024]{2,1,0:T(8,128)S(1)} %get-tuple-element.12.flow, f32[2,16,1024]{2,1,0:T(8,128)S(1)} %get-tuple-element.13.x), custom_call_target="tpu_custom_call" | custom-call | flops 10000000000 | tf_op jit(solution)/shard_map/store/pallas_call | solution.py:335
  17.7 1.0 %collective-permute-done.3 = f32[1,88,128]{2,1,0:T(8,128)S(1)} collective-permute-done((f32[1,88,128]{2,1,0:T(8,128)S(1)}, f32[1,88,128]{2,1,0:T(8,128)S(1)}, u32[]{:S(2)}, u32[]{:S(2)}) %collective-permute-start.3) | collective-permute-done | bytes 45088 | tf_op jit(solution)/shard_map/ppermute | solution.py:403
  18.7 0.5 %collective-permute-done.4 = f32[1,88,128]{2,1,0:T(8,128)S(1)} collective-permute-done((f32[1,88,128]{2,1,0:T(8,128)S(1)}, f32[1,88,128]{2,1,0:T(8,128)S(1)}, u32[]{:S(2)}, u32[]{:S(2)}) %collective-permute-start.4) | collective-permute-done | bytes 45088 | tf_op jit(solution)/shard_map/ppermute | solution.py:403
  19.2 1.2 %collective-permute-done.5 = f32[1,88,128]{2,1,0:T(8,128)S(1)} collective-permute-done((f32[1,88,128]{2,1,0:T(8,128)S(1)}, f32[1,88,128]{2,1,0:T(8,128)S(1)}, u32[]{:S(2)}, u32[]{:S(2)}) %collective-permute-start.5) | collective-permute-done | bytes 45088 | tf_op jit(solution)/shard_map/ppermute | solution.py:403
  20.4 0.2 collective-permute-start.6
  20.6 0.0 copy-start
  20.6 1.3 %collective-permute-done.6.refs_1_ = f32[4,88,128]{2,1,0:T(8,128)S(1)} collective-permute-done((f32[4,88,128]{2,1,0:T(8,128)S(1)}, f32[4,88,128]{2,1,0:T(8,128)S(1)}, u32[]{:S(2)}, u32[]{:S(2)}) %collective-permute-start.6) | collective-permute-done | bytes 180256 | tf_op jit(solution)/shard_map/ppermute | solution.py:403
  21.9 0.0 copy-done
  21.9 3.5 %gain.1 = f32[4,16,64]{2,1,0:T(8,128)S(1)} custom-call(s32[1]{0:T(128)} %bitcast.index, s32[3,32]{1,0:T(4,128)S(1)} %bitcast.8, f32[4,88,128]{2,1,0:T(8,128)S(1)} %pad_maximum_fusion.refs_0_, f32[4,88,128]{2,1,0:T(8,128)S(1)} %collective-permute-done.6.refs_1_), custom_call_target="tpu_custom_call" | custom-call | flops 1 | bytes 1 | tf_op jit(solution)/shard_map/gain/pallas_call | solution.py:297
  25.4 0.0 collective-permute-done.7.refs_1_
  25.4 0.1 collective-permute-done.8.refs_2_
  25.5 1.0 %update.1 = f32[16,4,1024]{2,1,0:T(4,128)} custom-call(f32[4,16,64]{2,1,0:T(8,128)S(1)} %gain.1, f32[17,16,128]{2,1,0:T(8,128)S(1)} %get-tuple-element.10.wet_own, f32[2,16,1024]{2,1,0:T(8,128)S(1)} %carry.1.dry, f32[17,16,128]{2,1,0:T(8,128)S(1)} %collective-permute-done.refs_0_, f32[17,16,128]{2,1,0:T(8,128)S(1)} %collective-permute-done.7.refs_1_, ...), custom_call_target="tpu_custom_call" | custom-call | tf_op jit(solution)/shard_map/update/pallas_call | solution.py:388
  (7 shorter events, 0.0 us)
Async XLA Ops:
  4.5 8.7 %collective-permute-start = (f32[17,16,128]{2,1,0:T(8,128)S(1)}, f32[17,16,128]{2,1,0:T(8,128)S(1)}, u32[]{:S(2)}, u32[]{:S(2)}) collective-permute-start(f32[17,16,128]{2,1,0:T(8,128)S(1)} %get-tuple-element.10.wet_own), channel_id=1, source_target_pairs={{0,1},{1,0},{2,3},{3,2},{4,5},{5,4},{6,7},{7,6},{8,9},{9,8},{10,11... | collective-permute-start | bytes 417800 | tf_op jit(solution)/shard_map/ppermute | solution.py:403
  7.6 5.6 %collective-permute-start.1 = (f32[16,128]{1,0:T(8,128)S(1)}, f32[16,128]{1,0:T(8,128)S(1)}, u32[]{:S(2)}, u32[]{:S(2)}) collective-permute-start(f32[16,128]{1,0:T(8,128)S(1)} %get-tuple-element.9), channel_id=1, source_target_pairs={{0,7},{1,6},{2,5},{3,4},{4,3},{5,2},{6,1},{7,0},{8,15},{9,14},{10,... | collective-permute-start | bytes 24584 | tf_op jit(solution)/shard_map/ppermute | solution.py:413
  9.2 4.0 %collective-permute-start.2 = (f32[16,128]{1,0:T(8,128)S(1)}, f32[16,128]{1,0:T(8,128)S(1)}, u32[]{:S(2)}, u32[]{:S(2)}) collective-permute-start(f32[16,128]{1,0:T(8,128)S(1)} %get-tuple-element.9), channel_id=1, source_target_pairs={{0,6},{1,7},{2,4},{3,5},{4,2},{5,3},{6,0},{7,1},{8,14},{9,15},{10,... | collective-permute-start | bytes 24584 | tf_op jit(solution)/shard_map/ppermute | solution.py:413
  9.3 16.1 %collective-permute-start.7 = (f32[17,16,128]{2,1,0:T(8,128)S(1)}, f32[17,16,128]{2,1,0:T(8,128)S(1)}, u32[]{:S(2)}, u32[]{:S(2)}) collective-permute-start(f32[17,16,128]{2,1,0:T(8,128)S(1)} %get-tuple-element.10.wet_own), channel_id=1, source_target_pairs={{0,3},{1,2},{2,1},{3,0},{4,7},{5,6},{6,5},{7,4},{8,11},{9,10},{10,... | collective-permute-start | bytes 417800 | tf_op jit(solution)/shard_map/ppermute | solution.py:403
  12.8 12.7 %collective-permute-start.8 = (f32[17,16,128]{2,1,0:T(8,128)S(1)}, f32[17,16,128]{2,1,0:T(8,128)S(1)}, u32[]{:S(2)}, u32[]{:S(2)}) collective-permute-start(f32[17,16,128]{2,1,0:T(8,128)S(1)} %get-tuple-element.10.wet_own), channel_id=1, source_target_pairs={{0,2},{1,3},{2,0},{3,1},{4,6},{5,7},{6,4},{7,5},{8,10},{9,11},{10,... | collective-permute-start | bytes 417800 | tf_op jit(solution)/shard_map/ppermute | solution.py:403
  13.2 5.5 %collective-permute-start.3 = (f32[1,88,128]{2,1,0:T(8,128)S(1)}, f32[1,88,128]{2,1,0:T(8,128)S(1)}, u32[]{:S(2)}, u32[]{:S(2)}) collective-permute-start(f32[1,88,128]{2,1,0:T(8,128)S(1)} %bitcast.9), channel_id=1, source_target_pairs={{0,24},{4,28},{8,16},{12,20},{16,8},{20,12},{24,0},{28,4},{1,25},{... | collective-permute-start | bytes 135176 | tf_op jit(solution)/shard_map/ppermute | solution.py:403
  15.7 3.5 %collective-permute-start.4 = (f32[1,88,128]{2,1,0:T(8,128)S(1)}, f32[1,88,128]{2,1,0:T(8,128)S(1)}, u32[]{:S(2)}, u32[]{:S(2)}) collective-permute-start(f32[1,88,128]{2,1,0:T(8,128)S(1)} %bitcast.10), channel_id=1, source_target_pairs={{0,20},{4,16},{8,28},{12,24},{16,4},{20,0},{24,12},{28,8},{1,21},{... | collective-permute-start | bytes 135176 | tf_op jit(solution)/shard_map/ppermute | solution.py:403
  16.5 3.9 %collective-permute-start.5 = (f32[1,88,128]{2,1,0:T(8,128)S(1)}, f32[1,88,128]{2,1,0:T(8,128)S(1)}, u32[]{:S(2)}, u32[]{:S(2)}) collective-permute-start(f32[1,88,128]{2,1,0:T(8,128)S(1)} %bitcast.11), channel_id=1, source_target_pairs={{0,12},{4,8},{8,4},{12,0},{16,28},{20,24},{24,20},{28,16},{1,13},{... | collective-permute-start | bytes 135176 | tf_op jit(solution)/shard_map/ppermute | solution.py:403
  20.4 1.5 %collective-permute-start.6 = (f32[4,88,128]{2,1,0:T(8,128)S(1)}, f32[4,88,128]{2,1,0:T(8,128)S(1)}, u32[]{:S(2)}, u32[]{:S(2)}) collective-permute-start(f32[4,88,128]{2,1,0:T(8,128)S(1)} %pad_maximum_fusion.refs_0_), channel_id=1, source_target_pairs={{0,4},{4,0},{8,12},{12,8},{16,20},{20,16},{24,28},{28,24},{1,5},{5... | collective-permute-start | bytes 540680 | tf_op jit(solution)/shard_map/ppermute | solution.py:403
  20.6 1.3 %copy-start = (s32[32,3]{0,1:T(4,128)S(1)}, s32[32,3]{0,1:T(4,128)}, u32[]{:S(2)}) copy-start(s32[32,3]{0,1:T(4,128)} %param.21) | copy-start | bytes 1156

commit v6 on v5

--- a/solution.py
+++ b/solution.py
@@ -20,7 +20,7 @@
 COSTS = (10**10, 10**10)
 MERGE = (1,)
 MEMBERS = (1, 3, 2)
-CHUNK = 6
+CHUNK = 8
 PACK = 40
 VMEM_LIMIT = 16 * 1024 * 1024
 
@@ -235,14 +235,11 @@
 
 
 def gain_kernel(total, count, relative, index, adjacency, *refs):
-    pieces, (gain_out, table) = refs[:count], refs[count:]
-    at = 0
-    for piece in pieces:
-        table[at : at + piece.shape[0]] = piece[...]
-        at += piece.shape[0]
+    pieces, gain_out = refs[:count], refs[count]
+    chips = pieces[0].shape[0]
     me = index[0]
     blocks, members, _ = gain_out.shape
-    rows = table.shape[1]
+    rows = pieces[0].shape[1]
     lane = lax.broadcasted_iota(jnp.int32, (rows, LOCAL), 1) // OBS
     systems = []
     for b in range(blocks):
@@ -253,9 +250,9 @@
             if relative:
                 owner = owner ^ me
                 far = (owner // 4 + owner // 2 + owner) % 2
-                place = (at // 2 - owner // 2) % (at // 2)
-                near = table[far * (at // 2) + place]
-                far = table[(1 - far) * (at // 2) + place]
+                place = (chips - owner // 2) % chips
+                here, there = pieces[0][place], pieces[1][place]
+                near, far = jnp.where(far == 0, here, there), jnp.where(far == 0, there, here)
                 flips = [0] + [k for k in MEMBERS if k < total // members]
                 parts = [
                     (near if k in (0,) + MERGE else far)[p * members : (p + 1) * members]
@@ -263,7 +260,7 @@
                 ]
                 found = jnp.concatenate(parts + [near[total:]], axis=0)
             else:
-                found = table[owner]
+                found = pieces[0][owner]
             shift = ((i + blocks - source % blocks) % blocks) * OBS
             local = jnp.where(lane == i, pltpu.roll(found, shift, 1), local)
         pred, drawn = local[:total], local[total : total + members]
@@ -293,13 +290,11 @@
 def find_gain(pieces, relative, index, adjacency, blocks, members, total):
     vmem = pl.BlockSpec(memory_space=pltpu.VMEM)
     smem = pl.BlockSpec(memory_space=pltpu.SMEM)
-    owners = sum(p.shape[0] for p in pieces)
     return pl.pallas_call(
         functools.partial(gain_kernel, total, len(pieces), relative),
         out_shape=jax.ShapeDtypeStruct((blocks, members, total), jnp.float32),
         in_specs=[smem, smem] + [vmem] * len(pieces),
         out_specs=vmem,
-        scratch_shapes=[pltpu.VMEM((owners,) + pieces[0].shape[1:], jnp.float32)],
         compiler_params=pltpu.CompilerParams(vmem_limit_bytes=VMEM_LIMIT),
         cost_estimate=pl.CostEstimate(flops=1, bytes_accessed=1, transcendentals=0),
         name="gain",

time: 26.7 us -> 26.6 us (level)
  transfers between devices with their start and end apart: 9 -> 9, of which waited for: 5 -> 5; matrix products, arithmetic and copies ran while one was open for 0% -> 0% of each run, Pallas kernels for 17% -> 18%
where the time goes in v6:
time: 26.6 us; the launch traced here: 26.4 us
  starting transfers between devices  12.2 us (46%)
  Pallas kernels  9.32 us (35%)
  waiting for transfers between devices  4.16 us (16%)
  between operations  0.71 us (3%)
    ppermute x7, starting transfers between devices, permute(): lax.ppermute(x, axis, [(i, i ^ mask) for i in range(lax.axis_size(axis))])  10.4 us
    ppermute x7, waiting for transfers between devices, permute(): lax.ppermute(x, axis, [(i, i ^ mask) for i in range(lax.axis_size(axis))])  4.14 us
    pallas_call x1, Pallas kernels, forecast(): pl.pallas_call(forecast_kernel, out_shape=(pltpu.VMEM((hours, members, wi...  3.65 us
    pallas_call x1, Pallas kernels, find_gain(): pl.pallas_call(functools.partial(gain_kernel, total, len(pieces), relativ...  3.47 us
    ppermute x2, starting transfers between devices, across(): return lax.ppermute(x, ('basin', 'member'), pairs)  1.75 us
    pallas_call x1, Pallas kernels, store(): pl.pallas_call(store_kernel, out_shape=(jax.ShapeDtypeStruct(flow.shape,...  1.15 us
    pallas_call x1, Pallas kernels, update(): pl.pallas_call(update_kernel, out_shape=jax.ShapeDtypeStruct((members, 4,...  1.03 us
  transfers between devices with their start and end apart: 9, of which 5 were waited for; matrix products, arithmetic and copies ran while one was open for 0% of the time, Pallas kernels for 18%

profile of v6, /device:TPU:0, one launch (start us, length us, event | category | flops | bytes accessed | tf_op | source)
XLA Modules:
  0.0 26.4 jit_solution(15241761786518650223)
XLA Ops:
  0.6 3.7 %forecast.1 = (f32[24,16,1024]{2,1,0:T(8,128)S(1)}, f32[17,16,128]{2,1,0:T(8,128)S(1)}, f32[2,16,1024]{2,1,0:T(8,128)S(1)}, f32[16,128]{1,0:T(8,128)S(1)}, f32[24,128]{1,0:T(8,128)S(1)}) custom-call(f32[16,4,1024]{2,1,0:T(4,128)} %refs_0_.1, f32[10,1024]{1,0:T(8,128)} %refs_1_.1, f32[24,16,1024]{2,1,0:T(8,128)} %refs_2_.1, f32[24,1024]{1,0:T(8,128)} %refs_3_.1, ...), custom_call_target="tpu_custom_call" | custom-call | tf_op jit(solution)/shard_map/forecast/pallas_call | solution.py:161
  4.3 3.1 %collective-permute-start = (f32[17,16,128]{2,1,0:T(8,128)S(1)}, f32[17,16,128]{2,1,0:T(8,128)S(1)}, u32[]{:S(2)}, u32[]{:S(2)}) collective-permute-start(f32[17,16,128]{2,1,0:T(8,128)S(1)} %get-tuple-element.10.wet_own), channel_id=1, source_target_pairs={{0,1},{1,0},{2,3},{3,2},{4,5},{5,4},{6,7},{7,6},{8,9},{9,8},{10,11... | collective-permute-start | bytes 417800 | tf_op jit(solution)/shard_map/ppermute | solution.py:398
  7.4 1.6 %collective-permute-start.1 = (f32[16,128]{1,0:T(8,128)S(1)}, f32[16,128]{1,0:T(8,128)S(1)}, u32[]{:S(2)}, u32[]{:S(2)}) collective-permute-start(f32[16,128]{1,0:T(8,128)S(1)} %get-tuple-element.9), channel_id=1, source_target_pairs={{0,7},{1,6},{2,5},{3,4},{4,3},{5,2},{6,1},{7,0},{8,15},{9,14},{10,... | collective-permute-start | bytes 24584 | tf_op jit(solution)/shard_map/ppermute | solution.py:408
  9.0 0.1 collective-permute-start.2
  9.1 3.5 %collective-permute-start.7 = (f32[17,16,128]{2,1,0:T(8,128)S(1)}, f32[17,16,128]{2,1,0:T(8,128)S(1)}, u32[]{:S(2)}, u32[]{:S(2)}) collective-permute-start(f32[17,16,128]{2,1,0:T(8,128)S(1)} %get-tuple-element.10.wet_own), channel_id=1, source_target_pairs={{0,3},{1,2},{2,1},{3,0},{4,7},{5,6},{6,5},{7,4},{8,11},{9,10},{10,... | collective-permute-start | bytes 417800 | tf_op jit(solution)/shard_map/ppermute | solution.py:398
  12.6 0.3 %collective-permute-start.8 = (f32[17,16,128]{2,1,0:T(8,128)S(1)}, f32[17,16,128]{2,1,0:T(8,128)S(1)}, u32[]{:S(2)}, u32[]{:S(2)}) collective-permute-start(f32[17,16,128]{2,1,0:T(8,128)S(1)} %get-tuple-element.10.wet_own), channel_id=1, source_target_pairs={{0,2},{1,3},{2,0},{3,1},{4,6},{5,7},{6,4},{7,5},{8,10},{9,11},{10,... | collective-permute-start | bytes 417800 | tf_op jit(solution)/shard_map/ppermute | solution.py:398
  13.0 0.0 collective-permute-done.refs_0_
  13.0 0.0 collective-permute-done.1
  13.0 0.0 collective-permute-done.2
  13.0 2.5 %collective-permute-start.3 = (f32[1,88,128]{2,1,0:T(8,128)S(1)}, f32[1,88,128]{2,1,0:T(8,128)S(1)}, u32[]{:S(2)}, u32[]{:S(2)}) collective-permute-start(f32[1,88,128]{2,1,0:T(8,128)S(1)} %bitcast.9), channel_id=1, source_target_pairs={{0,24},{4,28},{8,16},{12,20},{16,8},{20,12},{24,0},{28,4},{1,25},{... | collective-permute-start | bytes 135176 | tf_op jit(solution)/shard_map/ppermute | solution.py:398
  15.5 0.8 %collective-permute-start.4 = (f32[1,88,128]{2,1,0:T(8,128)S(1)}, f32[1,88,128]{2,1,0:T(8,128)S(1)}, u32[]{:S(2)}, u32[]{:S(2)}) collective-permute-start(f32[1,88,128]{2,1,0:T(8,128)S(1)} %bitcast.10), channel_id=1, source_target_pairs={{0,20},{4,16},{8,28},{12,24},{16,4},{20,0},{24,12},{28,8},{1,21},{... | collective-permute-start | bytes 135176 | tf_op jit(solution)/shard_map/ppermute | solution.py:398
  16.3 0.0 collective-permute-start.5
  16.4 1.1 %store.1 = (f32[24,16,1024]{2,1,0:T(8,128)}, f32[2,16,1024]{2,1,0:T(8,128)S(1)}) custom-call(f32[24,16,1024]{2,1,0:T(8,128)S(1)} %get-tuple-element.12.flow, f32[2,16,1024]{2,1,0:T(8,128)S(1)} %get-tuple-element.13.x), custom_call_target="tpu_custom_call" | custom-call | flops 10000000000 | tf_op jit(solution)/shard_map/store/pallas_call | solution.py:330
  17.5 1.0 %collective-permute-done.3 = f32[1,88,128]{2,1,0:T(8,128)S(1)} collective-permute-done((f32[1,88,128]{2,1,0:T(8,128)S(1)}, f32[1,88,128]{2,1,0:T(8,128)S(1)}, u32[]{:S(2)}, u32[]{:S(2)}) %collective-permute-start.3) | collective-permute-done | bytes 45088 | tf_op jit(solution)/shard_map/ppermute | solution.py:398
  18.5 0.5 %collective-permute-done.4 = f32[1,88,128]{2,1,0:T(8,128)S(1)} collective-permute-done((f32[1,88,128]{2,1,0:T(8,128)S(1)}, f32[1,88,128]{2,1,0:T(8,128)S(1)}, u32[]{:S(2)}, u32[]{:S(2)}) %collective-permute-start.4) | collective-permute-done | bytes 45088 | tf_op jit(solution)/shard_map/ppermute | solution.py:398
  19.0 1.2 %collective-permute-done.5 = f32[1,88,128]{2,1,0:T(8,128)S(1)} collective-permute-done((f32[1,88,128]{2,1,0:T(8,128)S(1)}, f32[1,88,128]{2,1,0:T(8,128)S(1)}, u32[]{:S(2)}, u32[]{:S(2)}) %collective-permute-start.5) | collective-permute-done | bytes 45088 | tf_op jit(solution)/shard_map/ppermute | solution.py:398
  20.2 0.2 collective-permute-start.6
  20.4 0.0 copy-start
  20.4 1.3 %collective-permute-done.6.refs_1_ = f32[4,88,128]{2,1,0:T(8,128)S(1)} collective-permute-done((f32[4,88,128]{2,1,0:T(8,128)S(1)}, f32[4,88,128]{2,1,0:T(8,128)S(1)}, u32[]{:S(2)}, u32[]{:S(2)}) %collective-permute-start.6) | collective-permute-done | bytes 180256 | tf_op jit(solution)/shard_map/ppermute | solution.py:398
  21.7 0.0 copy-done
  21.7 3.5 %gain.1 = f32[4,16,64]{2,1,0:T(8,128)S(1)} custom-call(s32[1]{0:T(128)} %bitcast.index, s32[3,32]{1,0:T(4,128)S(1)} %bitcast.8, f32[4,88,128]{2,1,0:T(8,128)S(1)} %pad_maximum_fusion.refs_0_, f32[4,88,128]{2,1,0:T(8,128)S(1)} %collective-permute-done.6.refs_1_), custom_call_target="tpu_custom_call" | custom-call | flops 1 | bytes 1 | tf_op jit(solution)/shard_map/gain/pallas_call | solution.py:293
  25.2 0.0 collective-permute-done.7.refs_1_
  25.2 0.2 collective-permute-done.8.refs_2_
  25.4 1.0 %update.1 = f32[16,4,1024]{2,1,0:T(4,128)} custom-call(f32[4,16,64]{2,1,0:T(8,128)S(1)} %gain.1, f32[17,16,128]{2,1,0:T(8,128)S(1)} %get-tuple-element.10.wet_own, f32[2,16,1024]{2,1,0:T(8,128)S(1)} %carry.1.dry, f32[17,16,128]{2,1,0:T(8,128)S(1)} %collective-permute-done.refs_0_, f32[17,16,128]{2,1,0:T(8,128)S(1)} %collective-permute-done.7.refs_1_, ...), custom_call_target="tpu_custom_call" | custom-call | tf_op jit(solution)/shard_map/update/pallas_call | solution.py:383
  (7 shorter events, 0.0 us)
Async XLA Ops:
  4.3 8.7 %collective-permute-start = (f32[17,16,128]{2,1,0:T(8,128)S(1)}, f32[17,16,128]{2,1,0:T(8,128)S(1)}, u32[]{:S(2)}, u32[]{:S(2)}) collective-permute-start(f32[17,16,128]{2,1,0:T(8,128)S(1)} %get-tuple-element.10.wet_own), channel_id=1, source_target_pairs={{0,1},{1,0},{2,3},{3,2},{4,5},{5,4},{6,7},{7,6},{8,9},{9,8},{10,11... | collective-permute-start | bytes 417800 | tf_op jit(solution)/shard_map/ppermute | solution.py:398
  7.4 5.6 %collective-permute-start.1 = (f32[16,128]{1,0:T(8,128)S(1)}, f32[16,128]{1,0:T(8,128)S(1)}, u32[]{:S(2)}, u32[]{:S(2)}) collective-permute-start(f32[16,128]{1,0:T(8,128)S(1)} %get-tuple-element.9), channel_id=1, source_target_pairs={{0,7},{1,6},{2,5},{3,4},{4,3},{5,2},{6,1},{7,0},{8,15},{9,14},{10,... | collective-permute-start | bytes 24584 | tf_op jit(solution)/shard_map/ppermute | solution.py:408
  9.0 4.0 %collective-permute-start.2 = (f32[16,128]{1,0:T(8,128)S(1)}, f32[16,128]{1,0:T(8,128)S(1)}, u32[]{:S(2)}, u32[]{:S(2)}) collective-permute-start(f32[16,128]{1,0:T(8,128)S(1)} %get-tuple-element.9), channel_id=1, source_target_pairs={{0,6},{1,7},{2,4},{3,5},{4,2},{5,3},{6,0},{7,1},{8,14},{9,15},{10,... | collective-permute-start | bytes 24584 | tf_op jit(solution)/shard_map/ppermute | solution.py:408
  9.1 16.1 %collective-permute-start.7 = (f32[17,16,128]{2,1,0:T(8,128)S(1)}, f32[17,16,128]{2,1,0:T(8,128)S(1)}, u32[]{:S(2)}, u32[]{:S(2)}) collective-permute-start(f32[17,16,128]{2,1,0:T(8,128)S(1)} %get-tuple-element.10.wet_own), channel_id=1, source_target_pairs={{0,3},{1,2},{2,1},{3,0},{4,7},{5,6},{6,5},{7,4},{8,11},{9,10},{10,... | collective-permute-start | bytes 417800 | tf_op jit(solution)/shard_map/ppermute | solution.py:398
  12.6 12.7 %collective-permute-start.8 = (f32[17,16,128]{2,1,0:T(8,128)S(1)}, f32[17,16,128]{2,1,0:T(8,128)S(1)}, u32[]{:S(2)}, u32[]{:S(2)}) collective-permute-start(f32[17,16,128]{2,1,0:T(8,128)S(1)} %get-tuple-element.10.wet_own), channel_id=1, source_target_pairs={{0,2},{1,3},{2,0},{3,1},{4,6},{5,7},{6,4},{7,5},{8,10},{9,11},{10,... | collective-permute-start | bytes 417800 | tf_op jit(solution)/shard_map/ppermute | solution.py:398
  13.0 5.5 %collective-permute-start.3 = (f32[1,88,128]{2,1,0:T(8,128)S(1)}, f32[1,88,128]{2,1,0:T(8,128)S(1)}, u32[]{:S(2)}, u32[]{:S(2)}) collective-permute-start(f32[1,88,128]{2,1,0:T(8,128)S(1)} %bitcast.9), channel_id=1, source_target_pairs={{0,24},{4,28},{8,16},{12,20},{16,8},{20,12},{24,0},{28,4},{1,25},{... | collective-permute-start | bytes 135176 | tf_op jit(solution)/shard_map/ppermute | solution.py:398
  15.5 3.5 %collective-permute-start.4 = (f32[1,88,128]{2,1,0:T(8,128)S(1)}, f32[1,88,128]{2,1,0:T(8,128)S(1)}, u32[]{:S(2)}, u32[]{:S(2)}) collective-permute-start(f32[1,88,128]{2,1,0:T(8,128)S(1)} %bitcast.10), channel_id=1, source_target_pairs={{0,20},{4,16},{8,28},{12,24},{16,4},{20,0},{24,12},{28,8},{1,21},{... | collective-permute-start | bytes 135176 | tf_op jit(solution)/shard_map/ppermute | solution.py:398
  16.3 3.9 %collective-permute-start.5 = (f32[1,88,128]{2,1,0:T(8,128)S(1)}, f32[1,88,128]{2,1,0:T(8,128)S(1)}, u32[]{:S(2)}, u32[]{:S(2)}) collective-permute-start(f32[1,88,128]{2,1,0:T(8,128)S(1)} %bitcast.11), channel_id=1, source_target_pairs={{0,12},{4,8},{8,4},{12,0},{16,28},{20,24},{24,20},{28,16},{1,13},{... | collective-permute-start | bytes 135176 | tf_op jit(solution)/shard_map/ppermute | solution.py:398
  20.2 1.5 %collective-permute-start.6 = (f32[4,88,128]{2,1,0:T(8,128)S(1)}, f32[4,88,128]{2,1,0:T(8,128)S(1)}, u32[]{:S(2)}, u32[]{:S(2)}) collective-permute-start(f32[4,88,128]{2,1,0:T(8,128)S(1)} %pad_maximum_fusion.refs_0_), channel_id=1, source_target_pairs={{0,4},{4,0},{8,12},{12,8},{16,20},{20,16},{24,28},{28,24},{1,5},{5... | collective-permute-start | bytes 540680 | tf_op jit(solution)/shard_map/ppermute | solution.py:398
  20.4 1.3 %copy-start = (s32[32,3]{0,1:T(4,128)S(1)}, s32[32,3]{0,1:T(4,128)}, u32[]{:S(2)}) copy-start(s32[32,3]{0,1:T(4,128)} %param.21) | copy-start | bytes 1156

commit v7 on v6

--- a/solution.py
+++ b/solution.py
@@ -89,20 +89,19 @@
             fall = rain[h, :, where]
             snow_fall = share[pl.ds(h, 1), where] * fall
             snow = snow + snow_fall
-            melt = jnp.minimum(melt_cap[pl.ds(h, 1), where], snow)
-            snow = snow - melt
+            cap = melt_cap[pl.ds(h, 1), where]
+            melt = jnp.minimum(cap, snow)
+            snow = jnp.maximum(snow - cap, 0.0)
             inflow = (fall - snow_fall) + melt
             recharge = inflow * jnp.exp2(shape_exp * jnp.log2(moist * inv_cap))
             moist = moist + inflow - recharge
             excess = jnp.maximum(moist - field_cap, 0.0)
-            moist = moist - excess
-            actual = jnp.minimum(
-                evap[pl.ds(h, 1), where] * jnp.minimum(moist * inv_limit, 1.0), moist
-            )
-            moist = moist - actual
+            moist = jnp.minimum(moist, field_cap)
+            demand = evap[pl.ds(h, 1), where] * jnp.minimum(moist * inv_limit, 1.0)
+            moist = jnp.maximum(moist - demand, 0.0)
             upper = upper + recharge + excess
             perc_flow = jnp.minimum(percolation, upper)
-            upper = upper - perc_flow
+            upper = jnp.maximum(upper - percolation, 0.0)
             lower = lower + perc_flow
             fast = quick_rate * jnp.maximum(upper - upper_limit, 0.0) + upper_rate * upper
             base = lower_rate * lower

time: 26.6 us -> 26.6 us (level)
  transfers between devices with their start and end apart: 9 -> 9, of which waited for: 5 -> 5; matrix products, arithmetic and copies ran while one was open for 0% -> 0% of each run, Pallas kernels for 18% -> 17%
where the time goes in v7:
time: 26.6 us; the launch traced here: 26.5 us
  starting transfers between devices  12.2 us (46%)
  Pallas kernels  9.41 us (35%)
  waiting for transfers between devices  4.16 us (16%)
  between operations  0.71 us (3%)
    ppermute x7, starting transfers between devices, permute(): lax.ppermute(x, axis, [(i, i ^ mask) for i in range(lax.axis_size(axis))])  10.4 us
    ppermute x7, waiting for transfers between devices, permute(): lax.ppermute(x, axis, [(i, i ^ mask) for i in range(lax.axis_size(axis))])  4.14 us
    pallas_call x1, Pallas kernels, forecast(): pl.pallas_call(forecast_kernel, out_shape=(pltpu.VMEM((hours, members, wi...  3.74 us
    pallas_call x1, Pallas kernels, find_gain(): pl.pallas_call(functools.partial(gain_kernel, total, len(pieces), relativ...  3.47 us
    ppermute x2, starting transfers between devices, across(): return lax.ppermute(x, ('basin', 'member'), pairs)  1.75 us
    pallas_call x1, Pallas kernels, store(): pl.pallas_call(store_kernel, out_shape=(jax.ShapeDtypeStruct(flow.shape,...  1.15 us
    pallas_call x1, Pallas kernels, update(): pl.pallas_call(update_kernel, out_shape=jax.ShapeDtypeStruct((members, 4,...  1.03 us
  transfers between devices with their start and end apart: 9, of which 5 were waited for; matrix products, arithmetic and copies ran while one was open for 0% of the time, Pallas kernels for 17%

profile of v7, /device:TPU:0, one launch (start us, length us, event | category | flops | bytes accessed | tf_op | source)
XLA Modules:
  0.0 26.5 jit_solution(11264798381980220236)
XLA Ops:
  0.6 3.7 %forecast.1 = (f32[24,16,1024]{2,1,0:T(8,128)S(1)}, f32[17,16,128]{2,1,0:T(8,128)S(1)}, f32[2,16,1024]{2,1,0:T(8,128)S(1)}, f32[16,128]{1,0:T(8,128)S(1)}, f32[24,128]{1,0:T(8,128)S(1)}) custom-call(f32[16,4,1024]{2,1,0:T(4,128)} %refs_0_.1, f32[10,1024]{1,0:T(8,128)} %refs_1_.1, f32[24,16,1024]{2,1,0:T(8,128)} %refs_2_.1, f32[24,1024]{1,0:T(8,128)} %refs_3_.1, ...), custom_call_target="tpu_custom_call" | custom-call | tf_op jit(solution)/shard_map/forecast/pallas_call | solution.py:160
  4.4 3.1 %collective-permute-start = (f32[17,16,128]{2,1,0:T(8,128)S(1)}, f32[17,16,128]{2,1,0:T(8,128)S(1)}, u32[]{:S(2)}, u32[]{:S(2)}) collective-permute-start(f32[17,16,128]{2,1,0:T(8,128)S(1)} %get-tuple-element.10.wet_own), channel_id=1, source_target_pairs={{0,1},{1,0},{2,3},{3,2},{4,5},{5,4},{6,7},{7,6},{8,9},{9,8},{10,11... | collective-permute-start | bytes 417800 | tf_op jit(solution)/shard_map/ppermute | solution.py:397
  7.5 1.6 %collective-permute-start.1 = (f32[16,128]{1,0:T(8,128)S(1)}, f32[16,128]{1,0:T(8,128)S(1)}, u32[]{:S(2)}, u32[]{:S(2)}) collective-permute-start(f32[16,128]{1,0:T(8,128)S(1)} %get-tuple-element.9), channel_id=1, source_target_pairs={{0,7},{1,6},{2,5},{3,4},{4,3},{5,2},{6,1},{7,0},{8,15},{9,14},{10,... | collective-permute-start | bytes 24584 | tf_op jit(solution)/shard_map/ppermute | solution.py:407
  9.1 0.1 collective-permute-start.2
  9.2 3.5 %collective-permute-start.7 = (f32[17,16,128]{2,1,0:T(8,128)S(1)}, f32[17,16,128]{2,1,0:T(8,128)S(1)}, u32[]{:S(2)}, u32[]{:S(2)}) collective-permute-start(f32[17,16,128]{2,1,0:T(8,128)S(1)} %get-tuple-element.10.wet_own), channel_id=1, source_target_pairs={{0,3},{1,2},{2,1},{3,0},{4,7},{5,6},{6,5},{7,4},{8,11},{9,10},{10,... | collective-permute-start | bytes 417800 | tf_op jit(solution)/shard_map/ppermute | solution.py:397
  12.7 0.3 %collective-permute-start.8 = (f32[17,16,128]{2,1,0:T(8,128)S(1)}, f32[17,16,128]{2,1,0:T(8,128)S(1)}, u32[]{:S(2)}, u32[]{:S(2)}) collective-permute-start(f32[17,16,128]{2,1,0:T(8,128)S(1)} %get-tuple-element.10.wet_own), channel_id=1, source_target_pairs={{0,2},{1,3},{2,0},{3,1},{4,6},{5,7},{6,4},{7,5},{8,10},{9,11},{10,... | collective-permute-start | bytes 417800 | tf_op jit(solution)/shard_map/ppermute | solution.py:397
  13.0 0.0 collective-permute-done.refs_0_
  13.1 0.0 collective-permute-done.1
  13.1 0.0 collective-permute-done.2
  13.1 2.5 %collective-permute-start.3 = (f32[1,88,128]{2,1,0:T(8,128)S(1)}, f32[1,88,128]{2,1,0:T(8,128)S(1)}, u32[]{:S(2)}, u32[]{:S(2)}) collective-permute-start(f32[1,88,128]{2,1,0:T(8,128)S(1)} %bitcast.9), channel_id=1, source_target_pairs={{0,24},{4,28},{8,16},{12,20},{16,8},{20,12},{24,0},{28,4},{1,25},{... | collective-permute-start | bytes 135176 | tf_op jit(solution)/shard_map/ppermute | solution.py:397
  15.6 0.8 %collective-permute-start.4 = (f32[1,88,128]{2,1,0:T(8,128)S(1)}, f32[1,88,128]{2,1,0:T(8,128)S(1)}, u32[]{:S(2)}, u32[]{:S(2)}) collective-permute-start(f32[1,88,128]{2,1,0:T(8,128)S(1)} %bitcast.10), channel_id=1, source_target_pairs={{0,20},{4,16},{8,28},{12,24},{16,4},{20,0},{24,12},{28,8},{1,21},{... | collective-permute-start | bytes 135176 | tf_op jit(solution)/shard_map/ppermute | solution.py:397
  16.4 0.0 collective-permute-start.5
  16.4 1.1 %store.1 = (f32[24,16,1024]{2,1,0:T(8,128)}, f32[2,16,1024]{2,1,0:T(8,128)S(1)}) custom-call(f32[24,16,1024]{2,1,0:T(8,128)S(1)} %get-tuple-element.12.flow, f32[2,16,1024]{2,1,0:T(8,128)S(1)} %get-tuple-element.13.x), custom_call_target="tpu_custom_call" | custom-call | flops 10000000000 | tf_op jit(solution)/shard_map/store/pallas_call | solution.py:329
  17.6 1.0 %collective-permute-done.3 = f32[1,88,128]{2,1,0:T(8,128)S(1)} collective-permute-done((f32[1,88,128]{2,1,0:T(8,128)S(1)}, f32[1,88,128]{2,1,0:T(8,128)S(1)}, u32[]{:S(2)}, u32[]{:S(2)}) %collective-permute-start.3) | collective-permute-done | bytes 45088 | tf_op jit(solution)/shard_map/ppermute | solution.py:397
  18.6 0.5 %collective-permute-done.4 = f32[1,88,128]{2,1,0:T(8,128)S(1)} collective-permute-done((f32[1,88,128]{2,1,0:T(8,128)S(1)}, f32[1,88,128]{2,1,0:T(8,128)S(1)}, u32[]{:S(2)}, u32[]{:S(2)}) %collective-permute-start.4) | collective-permute-done | bytes 45088 | tf_op jit(solution)/shard_map/ppermute | solution.py:397
  19.1 1.2 %collective-permute-done.5 = f32[1,88,128]{2,1,0:T(8,128)S(1)} collective-permute-done((f32[1,88,128]{2,1,0:T(8,128)S(1)}, f32[1,88,128]{2,1,0:T(8,128)S(1)}, u32[]{:S(2)}, u32[]{:S(2)}) %collective-permute-start.5) | collective-permute-done | bytes 45088 | tf_op jit(solution)/shard_map/ppermute | solution.py:397
  20.3 0.2 collective-permute-start.6
  20.5 0.0 copy-start
  20.5 1.3 %collective-permute-done.6.refs_1_ = f32[4,88,128]{2,1,0:T(8,128)S(1)} collective-permute-done((f32[4,88,128]{2,1,0:T(8,128)S(1)}, f32[4,88,128]{2,1,0:T(8,128)S(1)}, u32[]{:S(2)}, u32[]{:S(2)}) %collective-permute-start.6) | collective-permute-done | bytes 180256 | tf_op jit(solution)/shard_map/ppermute | solution.py:397
  21.8 0.0 copy-done
  21.8 3.5 %gain.1 = f32[4,16,64]{2,1,0:T(8,128)S(1)} custom-call(s32[1]{0:T(128)} %bitcast.index, s32[3,32]{1,0:T(4,128)S(1)} %bitcast.8, f32[4,88,128]{2,1,0:T(8,128)S(1)} %pad_maximum_fusion.refs_0_, f32[4,88,128]{2,1,0:T(8,128)S(1)} %collective-permute-done.6.refs_1_), custom_call_target="tpu_custom_call" | custom-call | flops 1 | bytes 1 | tf_op jit(solution)/shard_map/gain/pallas_call | solution.py:292
  25.3 0.0 collective-permute-done.7.refs_1_
  25.3 0.2 collective-permute-done.8.refs_2_
  25.5 1.0 %update.1 = f32[16,4,1024]{2,1,0:T(4,128)} custom-call(f32[4,16,64]{2,1,0:T(8,128)S(1)} %gain.1, f32[17,16,128]{2,1,0:T(8,128)S(1)} %get-tuple-element.10.wet_own, f32[2,16,1024]{2,1,0:T(8,128)S(1)} %carry.1.dry, f32[17,16,128]{2,1,0:T(8,128)S(1)} %collective-permute-done.refs_0_, f32[17,16,128]{2,1,0:T(8,128)S(1)} %collective-permute-done.7.refs_1_, ...), custom_call_target="tpu_custom_call" | custom-call | tf_op jit(solution)/shard_map/update/pallas_call | solution.py:382
  (7 shorter events, 0.0 us)
Async XLA Ops:
  4.4 8.7 %collective-permute-start = (f32[17,16,128]{2,1,0:T(8,128)S(1)}, f32[17,16,128]{2,1,0:T(8,128)S(1)}, u32[]{:S(2)}, u32[]{:S(2)}) collective-permute-start(f32[17,16,128]{2,1,0:T(8,128)S(1)} %get-tuple-element.10.wet_own), channel_id=1, source_target_pairs={{0,1},{1,0},{2,3},{3,2},{4,5},{5,4},{6,7},{7,6},{8,9},{9,8},{10,11... | collective-permute-start | bytes 417800 | tf_op jit(solution)/shard_map/ppermute | solution.py:397
  7.5 5.6 %collective-permute-start.1 = (f32[16,128]{1,0:T(8,128)S(1)}, f32[16,128]{1,0:T(8,128)S(1)}, u32[]{:S(2)}, u32[]{:S(2)}) collective-permute-start(f32[16,128]{1,0:T(8,128)S(1)} %get-tuple-element.9), channel_id=1, source_target_pairs={{0,7},{1,6},{2,5},{3,4},{4,3},{5,2},{6,1},{7,0},{8,15},{9,14},{10,... | collective-permute-start | bytes 24584 | tf_op jit(solution)/shard_map/ppermute | solution.py:407
  9.1 4.0 %collective-permute-start.2 = (f32[16,128]{1,0:T(8,128)S(1)}, f32[16,128]{1,0:T(8,128)S(1)}, u32[]{:S(2)}, u32[]{:S(2)}) collective-permute-start(f32[16,128]{1,0:T(8,128)S(1)} %get-tuple-element.9), channel_id=1, source_target_pairs={{0,6},{1,7},{2,4},{3,5},{4,2},{5,3},{6,0},{7,1},{8,14},{9,15},{10,... | collective-permute-start | bytes 24584 | tf_op jit(solution)/shard_map/ppermute | solution.py:407
  9.2 16.1 %collective-permute-start.7 = (f32[17,16,128]{2,1,0:T(8,128)S(1)}, f32[17,16,128]{2,1,0:T(8,128)S(1)}, u32[]{:S(2)}, u32[]{:S(2)}) collective-permute-start(f32[17,16,128]{2,1,0:T(8,128)S(1)} %get-tuple-element.10.wet_own), channel_id=1, source_target_pairs={{0,3},{1,2},{2,1},{3,0},{4,7},{5,6},{6,5},{7,4},{8,11},{9,10},{10,... | collective-permute-start | bytes 417800 | tf_op jit(solution)/shard_map/ppermute | solution.py:397
  12.7 12.7 %collective-permute-start.8 = (f32[17,16,128]{2,1,0:T(8,128)S(1)}, f32[17,16,128]{2,1,0:T(8,128)S(1)}, u32[]{:S(2)}, u32[]{:S(2)}) collective-permute-start(f32[17,16,128]{2,1,0:T(8,128)S(1)} %get-tuple-element.10.wet_own), channel_id=1, source_target_pairs={{0,2},{1,3},{2,0},{3,1},{4,6},{5,7},{6,4},{7,5},{8,10},{9,11},{10,... | collective-permute-start | bytes 417800 | tf_op jit(solution)/shard_map/ppermute | solution.py:397
  13.1 5.5 %collective-permute-start.3 = (f32[1,88,128]{2,1,0:T(8,128)S(1)}, f32[1,88,128]{2,1,0:T(8,128)S(1)}, u32[]{:S(2)}, u32[]{:S(2)}) collective-permute-start(f32[1,88,128]{2,1,0:T(8,128)S(1)} %bitcast.9), channel_id=1, source_target_pairs={{0,24},{4,28},{8,16},{12,20},{16,8},{20,12},{24,0},{28,4},{1,25},{... | collective-permute-start | bytes 135176 | tf_op jit(solution)/shard_map/ppermute | solution.py:397
  15.6 3.5 %collective-permute-start.4 = (f32[1,88,128]{2,1,0:T(8,128)S(1)}, f32[1,88,128]{2,1,0:T(8,128)S(1)}, u32[]{:S(2)}, u32[]{:S(2)}) collective-permute-start(f32[1,88,128]{2,1,0:T(8,128)S(1)} %bitcast.10), channel_id=1, source_target_pairs={{0,20},{4,16},{8,28},{12,24},{16,4},{20,0},{24,12},{28,8},{1,21},{... | collective-permute-start | bytes 135176 | tf_op jit(solution)/shard_map/ppermute | solution.py:397
  16.4 3.9 %collective-permute-start.5 = (f32[1,88,128]{2,1,0:T(8,128)S(1)}, f32[1,88,128]{2,1,0:T(8,128)S(1)}, u32[]{:S(2)}, u32[]{:S(2)}) collective-permute-start(f32[1,88,128]{2,1,0:T(8,128)S(1)} %bitcast.11), channel_id=1, source_target_pairs={{0,12},{4,8},{8,4},{12,0},{16,28},{20,24},{24,20},{28,16},{1,13},{... | collective-permute-start | bytes 135176 | tf_op jit(solution)/shard_map/ppermute | solution.py:397
  20.3 1.5 %collective-permute-start.6 = (f32[4,88,128]{2,1,0:T(8,128)S(1)}, f32[4,88,128]{2,1,0:T(8,128)S(1)}, u32[]{:S(2)}, u32[]{:S(2)}) collective-permute-start(f32[4,88,128]{2,1,0:T(8,128)S(1)} %pad_maximum_fusion.refs_0_), channel_id=1, source_target_pairs={{0,4},{4,0},{8,12},{12,8},{16,20},{20,16},{24,28},{28,24},{1,5},{5... | collective-permute-start | bytes 540680 | tf_op jit(solution)/shard_map/ppermute | solution.py:397
  20.5 1.3 %copy-start = (s32[32,3]{0,1:T(4,128)S(1)}, s32[32,3]{0,1:T(4,128)}, u32[]{:S(2)}) copy-start(s32[32,3]{0,1:T(4,128)} %param.21) | copy-start | bytes 1156
